TPU v7x, 256 devices: a whole 4x4x8 slice. The times are simulated.
256 devices in a mesh: seq: 32 (over y, z), head: 8 (over x, core).
Axes of the slice: x: 4, y: 4, z: 8, core: 2. Of those that a mesh axis runs over, the one named last changes fastest.
Arguments:
- teacher_query: bfloat16 [4096, 4096], P('seq', 'head'), may hold values from -20 to 20
- teacher_key: bfloat16 [4096, 4096], P('seq', 'head'), may hold values from -20 to 20
- student_query: bfloat16 [4096, 2048], P('seq', 'head'), may hold values from -20 to 20
- student_key: bfloat16 [4096, 2048], P('seq', 'head'), may hold values from -20 to 20
- doc_ids: int32 [4096], P('seq'), may hold values from 0 to 15, never falling along the last dimension, each value on 1 to 3072 neighbouring positions
Outputs:
- kl_loss: float32 [], replicated
- grad_query: bfloat16 [4096, 2048], P('seq', 'head')
- grad_key: bfloat16 [4096, 2048], P('seq', 'head')
Inputs may be any that keep to these rules, and one draw needn't show every extreme that they name: `doc_ids`: ids never fall along the positions; every document is a run of at most 3072 positions and one has exactly 3072.
All inputs are finite; a program needn't handle non-finite values.
Results may differ from a plain program's by a relative error of at most 0.009.
Values may be sent and summed in bfloat16 or wider, within the bound.
No kernel may reach another device: no remote copies, remote signals or barrier semaphores. Data moves between devices by JAX's collectives and lax.ppermute only.
A program may use at most 64 MiB of HBM per device.

v0:
```python
import functools
import math

import jax
import jax.numpy as jnp
from jax import lax
from jax.experimental import pallas as pl
from jax.experimental.pallas import tpu as pltpu
from jax.sharding import PartitionSpec as P

HDIM = 128
TDIM = 256
WIDE = TDIM + HDIM
NY, NZ, NX = 4, 8, 4
ROWS = 128
BLOCK = 512
TILE = 256
TOKENS = 4096
TILES = TOKENS // TILE
NEG = -1e30
LOG2E = 1.4426950408889634
LN2 = 0.6931471805599453
KT = LOG2E / math.sqrt(TDIM)
KS = LOG2E / math.sqrt(HDIM)
VMEM_LIMIT = 48 * 1024 * 1024
ORDER = (0, 1, 3, 2)
PIECE = 2 * ROWS + 16
UNROLL = 2
PACK_FLOPS = 20_000_000_000
F32 = jnp.float32
BF16 = jnp.bfloat16
AXES = ("seq", "head")
ALL = pl.BlockSpec(memory_space=pltpu.VMEM)
SMEM = pl.BlockSpec(memory_space=pltpu.SMEM)
ANY = pl.BlockSpec(memory_space=pl.ANY)


def device(y, z, x, core):
    return (y * NZ + z) * (2 * NX) + x * 2 + core


def pairs_of(move):
    pairs = []
    for y in range(NY):
        for z in range(NZ):
            for x in range(NX):
                for core in range(2):
                    pairs.append((device(y, z, x, core), device(*move(y, z, x, core))))
    return pairs


def spread_pairs(j):
    return pairs_of(lambda y, z, x, c: (y, 2 * ((z // 2 + j) % 4) + c, x, z % 2))


def collect_pairs(j):
    return [(target, source) for source, target in spread_pairs(j)]


def y_pairs(step):
    return pairs_of(lambda y, z, x, c: ((y + step) % NY, z, x, c))


def x_pairs(bit):
    return pairs_of(lambda y, z, x, c: (y, z, x ^ bit, c))


CORE_PAIRS = pairs_of(lambda y, z, x, c: (y, z, x, 1 - c))


def params(limit=VMEM_LIMIT):
    return pltpu.CompilerParams(vmem_limit_bytes=limit)


def nt_dot(left, right):
    return lax.dot_general(left, right, (((1,), (1,)), ((), ())), preferred_element_type=F32)


def send_kernel(place, tq, tk, sq, sk, doc, o0, o1, o2, o3, held, docs, sems):
    copies = []
    for m, (teach, pupil) in enumerate(((tq, sq), (tq, sq), (tk, sk), (tk, sk))):
        h = m % 2
        block = held.at[m, pl.ds(0, ROWS)]
        copies.append((teach.at[:, pl.ds(h * TDIM, TDIM)], block.at[:, pl.ds(0, TDIM)]))
        copies.append((pupil.at[:, pl.ds(h * HDIM, HDIM)], block.at[:, pl.ds(TDIM, HDIM)]))
    copies.append((doc, docs))
    copies = [pltpu.make_async_copy(src, dst, sems.at[n]) for n, (src, dst) in enumerate(copies)]
    for copy in copies:
        copy.start()
    for copy in copies:
        copy.wait()
    below = docs[...] < lax.broadcasted_iota(jnp.int32, (128, ROWS), 0)
    counts = nt_dot(jnp.ones((16, ROWS), BF16), below.astype(F32).astype(BF16))
    b = place[1] // 2
    for j, out in enumerate((o0, o1, o2, o3)):
        out[0:ROWS, :] = held[(b + j) % 4]
        out[ROWS:ROWS + 16, 0:128] = counts.astype(BF16)
        out[ROWS:ROWS + 16, 128:WIDE] = jnp.zeros((16, 256), BF16)


def pack_kernel(first, second, out):
    out[0:ROWS, :] = first[0:ROWS, :]
    out[ROWS:2 * ROWS, :] = second[0:ROWS, :]
    out[2 * ROWS:PIECE, :] = first[ROWS:ROWS + 16, :] + second[ROWS:ROWS + 16, :]


def pack_both_kernel(before, first, second, out, both):
    pack_kernel(first, second, out)
    both[0:PIECE, :] = before[...]
    both[PIECE:2 * PIECE, :] = out[...]


def pieces_of(parts):
    found = []
    for other in range(2):
        for chunk in range(2):
            found.append((parts[other], chunk * PIECE, 0, other, chunk))
    for n, part in enumerate(parts[2:]):
        chunk, i, other = n // 6, n % 6 // 2 + 1, n % 2
        found.append((part, 0, i, other, chunk))
    return found


def assemble(place, parts, rows):
    y, core = place[0], place[2]
    m = place[1] // 2
    total = jnp.zeros((16, 128), F32)
    for part, base, i, other, chunk in pieces_of(parts):
        from_core = core if other == 0 else 1 - core
        from_y = (y - i + NY) % NY
        for k in range(2):
            b = (m - ORDER[2 * chunk + k] + 4) % 4
            at = (from_y * 8 + 2 * b + from_core) * ROWS
            rows[pl.ds(pl.multiple_of(at, ROWS), ROWS), :] = part[base + k * ROWS:base + (k + 1) * ROWS, :]
        total = total + part[base + 2 * ROWS:base + PIECE, 0:128].astype(F32)
    return total[0:1]


def start_of(bounds, position):
    return jnp.max(jnp.where(bounds <= position, bounds, 0.0))


def end_of(bounds, position):
    return jnp.min(jnp.where(bounds > position, bounds, float(TOKENS)))


def tile_rows(t):
    return pl.ds(pl.multiple_of(t * TILE, TILE), TILE)


def folded(values):
    return values.reshape(TILE // 8, 8, TILE)


def norm_kernel(place, *refs):
    parts, out = refs[:14], refs[14]
    rows, scores_t, scores_s = refs[15:]
    bounds = assemble(place, parts, rows)
    r = place[0] * 2 + place[2]
    bounds_down = jnp.transpose(jnp.broadcast_to(bounds, (128, 128)))[0:16, 0:1]
    out[...] = jnp.zeros_like(out)
    for half in range(2):
        t = r if half == 0 else TILES - 1 - r
        first = t * TILE
        mine_t = rows[tile_rows(t), 0:TDIM]
        mine_s = rows[tile_rows(t), TDIM:WIDE]
        low = start_of(bounds, first.astype(F32)).astype(jnp.int32)
        high = start_of(bounds, (first + TILE - 1).astype(F32)).astype(jnp.int32)
        my_pos = first + lax.broadcasted_iota(jnp.int32, (1, TILE), 1)
        my_start = jnp.max(
            jnp.where(bounds_down <= my_pos.astype(F32), bounds_down, 0.0), axis=0, keepdims=True
        ).astype(jnp.int32)

        def span(c, n):
            return pl.ds(pl.multiple_of(c * TILE, TILE), n * TILE)

        def eights(values):
            return values.reshape(values.shape[0] // 8, 8, TILE)

        def score(c, tops, n, masked):
            t_tile = nt_dot(rows[span(c, n), 0:TDIM], mine_t) * KT
            s_tile = nt_dot(rows[span(c, n), TDIM:WIDE], mine_s) * KS
            if masked:
                pos = c * TILE + lax.broadcasted_iota(jnp.int32, (n * TILE, TILE), 0)
                seen = (pos <= my_pos) & (pos >= my_start)
                t_tile = jnp.where(seen, t_tile, NEG)
                s_tile = jnp.where(seen, s_tile, NEG)
            scores_t[span(c, n), :] = t_tile
            scores_s[span(c, n), :] = s_tile
            return (
                jnp.maximum(tops[0], jnp.max(eights(t_tile), axis=0)),
                jnp.maximum(tops[1], jnp.max(eights(s_tile), axis=0)),
            )

        def run(begin, stop, carry, body, n=1):
            return lax.fori_loop(0, (stop - begin) // n, lambda i, v: body(begin + n * i, v, n), carry)

        def run_all(begin, stop, carry, body):
            for n in (4, 2, 1):
                middle = stop - (stop - begin) % n
                carry = run(begin, middle, carry, body, n)
                begin = middle
            return carry

        from_tile = low // TILE
        plain_tile = jnp.minimum((high + TILE - 1) // TILE, t)
        tops = (jnp.full((8, TILE), NEG, F32), jnp.full((8, TILE), NEG, F32))
        tops = run_all(from_tile, plain_tile, tops, functools.partial(score, masked=True))
        tops = run_all(plain_tile, t, tops, functools.partial(score, masked=False))
        tops = score(t, tops, 1, True)
        top_t = jnp.max(tops[0], axis=0, keepdims=True)
        top_s = jnp.max(tops[1], axis=0, keepdims=True)

        def add(c, sums, n):
            sum_t, sum_s, cross = sums
            t_tile = scores_t[span(c, n), :]
            s_tile = scores_s[span(c, n), :]
            p = jnp.exp2(t_tile - top_t)
            q = jnp.exp2(s_tile - top_s)
            return (
                sum_t + jnp.sum(eights(p), axis=0),
                sum_s + jnp.sum(eights(q), axis=0),
                cross + jnp.sum(eights(p * (t_tile - s_tile)), axis=0),
            )

        zero = jnp.zeros((8, TILE), F32)
        sums = run_all(from_tile, t + 1, (zero, zero, zero), add)
        sum_t, sum_s, cross = (jnp.sum(v, axis=0, keepdims=True) for v in sums)
        lse_t = top_t * LN2 + jnp.log(sum_t)
        lse_s = top_s * LN2 + jnp.log(sum_s)
        row_kl = cross * LN2 / sum_t - lse_t + lse_s
        for k, lse in enumerate((lse_t, lse_s)):
            high_part = lse.astype(BF16).astype(F32)
            low_part = (lse - high_part).astype(BF16).astype(F32)
            out[2 * half + k:2 * half + k + 1, :] = (high_part + low_part) * LOG2E
        out[4 + half:5 + half, :] = row_kl


def grad_kernel(place, *refs):
    parts, packets, outs = refs[:14], refs[14:18], refs[18:22]
    rows, norms, row_norm, acc, mine = refs[22:]
    bounds = assemble(place, parts, rows)
    y, core = place[0], place[2]
    m = place[1] // 2
    kl = jnp.zeros((1, TILE), F32)
    for i, packet in enumerate(packets):
        for other in range(2):
            from_core = core if other == 0 else 1 - core
            from_r = ((y - i + NY) % NY) * 2 + from_core
            norms[from_r, 0:2, :] = packet[8 * other:8 * other + 2, :]
            norms[TILES - 1 - from_r, 0:2, :] = packet[8 * other + 2:8 * other + 4, :]
            kl = kl + packet[8 * other + 4:8 * other + 5, :] + packet[8 * other + 5:8 * other + 6, :]
    kl = kl[:, 0:128] + kl[:, 128:256]
    first = y * (2 * BLOCK) + core * ROWS
    last = first + 7 * ROWS - 1
    for b in range(4):
        sub = slice(b * ROWS, (b + 1) * ROWS)
        mine[sub, :] = rows[pl.ds(pl.multiple_of(first + 2 * b * ROWS, ROWS), ROWS), :]
        for k in range(2):
            line = norms[4 * y + b, k:k + 1, :]
            line = jnp.where(core == 0, line[:, 0:ROWS], line[:, ROWS:TILE])
            row_norm[k, sub] = jnp.transpose(jnp.broadcast_to(line, (ROWS, ROWS)))
    my_index = lax.broadcasted_iota(jnp.int32, (BLOCK, 1), 0)
    my_pos = first + my_index + (my_index // ROWS) * ROWS
    my_posf = my_pos.astype(F32)
    my_start = jnp.max(jnp.where(bounds <= my_posf, bounds, 0.0), axis=1, keepdims=True)
    my_end = jnp.min(jnp.where(bounds > my_posf, bounds, float(TOKENS)), axis=1, keepdims=True)
    my_start, my_end = my_start.astype(jnp.int32), my_end.astype(jnp.int32)
    firstf, lastf = first.astype(F32), last.astype(F32)
    start_low = start_of(bounds, firstf).astype(jnp.int32)
    start_high = start_of(bounds, lastf).astype(jnp.int32)
    end_low = end_of(bounds, firstf).astype(jnp.int32)
    end_high = end_of(bounds, lastf).astype(jnp.int32)
    acc[...] = jnp.zeros_like(acc)

    def columns(c, n):
        return pl.ds(pl.multiple_of(c * TILE, TILE), n * TILE)

    def step(c, n, kind, masked):
        width = n * TILE
        pupil = rows[columns(c, n), TDIM:WIDE]
        t_tile = nt_dot(mine[:, 0:TDIM], rows[columns(c, n), 0:TDIM]) * KT
        s_tile = nt_dot(mine[:, TDIM:WIDE], pupil) * KS
        own_norm = [jnp.concatenate([row_norm[k]] * (2 * n), axis=1) for k in range(2)]
        their_norm = [jnp.concatenate([norms[c + q, k:k + 1, :] for q in range(n)], axis=1) for k in range(2)]
        pos = c * TILE + lax.broadcasted_iota(jnp.int32, (BLOCK, width), 1)
        if kind == "below":
            norm_t, norm_s = own_norm
        elif kind == "above":
            norm_t, norm_s = their_norm
        else:
            own = pos <= my_pos
            norm_t, norm_s = (jnp.where(own, own_norm[k], their_norm[k]) for k in range(2))
        weight = jnp.exp2(s_tile - norm_s) - jnp.exp2(t_tile - norm_t)
        if kind == "diagonal":
            weight = jnp.where(pos == my_pos, 2.0 * weight, weight)
        if masked:
            weight = jnp.where((pos >= my_start) & (pos < my_end), weight, 0.0)
        acc[...] += jnp.dot(weight.astype(BF16), pupil, preferred_element_type=F32)

    def run(begin, stop, kind, masked, n=1):
        def body(i, unused):
            step(begin + n * i, n, kind, masked)
            return unused

        lax.fori_loop(0, (stop - begin) // n, body, 0)

    diag = 4 * y
    plain = jnp.minimum((start_high + TILE - 1) // TILE, diag)
    begin = start_low // TILE
    odd = plain - (plain - begin) % UNROLL
    run(begin, odd, "below", True, UNROLL)
    run(odd, plain, "below", True)
    odd = plain + (diag - plain) % UNROLL
    run(plain, odd, "below", False)
    run(odd, diag, "below", False, UNROLL)
    run(diag, diag + 4, "diagonal", True, 2)
    plain = jnp.maximum(end_low // TILE, diag + 4)
    odd = diag + 4 + (plain - diag - 4) % UNROLL
    run(diag + 4, odd, "above", False)
    run(odd, plain, "above", False, UNROLL)
    stop = (end_high + TILE - 1) // TILE
    odd = plain + (stop - plain) % UNROLL
    run(plain, odd, "above", True)
    run(odd, stop, "above", True, UNROLL)
    for b in range(4):
        for j in range(4):

            @pl.when((m - j + 4) % 4 == b)
            def _():
                outs[j][0:ROWS, :] = acc[b * ROWS:(b + 1) * ROWS, :].astype(BF16)

    high_part = kl.astype(BF16).astype(F32)
    mid_part = (kl - high_part).astype(BF16).astype(F32)
    low_part = (kl - high_part - mid_part).astype(BF16).astype(F32)
    line = lax.broadcasted_iota(jnp.int32, (16, 128), 0)
    tail = jnp.where(line == 0, high_part, jnp.where(line == 1, mid_part, jnp.where(line == 2, low_part, 0.0)))
    for j in range(4):
        outs[j][ROWS:ROWS + 16, :] = tail.astype(BF16)


def finish_kernel(place, g0, g1, g2, g3, grad_q, grad_k, held):
    b = place[1] // 2
    for j, got in enumerate((g0, g1, g2, g3)):
        held[(b + j) % 4] = got[0:ROWS, :]
    for m in range(4):
        out = grad_q if m < 2 else grad_k
        h = m % 2
        out[:, h * HDIM:(h + 1) * HDIM] = held[m]


def call_norm(place, parts):
    return pl.pallas_call(
        norm_kernel,
        out_shape=jax.ShapeDtypeStruct((8, TILE), F32),
        in_specs=[SMEM] + [ALL] * 14,
        out_specs=ALL,
        scratch_shapes=[
            pltpu.VMEM((TOKENS, WIDE), BF16),
            pltpu.VMEM((TOKENS, TILE), F32),
            pltpu.VMEM((TOKENS, TILE), F32),
        ],
        compiler_params=params(),
    )(place, *parts)


def call_grad(place, parts, packets):
    return pl.pallas_call(
        grad_kernel,
        out_shape=[jax.ShapeDtypeStruct((ROWS + 16, HDIM), BF16)] * 4,
        in_specs=[SMEM] + [ALL] * 18,
        out_specs=[ALL] * 4,
        scratch_shapes=[
            pltpu.VMEM((TOKENS, WIDE), BF16),
            pltpu.VMEM((TILES, 8, TILE), F32),
            pltpu.VMEM((2, BLOCK, 128), F32),
            pltpu.VMEM((BLOCK, HDIM), F32),
            pltpu.VMEM((BLOCK, WIDE), BF16),
        ],
        compiler_params=params(),
    )(place, *parts, *packets)


def per_device(teacher_query, teacher_key, student_query, student_key, doc_ids):
    seq, head = lax.axis_index("seq"), lax.axis_index("head")
    place = jnp.stack([seq // NZ, seq % NZ, head % 2]).astype(jnp.int32)

    block = jax.ShapeDtypeStruct((ROWS + 16, WIDE), BF16)
    sends = pl.pallas_call(
        send_kernel,
        out_shape=[block] * 4,
        in_specs=[SMEM] + [ANY] * 5,
        out_specs=[ALL] * 4,
        scratch_shapes=[
            pltpu.VMEM((4, ROWS, WIDE), BF16),
            pltpu.VMEM((1, ROWS), jnp.int32),
            pltpu.SemaphoreType.DMA((9,)),
        ],
        compiler_params=params(60 * 1024 * 1024),
    )(place, teacher_query, teacher_key, student_query, student_key, doc_ids.reshape(1, ROWS))
    gots = [lax.ppermute(sends[j], AXES, spread_pairs(j)) for j in ORDER]
    piece = jax.ShapeDtypeStruct((PIECE, WIDE), BF16)
    own_a = pl.pallas_call(
        pack_kernel,
        out_shape=piece,
        in_specs=[ALL] * 2,
        out_specs=ALL,
        compiler_params=params(),
        cost_estimate=pl.CostEstimate(
            flops=PACK_FLOPS, bytes_accessed=4 * PIECE * WIDE, transcendentals=0
        ),
    )(*gots[0:2])
    own_b, own = pl.pallas_call(
        pack_both_kernel,
        out_shape=[piece, jax.ShapeDtypeStruct((2 * PIECE, WIDE), BF16)],
        in_specs=[ALL] * 3,
        out_specs=[ALL] * 2,
        compiler_params=params(),
    )(own_a, *gots[2:4])
    parts = [own, lax.ppermute(own, AXES, CORE_PAIRS)]
    for mine in (own_a, own_b):
        for step in (1, 2, 3):
            part = lax.ppermute(mine, AXES, y_pairs(step))
            parts += [part, lax.ppermute(part, AXES, CORE_PAIRS)]
    packet = call_norm(place, parts)
    both = jnp.concatenate([packet, lax.ppermute(packet, AXES, CORE_PAIRS)])
    packets = [both] + [lax.ppermute(both, AXES, y_pairs(step)) for step in (1, 2, 3)]
    grads = call_grad(place, parts, packets)
    backs = [lax.ppermute(grads[j], AXES, collect_pairs(j)) for j in range(4)]
    kl = sum(back[ROWS:ROWS + 16].astype(F32) for back in backs)
    kl = jnp.sum(kl.reshape(2, 8, HDIM), axis=0)
    kl = kl + lax.ppermute(kl, AXES, CORE_PAIRS)
    kl = kl + sum(lax.ppermute(kl, AXES, x_pairs(bits)) for bits in (1, 2, 3))
    kl_loss = jnp.sum(kl) / (2.0 * TOKENS * 16)
    half_grad = jax.ShapeDtypeStruct((ROWS, 2 * HDIM), BF16)
    grad_query, grad_key = pl.pallas_call(
        finish_kernel,
        out_shape=[half_grad, half_grad],
        in_specs=[SMEM] + [ALL] * 4,
        out_specs=[ALL] * 2,
        scratch_shapes=[pltpu.VMEM((4, ROWS, HDIM), BF16)],
        compiler_params=params(),
    )(place, *backs)
    return (kl_loss, grad_query, grad_key)


def solution(mesh):
    in_specs = (P("seq", "head"), P("seq", "head"), P("seq", "head"), P("seq", "head"), P("seq"))
    out_specs = (P(), P("seq", "head"), P("seq", "head"))
    return jax.shard_map(
        per_device, mesh=mesh, in_specs=in_specs, out_specs=out_specs, check_vma=False
    )
```

profile of v0, /device:TPU:32, one launch (start us, length us, event | category | flops | bytes accessed | tf_op | source)
XLA Modules:
  0.0 86.8 jit_solution(3760472680588795707)
XLA Ops:
  1.3 2.7 %shard_map.76 = (bf16[144,384]{1,0:T(8,128)(2,1)}, bf16[144,384]{1,0:T(8,128)(2,1)}, bf16[144,384]{1,0:T(8,128)(2,1)}, bf16[144,384]{1,0:T(8,128)(2,1)}) custom-call(s32[3]{0:T(128)} %pad_add_fusion.place, bf16[128,512]{1,0:T(8,128)(2,1)} %tq.1, bf16[128,512]{1,0:T(8,128)(2,1)} %tk.1, bf16[128,256]{1,0:T(8,128)(2,1)} %sq.1, bf16[128,256]{1,0:T(8,128)(2,1)} %sk.1, ...), custom_call_target="tpu_custom_call" | custom-call | tf_op jit(solution)/shard_map/pallas_call | solution.py:389
  4.0 1.9 %collective-permute-start = (bf16[144,384]{1,0:T(8,128)(2,1)}, bf16[144,384]{1,0:T(8,128)(2,1)S(1)}, u32[]{:S(2)}, u32[]{:S(2)}) collective-permute-start(bf16[144,384]{1,0:T(8,128)(2,1)} %get-tuple-element.15), channel_id=1, source_target_pairs={{0,0},{1,8},{2,2},{3,10},{4,4},{5,12},{6,6},{7,14},{8,1},{9,9},{10... | collective-permute-start | bytes 331784 | tf_op jit(solution)/shard_map/ppermute | solution.py:401
  5.9 3.6 %collective-permute-start.1 = (bf16[144,384]{1,0:T(8,128)(2,1)}, bf16[144,384]{1,0:T(8,128)(2,1)S(1)}, u32[]{:S(2)}, u32[]{:S(2)}) collective-permute-start(bf16[144,384]{1,0:T(8,128)(2,1)} %get-tuple-element.16), channel_id=1, source_target_pairs={{0,16},{1,24},{2,18},{3,26},{4,20},{5,28},{6,22},{7,30},{8,17},{9,... | collective-permute-start | bytes 331784 | tf_op jit(solution)/shard_map/ppermute | solution.py:401
  9.5 3.1 %collective-permute-start.2 = (bf16[144,384]{1,0:T(8,128)(2,1)}, bf16[144,384]{1,0:T(8,128)(2,1)S(1)}, u32[]{:S(2)}, u32[]{:S(2)}) collective-permute-start(bf16[144,384]{1,0:T(8,128)(2,1)} %get-tuple-element.17), channel_id=1, source_target_pairs={{0,48},{1,56},{2,50},{3,58},{4,52},{5,60},{6,54},{7,62},{8,49},{9,... | collective-permute-start | bytes 331784 | tf_op jit(solution)/shard_map/ppermute | solution.py:401
  12.7 2.9 %collective-permute-start.3 = (bf16[144,384]{1,0:T(8,128)(2,1)}, bf16[144,384]{1,0:T(8,128)(2,1)S(1)}, u32[]{:S(2)}, u32[]{:S(2)}) collective-permute-start(bf16[144,384]{1,0:T(8,128)(2,1)} %get-tuple-element.18), channel_id=1, source_target_pairs={{0,32},{1,40},{2,34},{3,42},{4,36},{5,44},{6,38},{7,46},{8,33},{9,... | collective-permute-start | bytes 331784 | tf_op jit(solution)/shard_map/ppermute | solution.py:401
  15.5 2.5 %collective-permute-done.1.second = bf16[144,384]{1,0:T(8,128)(2,1)S(1)} collective-permute-done((bf16[144,384]{1,0:T(8,128)(2,1)}, bf16[144,384]{1,0:T(8,128)(2,1)S(1)}, u32[]{:S(2)}, u32[]{:S(2)}) %collective-permute-start.1) | collective-permute-done | bytes 110624 | tf_op jit(solution)/shard_map/ppermute | solution.py:401
  18.1 3.1 %collective-permute-start.9 = (bf16[272,384]{1,0:T(8,128)(2,1)S(1)}, bf16[272,384]{1,0:T(8,128)(2,1)S(1)}, u32[]{:S(2)}, u32[]{:S(2)}) collective-permute-start(bf16[272,384]{1,0:T(8,128)(2,1)S(1)} %shard_map.77.before), channel_id=1, source_target_pairs={{0,192},{1,193},{2,194},{3,195},{4,196},{5,197},{6,198},{7,199},{8... | collective-permute-start | bytes 626696 | tf_op jit(solution)/shard_map/ppermute | solution.py:423
  21.8 1.0 %collective-permute-start.5 = (bf16[272,384]{1,0:T(8,128)(2,1)S(1)}, bf16[272,384]{1,0:T(8,128)(2,1)S(1)}, u32[]{:S(2)}, u32[]{:S(2)}) collective-permute-start(bf16[272,384]{1,0:T(8,128)(2,1)S(1)} %shard_map.77.before), channel_id=1, source_target_pairs={{0,64},{1,65},{2,66},{3,67},{4,68},{5,69},{6,70},{7,71},{8,72},{9,... | collective-permute-start | bytes 626696 | tf_op jit(solution)/shard_map/ppermute | solution.py:423
  22.8 3.0 %collective-permute-done.3.second = bf16[144,384]{1,0:T(8,128)(2,1)S(1)} collective-permute-done((bf16[144,384]{1,0:T(8,128)(2,1)}, bf16[144,384]{1,0:T(8,128)(2,1)S(1)}, u32[]{:S(2)}, u32[]{:S(2)}) %collective-permute-start.3) | collective-permute-done | bytes 110624 | tf_op jit(solution)/shard_map/ppermute | solution.py:401
  25.9 3.1 %collective-permute-start.15 = (bf16[272,384]{1,0:T(8,128)(2,1)S(1)}, bf16[272,384]{1,0:T(8,128)(2,1)S(1)}, u32[]{:S(2)}, u32[]{:S(2)}) collective-permute-start(bf16[272,384]{1,0:T(8,128)(2,1)S(1)} %get-tuple-element.20), channel_id=1, source_target_pairs={{0,192},{1,193},{2,194},{3,195},{4,196},{5,197},{6,198},{7,199},{8... | collective-permute-start | bytes 626696 | tf_op jit(solution)/shard_map/ppermute | solution.py:423
  29.6 1.0 %collective-permute-start.11 = (bf16[272,384]{1,0:T(8,128)(2,1)S(1)}, bf16[272,384]{1,0:T(8,128)(2,1)S(1)}, u32[]{:S(2)}, u32[]{:S(2)}) collective-permute-start(bf16[272,384]{1,0:T(8,128)(2,1)S(1)} %get-tuple-element.20), channel_id=1, source_target_pairs={{0,64},{1,65},{2,66},{3,67},{4,68},{5,69},{6,70},{7,71},{8,72},{9,... | collective-permute-start | bytes 626696 | tf_op jit(solution)/shard_map/ppermute | solution.py:423
  30.6 3.2 %collective-permute-done.5.refs_2_ = bf16[272,384]{1,0:T(8,128)(2,1)S(1)} collective-permute-done((bf16[272,384]{1,0:T(8,128)(2,1)S(1)}, bf16[272,384]{1,0:T(8,128)(2,1)S(1)}, u32[]{:S(2)}, u32[]{:S(2)}) %collective-permute-start.5) | collective-permute-done | bytes 208928 | tf_op jit(solution)/shard_map/ppermute | solution.py:423
  33.8 2.3 %collective-permute-done.15.refs_12_ = bf16[272,384]{1,0:T(8,128)(2,1)S(1)} collective-permute-done((bf16[272,384]{1,0:T(8,128)(2,1)S(1)}, bf16[272,384]{1,0:T(8,128)(2,1)S(1)}, u32[]{:S(2)}, u32[]{:S(2)}) %collective-permute-start.15) | collective-permute-done | bytes 208928 | tf_op jit(solution)/shard_map/ppermute | solution.py:423
  36.1 1.6 %collective-permute-done.13.refs_10_ = bf16[272,384]{1,0:T(8,128)(2,1)S(1)} collective-permute-done((bf16[272,384]{1,0:T(8,128)(2,1)S(1)}, bf16[272,384]{1,0:T(8,128)(2,1)S(1)}, u32[]{:S(2)}, u32[]{:S(2)}) %collective-permute-start.13) | collective-permute-done | bytes 208928 | tf_op jit(solution)/shard_map/ppermute | solution.py:423
  37.8 2.1 %collective-permute-done.11.refs_8_ = bf16[272,384]{1,0:T(8,128)(2,1)S(1)} collective-permute-done((bf16[272,384]{1,0:T(8,128)(2,1)S(1)}, bf16[272,384]{1,0:T(8,128)(2,1)S(1)}, u32[]{:S(2)}, u32[]{:S(2)}) %collective-permute-start.11) | collective-permute-done | bytes 208928 | tf_op jit(solution)/shard_map/ppermute | solution.py:423
  40.5 0.8 collective-permute-done.16.refs_13_
  41.9 4.9 %shard_map.79 = f32[8,256]{1,0:T(8,128)S(1)} custom-call(s32[3]{0:T(128)S(1)} %copy-done, bf16[544,384]{1,0:T(8,128)(2,1)S(1)} %get-tuple-element.19.refs_0_, bf16[544,384]{1,0:T(8,128)(2,1)S(1)} %collective-permute-done.4.refs_1_, bf16[272,384]{1,0:T(8,128)(2,1)S(1)} %collective-permute-done.5.refs_2_, bf16[272,384]{1,0:T(8,128)(2,1)S(1)} %collective-permute-done.6.refs_3_, ...), custom_call_target="tpu_custom_call" | custom-call | tf_op jit(solution)/shard_map/pallas_call | solution.py:353
  47.3 0.8 collective-permute-done.17
  49.0 1.2 %collective-permute-start.18 = (f32[16,256]{1,0:T(8,128)S(1)}, f32[16,256]{1,0:T(8,128)S(1)}, u32[]{:S(2)}, u32[]{:S(2)}) collective-permute-start(f32[16,256]{1,0:T(8,128)S(1)} %pad_maximum_fusion.refs_14_), channel_id=1, source_target_pairs={{0,64},{1,65},{2,66},{3,67},{4,68},{5,69},{6,70},{7,71},{8,72},{9,... | collective-permute-start | bytes 49160 | tf_op jit(solution)/shard_map/ppermute | solution.py:427
  50.2 1.7 %collective-permute-done.20.refs_17_ = f32[16,256]{1,0:T(8,128)S(1)} collective-permute-done((f32[16,256]{1,0:T(8,128)S(1)}, f32[16,256]{1,0:T(8,128)S(1)}, u32[]{:S(2)}, u32[]{:S(2)}) %collective-permute-start.20) | collective-permute-done | bytes 16416 | tf_op jit(solution)/shard_map/ppermute | solution.py:427
  51.9 2.0 %collective-permute-done.19.refs_16_ = f32[16,256]{1,0:T(8,128)S(1)} collective-permute-done((f32[16,256]{1,0:T(8,128)S(1)}, f32[16,256]{1,0:T(8,128)S(1)}, u32[]{:S(2)}, u32[]{:S(2)}) %collective-permute-start.19) | collective-permute-done | bytes 16416 | tf_op jit(solution)/shard_map/ppermute | solution.py:427
  54.6 3.5 %shard_map.80 = (bf16[144,128]{1,0:T(8,128)(2,1)S(1)}, bf16[144,128]{1,0:T(8,128)(2,1)S(1)}, bf16[144,128]{1,0:T(8,128)(2,1)S(1)}, bf16[144,128]{1,0:T(8,128)(2,1)S(1)}) custom-call(s32[3]{0:T(128)S(1)} %copy-done, bf16[544,384]{1,0:T(8,128)(2,1)S(1)} %get-tuple-element.19.refs_0_, bf16[544,384]{1,0:T(8,128)(2,1)S(1)} %collective-permute-done.4.refs_1_, ...), custom_call_target="tpu_custom_call" | custom-call | tf_op jit(solution)/shard_map/pallas_call | solution.py:368
  58.1 8.2 %collective-permute-start.21 = (bf16[144,128]{1,0:T(8,128)(2,1)S(1)}, bf16[144,128]{1,0:T(8,128)(2,1)S(1)}, u32[]{:S(2)}, u32[]{:S(2)}) collective-permute-start(bf16[144,128]{1,0:T(8,128)(2,1)S(1)} %get-tuple-element.21), channel_id=1, source_target_pairs={{0,0},{8,1},{2,2},{10,3},{4,4},{12,5},{6,6},{14,7},{1,8},{9,9},{3,... | collective-permute-start | bytes 110600 | tf_op jit(solution)/shard_map/ppermute | solution.py:429
  66.4 2.6 %collective-permute-start.23 = (bf16[144,128]{1,0:T(8,128)(2,1)S(1)}, bf16[144,128]{1,0:T(8,128)(2,1)S(1)}, u32[]{:S(2)}, u32[]{:S(2)}) collective-permute-start(bf16[144,128]{1,0:T(8,128)(2,1)S(1)} %get-tuple-element.23), channel_id=1, source_target_pairs={{32,0},{40,1},{34,2},{42,3},{36,4},{44,5},{38,6},{46,7},{33,8},{41... | collective-permute-start | bytes 110600 | tf_op jit(solution)/shard_map/ppermute | solution.py:429
  69.0 0.9 %collective-permute-start.24 = (bf16[144,128]{1,0:T(8,128)(2,1)S(1)}, bf16[144,128]{1,0:T(8,128)(2,1)S(1)}, u32[]{:S(2)}, u32[]{:S(2)}) collective-permute-start(bf16[144,128]{1,0:T(8,128)(2,1)S(1)} %get-tuple-element.24), channel_id=1, source_target_pairs={{48,0},{56,1},{50,2},{58,3},{52,4},{60,5},{54,6},{62,7},{49,8},{57... | collective-permute-start | bytes 110600 | tf_op jit(solution)/shard_map/ppermute | solution.py:429
  70.5 2.3 %collective-permute-done.23.g2 = bf16[144,128]{1,0:T(8,128)(2,1)S(1)} collective-permute-done((bf16[144,128]{1,0:T(8,128)(2,1)S(1)}, bf16[144,128]{1,0:T(8,128)(2,1)S(1)}, u32[]{:S(2)}, u32[]{:S(2)}) %collective-permute-start.23) | collective-permute-done | bytes 36896 | tf_op jit(solution)/shard_map/ppermute | solution.py:429
  72.9 2.6 %collective-permute-done.24.g3 = bf16[144,128]{1,0:T(8,128)(2,1)S(1)} collective-permute-done((bf16[144,128]{1,0:T(8,128)(2,1)S(1)}, bf16[144,128]{1,0:T(8,128)(2,1)S(1)}, u32[]{:S(2)}, u32[]{:S(2)}) %collective-permute-start.24) | collective-permute-done | bytes 36896 | tf_op jit(solution)/shard_map/ppermute | solution.py:429
  75.4 1.2 %collective-permute-done.25 = f32[8,128]{1,0:T(8,128)S(1)} collective-permute-done((f32[8,128]{1,0:T(8,128)S(1)}, f32[8,128]{1,0:T(8,128)S(1)}, u32[]{:S(2)}, u32[]{:S(2)}) %collective-permute-start.25) | collective-permute-done | bytes 4128 | tf_op jit(solution)/shard_map/ppermute | solution.py:432
  76.6 2.8 %collective-permute-start.28 = (f32[8,128]{1,0:T(8,128)S(1)}, f32[8,128]{1,0:T(8,128)S(1)}, u32[]{:S(2)}, u32[]{:S(2)}) collective-permute-start(f32[8,128]{1,0:T(8,128)S(1)} %add.34), channel_id=1, source_target_pairs={{0,6},{1,7},{2,4},{3,5},{4,2},{5,3},{6,0},{7,1},{8,14},{9,15},{10,... | collective-permute-start | bytes 12296 | tf_op jit(solution)/shard_map/ppermute | solution.py:433
  79.3 0.8 collective-permute-start.27
  80.7 1.2 %shard_map.81 = (bf16[128,256]{1,0:T(8,128)(2,1)}, bf16[128,256]{1,0:T(8,128)(2,1)}) custom-call(s32[3]{0:T(128)S(1)} %copy-done, bf16[144,128]{1,0:T(8,128)(2,1)S(1)} %collective-permute-done.21.g0, bf16[144,128]{1,0:T(8,128)(2,1)S(1)} %collective-permute-done.22.g1, bf16[144,128]{1,0:T(8,128)(2,1)S(1)} %collective-permute-done.23.g2, ...), custom_call_target="tpu_custom_call" | custom-call | tf_op jit(solution)/shard_map/pallas_call | solution.py:436
  81.9 2.5 %collective-permute-done.27 = f32[8,128]{1,0:T(8,128)S(1)} collective-permute-done((f32[8,128]{1,0:T(8,128)S(1)}, f32[8,128]{1,0:T(8,128)S(1)}, u32[]{:S(2)}, u32[]{:S(2)}) %collective-permute-start.27) | collective-permute-done | bytes 4128 | tf_op jit(solution)/shard_map/ppermute | solution.py:433
  (39 shorter events, 7.1 us)
Async XLA Ops:
  4.0 11.5 %collective-permute-start = (bf16[144,384]{1,0:T(8,128)(2,1)}, bf16[144,384]{1,0:T(8,128)(2,1)S(1)}, u32[]{:S(2)}, u32[]{:S(2)}) collective-permute-start(bf16[144,384]{1,0:T(8,128)(2,1)} %get-tuple-element.15), channel_id=1, source_target_pairs={{0,0},{1,8},{2,2},{3,10},{4,4},{5,12},{6,6},{7,14},{8,1},{9,9},{10... | collective-permute-start | bytes 331784 | tf_op jit(solution)/shard_map/ppermute | solution.py:401
  5.9 12.1 %collective-permute-start.1 = (bf16[144,384]{1,0:T(8,128)(2,1)}, bf16[144,384]{1,0:T(8,128)(2,1)S(1)}, u32[]{:S(2)}, u32[]{:S(2)}) collective-permute-start(bf16[144,384]{1,0:T(8,128)(2,1)} %get-tuple-element.16), channel_id=1, source_target_pairs={{0,16},{1,24},{2,18},{3,26},{4,20},{5,28},{6,22},{7,30},{8,17},{9,... | collective-permute-start | bytes 331784 | tf_op jit(solution)/shard_map/ppermute | solution.py:401
  9.5 13.2 %collective-permute-start.2 = (bf16[144,384]{1,0:T(8,128)(2,1)}, bf16[144,384]{1,0:T(8,128)(2,1)S(1)}, u32[]{:S(2)}, u32[]{:S(2)}) collective-permute-start(bf16[144,384]{1,0:T(8,128)(2,1)} %get-tuple-element.17), channel_id=1, source_target_pairs={{0,48},{1,56},{2,50},{3,58},{4,52},{5,60},{6,54},{7,62},{8,49},{9,... | collective-permute-start | bytes 331784 | tf_op jit(solution)/shard_map/ppermute | solution.py:401
  12.7 13.1 %collective-permute-start.3 = (bf16[144,384]{1,0:T(8,128)(2,1)}, bf16[144,384]{1,0:T(8,128)(2,1)S(1)}, u32[]{:S(2)}, u32[]{:S(2)}) collective-permute-start(bf16[144,384]{1,0:T(8,128)(2,1)} %get-tuple-element.18), channel_id=1, source_target_pairs={{0,32},{1,40},{2,34},{3,42},{4,36},{5,44},{6,38},{7,46},{8,33},{9,... | collective-permute-start | bytes 331784 | tf_op jit(solution)/shard_map/ppermute | solution.py:401
  18.1 11.5 %collective-permute-start.9 = (bf16[272,384]{1,0:T(8,128)(2,1)S(1)}, bf16[272,384]{1,0:T(8,128)(2,1)S(1)}, u32[]{:S(2)}, u32[]{:S(2)}) collective-permute-start(bf16[272,384]{1,0:T(8,128)(2,1)S(1)} %shard_map.77.before), channel_id=1, source_target_pairs={{0,192},{1,193},{2,194},{3,195},{4,196},{5,197},{6,198},{7,199},{8... | collective-permute-start | bytes 626696 | tf_op jit(solution)/shard_map/ppermute | solution.py:423
  21.2 9.4 %collective-permute-start.7 = (bf16[272,384]{1,0:T(8,128)(2,1)S(1)}, bf16[272,384]{1,0:T(8,128)(2,1)S(1)}, u32[]{:S(2)}, u32[]{:S(2)}) collective-permute-start(bf16[272,384]{1,0:T(8,128)(2,1)S(1)} %shard_map.77.before), channel_id=1, source_target_pairs={{0,128},{1,129},{2,130},{3,131},{4,132},{5,133},{6,134},{7,135},{8... | collective-permute-start | bytes 626696 | tf_op jit(solution)/shard_map/ppermute | solution.py:423
  21.8 12.0 %collective-permute-start.5 = (bf16[272,384]{1,0:T(8,128)(2,1)S(1)}, bf16[272,384]{1,0:T(8,128)(2,1)S(1)}, u32[]{:S(2)}, u32[]{:S(2)}) collective-permute-start(bf16[272,384]{1,0:T(8,128)(2,1)S(1)} %shard_map.77.before), channel_id=1, source_target_pairs={{0,64},{1,65},{2,66},{3,67},{4,68},{5,69},{6,70},{7,71},{8,72},{9,... | collective-permute-start | bytes 626696 | tf_op jit(solution)/shard_map/ppermute | solution.py:423
  25.8 16.1 %copy-start = (s32[3]{0:T(128)S(1)}, s32[3]{0:T(128)}, u32[]{:S(2)}) copy-start(s32[3]{0:T(128)} %pad_add_fusion.place) | copy-start | bytes 40
  25.9 10.3 %collective-permute-start.15 = (bf16[272,384]{1,0:T(8,128)(2,1)S(1)}, bf16[272,384]{1,0:T(8,128)(2,1)S(1)}, u32[]{:S(2)}, u32[]{:S(2)}) collective-permute-start(bf16[272,384]{1,0:T(8,128)(2,1)S(1)} %get-tuple-element.20), channel_id=1, source_target_pairs={{0,192},{1,193},{2,194},{3,195},{4,196},{5,197},{6,198},{7,199},{8... | collective-permute-start | bytes 626696 | tf_op jit(solution)/shard_map/ppermute | solution.py:423
  28.9 8.8 %collective-permute-start.13 = (bf16[272,384]{1,0:T(8,128)(2,1)S(1)}, bf16[272,384]{1,0:T(8,128)(2,1)S(1)}, u32[]{:S(2)}, u32[]{:S(2)}) collective-permute-start(bf16[272,384]{1,0:T(8,128)(2,1)S(1)} %get-tuple-element.20), channel_id=1, source_target_pairs={{0,128},{1,129},{2,130},{3,131},{4,132},{5,133},{6,134},{7,135},{8... | collective-permute-start | bytes 626696 | tf_op jit(solution)/shard_map/ppermute | solution.py:423
  29.6 10.3 %collective-permute-start.11 = (bf16[272,384]{1,0:T(8,128)(2,1)S(1)}, bf16[272,384]{1,0:T(8,128)(2,1)S(1)}, u32[]{:S(2)}, u32[]{:S(2)}) collective-permute-start(bf16[272,384]{1,0:T(8,128)(2,1)S(1)} %get-tuple-element.20), channel_id=1, source_target_pairs={{0,64},{1,65},{2,66},{3,67},{4,68},{5,69},{6,70},{7,71},{8,72},{9,... | collective-permute-start | bytes 626696 | tf_op jit(solution)/shard_map/ppermute | solution.py:423
  30.6 9.3 %collective-permute-start.10 = (bf16[272,384]{1,0:T(8,128)(2,1)S(1)}, bf16[272,384]{1,0:T(8,128)(2,1)S(1)}, u32[]{:S(2)}, u32[]{:S(2)}) collective-permute-start(bf16[272,384]{1,0:T(8,128)(2,1)S(1)} %collective-permute-done.9.refs_6_), channel_id=1, source_target_pairs={{0,1},{1,0},{2,3},{3,2},{4,5},{5,4},{6,7},{7,6},{8,9},{9,8},{10,11... | collective-permute-start | bytes 626696 | tf_op jit(solution)/shard_map/ppermute | solution.py:424
  33.8 6.6 %collective-permute-start.8 = (bf16[272,384]{1,0:T(8,128)(2,1)S(1)}, bf16[272,384]{1,0:T(8,128)(2,1)S(1)}, u32[]{:S(2)}, u32[]{:S(2)}) collective-permute-start(bf16[272,384]{1,0:T(8,128)(2,1)S(1)} %collective-permute-done.7.refs_4_), channel_id=1, source_target_pairs={{0,1},{1,0},{2,3},{3,2},{4,5},{5,4},{6,7},{7,6},{8,9},{9,8},{10,11... | collective-permute-start | bytes 626696 | tf_op jit(solution)/shard_map/ppermute | solution.py:424
  36.1 5.8 %collective-permute-start.4 = (bf16[544,384]{1,0:T(8,128)(2,1)S(1)}, bf16[544,384]{1,0:T(8,128)(2,1)S(1)}, u32[]{:S(2)}, u32[]{:S(2)}) collective-permute-start(bf16[544,384]{1,0:T(8,128)(2,1)S(1)} %get-tuple-element.19.refs_0_), channel_id=1, source_target_pairs={{0,1},{1,0},{2,3},{3,2},{4,5},{5,4},{6,7},{7,6},{8,9},{9,8},{10,11... | collective-permute-start | bytes 1253384 | tf_op jit(solution)/shard_map/ppermute | solution.py:420
  37.8 2.7 %collective-permute-start.6 = (bf16[272,384]{1,0:T(8,128)(2,1)S(1)}, bf16[272,384]{1,0:T(8,128)(2,1)S(1)}, u32[]{:S(2)}, u32[]{:S(2)}) collective-permute-start(bf16[272,384]{1,0:T(8,128)(2,1)S(1)} %collective-permute-done.5.refs_2_), channel_id=1, source_target_pairs={{0,1},{1,0},{2,3},{3,2},{4,5},{5,4},{6,7},{7,6},{8,9},{9,8},{10,11... | collective-permute-start | bytes 626696 | tf_op jit(solution)/shard_map/ppermute | solution.py:424
  39.9 1.5 %collective-permute-start.16 = (bf16[272,384]{1,0:T(8,128)(2,1)S(1)}, bf16[272,384]{1,0:T(8,128)(2,1)S(1)}, u32[]{:S(2)}, u32[]{:S(2)}) collective-permute-start(bf16[272,384]{1,0:T(8,128)(2,1)S(1)} %collective-permute-done.15.refs_12_), channel_id=1, source_target_pairs={{0,1},{1,0},{2,3},{3,2},{4,5},{5,4},{6,7},{7,6},{8,9},{9,8},{10,11... | collective-permute-start | bytes 626696 | tf_op jit(solution)/shard_map/ppermute | solution.py:424
  39.9 1.8 %collective-permute-start.14 = (bf16[272,384]{1,0:T(8,128)(2,1)S(1)}, bf16[272,384]{1,0:T(8,128)(2,1)S(1)}, u32[]{:S(2)}, u32[]{:S(2)}) collective-permute-start(bf16[272,384]{1,0:T(8,128)(2,1)S(1)} %collective-permute-done.13.refs_10_), channel_id=1, source_target_pairs={{0,1},{1,0},{2,3},{3,2},{4,5},{5,4},{6,7},{7,6},{8,9},{9,8},{10,11... | collective-permute-start | bytes 626696 | tf_op jit(solution)/shard_map/ppermute | solution.py:424
  40.4 1.5 %collective-permute-start.12 = (bf16[272,384]{1,0:T(8,128)(2,1)S(1)}, bf16[272,384]{1,0:T(8,128)(2,1)S(1)}, u32[]{:S(2)}, u32[]{:S(2)}) collective-permute-start(bf16[272,384]{1,0:T(8,128)(2,1)S(1)} %collective-permute-done.11.refs_8_), channel_id=1, source_target_pairs={{0,1},{1,0},{2,3},{3,2},{4,5},{5,4},{6,7},{7,6},{8,9},{9,8},{10,11... | collective-permute-start | bytes 626696 | tf_op jit(solution)/shard_map/ppermute | solution.py:424
  46.8 1.3 %collective-permute-start.17 = (f32[8,256]{1,0:T(8,128)S(1)}, f32[8,256]{1,0:T(8,128)S(1)}, u32[]{:S(2)}, u32[]{:S(2)}) collective-permute-start(f32[8,256]{1,0:T(8,128)S(1)} %shard_map.79), channel_id=1, source_target_pairs={{0,1},{1,0},{2,3},{3,2},{4,5},{5,4},{6,7},{7,6},{8,9},{9,8},{10,11... | collective-permute-start | bytes 24584 | tf_op jit(solution)/shard_map/ppermute | solution.py:426
  48.1 3.7 %collective-permute-start.20 = (f32[16,256]{1,0:T(8,128)S(1)}, f32[16,256]{1,0:T(8,128)S(1)}, u32[]{:S(2)}, u32[]{:S(2)}) collective-permute-start(f32[16,256]{1,0:T(8,128)S(1)} %pad_maximum_fusion.refs_14_), channel_id=1, source_target_pairs={{0,192},{1,193},{2,194},{3,195},{4,196},{5,197},{6,198},{7,199},{8... | collective-permute-start | bytes 49160 | tf_op jit(solution)/shard_map/ppermute | solution.py:427
  48.6 5.2 %collective-permute-start.19 = (f32[16,256]{1,0:T(8,128)S(1)}, f32[16,256]{1,0:T(8,128)S(1)}, u32[]{:S(2)}, u32[]{:S(2)}) collective-permute-start(f32[16,256]{1,0:T(8,128)S(1)} %pad_maximum_fusion.refs_14_), channel_id=1, source_target_pairs={{0,128},{1,129},{2,130},{3,131},{4,132},{5,133},{6,134},{7,135},{8... | collective-permute-start | bytes 49160 | tf_op jit(solution)/shard_map/ppermute | solution.py:427
  49.0 5.6 %collective-permute-start.18 = (f32[16,256]{1,0:T(8,128)S(1)}, f32[16,256]{1,0:T(8,128)S(1)}, u32[]{:S(2)}, u32[]{:S(2)}) collective-permute-start(f32[16,256]{1,0:T(8,128)S(1)} %pad_maximum_fusion.refs_14_), channel_id=1, source_target_pairs={{0,64},{1,65},{2,66},{3,67},{4,68},{5,69},{6,70},{7,71},{8,72},{9,... | collective-permute-start | bytes 49160 | tf_op jit(solution)/shard_map/ppermute | solution.py:427
  58.1 11.8 %collective-permute-start.21 = (bf16[144,128]{1,0:T(8,128)(2,1)S(1)}, bf16[144,128]{1,0:T(8,128)(2,1)S(1)}, u32[]{:S(2)}, u32[]{:S(2)}) collective-permute-start(bf16[144,128]{1,0:T(8,128)(2,1)S(1)} %get-tuple-element.21), channel_id=1, source_target_pairs={{0,0},{8,1},{2,2},{10,3},{4,4},{12,5},{6,6},{14,7},{1,8},{9,9},{3,... | collective-permute-start | bytes 110600 | tf_op jit(solution)/shard_map/ppermute | solution.py:429
  66.3 4.3 %collective-permute-start.22 = (bf16[144,128]{1,0:T(8,128)(2,1)S(1)}, bf16[144,128]{1,0:T(8,128)(2,1)S(1)}, u32[]{:S(2)}, u32[]{:S(2)}) collective-permute-start(bf16[144,128]{1,0:T(8,128)(2,1)S(1)} %get-tuple-element.22), channel_id=1, source_target_pairs={{16,0},{24,1},{18,2},{26,3},{20,4},{28,5},{22,6},{30,7},{17,8},{25... | collective-permute-start | bytes 110600 | tf_op jit(solution)/shard_map/ppermute | solution.py:429
  66.4 6.5 %collective-permute-start.23 = (bf16[144,128]{1,0:T(8,128)(2,1)S(1)}, bf16[144,128]{1,0:T(8,128)(2,1)S(1)}, u32[]{:S(2)}, u32[]{:S(2)}) collective-permute-start(bf16[144,128]{1,0:T(8,128)(2,1)S(1)} %get-tuple-element.23), channel_id=1, source_target_pairs={{32,0},{40,1},{34,2},{42,3},{36,4},{44,5},{38,6},{46,7},{33,8},{41... | collective-permute-start | bytes 110600 | tf_op jit(solution)/shard_map/ppermute | solution.py:429
  69.0 6.4 %collective-permute-start.24 = (bf16[144,128]{1,0:T(8,128)(2,1)S(1)}, bf16[144,128]{1,0:T(8,128)(2,1)S(1)}, u32[]{:S(2)}, u32[]{:S(2)}) collective-permute-start(bf16[144,128]{1,0:T(8,128)(2,1)S(1)} %get-tuple-element.24), channel_id=1, source_target_pairs={{48,0},{56,1},{50,2},{58,3},{52,4},{60,5},{54,6},{62,7},{49,8},{57... | collective-permute-start | bytes 110600 | tf_op jit(solution)/shard_map/ppermute | solution.py:429
  75.4 1.2 %collective-permute-start.25 = (f32[8,128]{1,0:T(8,128)S(1)}, f32[8,128]{1,0:T(8,128)S(1)}, u32[]{:S(2)}, u32[]{:S(2)}) collective-permute-start(f32[8,128]{1,0:T(8,128)S(1)} %bitcast_reduce_fusion), channel_id=1, source_target_pairs={{0,1},{1,0},{2,3},{3,2},{4,5},{5,4},{6,7},{7,6},{8,9},{9,8},{10,11... | collective-permute-start | bytes 12296 | tf_op jit(solution)/shard_map/ppermute | solution.py:432
  76.6 5.3 %collective-permute-start.28 = (f32[8,128]{1,0:T(8,128)S(1)}, f32[8,128]{1,0:T(8,128)S(1)}, u32[]{:S(2)}, u32[]{:S(2)}) collective-permute-start(f32[8,128]{1,0:T(8,128)S(1)} %add.34), channel_id=1, source_target_pairs={{0,6},{1,7},{2,4},{3,5},{4,2},{5,3},{6,0},{7,1},{8,14},{9,15},{10,... | collective-permute-start | bytes 12296 | tf_op jit(solution)/shard_map/ppermute | solution.py:433
  79.3 5.1 %collective-permute-start.27 = (f32[8,128]{1,0:T(8,128)S(1)}, f32[8,128]{1,0:T(8,128)S(1)}, u32[]{:S(2)}, u32[]{:S(2)}) collective-permute-start(f32[8,128]{1,0:T(8,128)S(1)} %add.34), channel_id=1, source_target_pairs={{0,4},{1,5},{2,6},{3,7},{4,0},{5,1},{6,2},{7,3},{8,12},{9,13},{10,... | collective-permute-start | bytes 12296 | tf_op jit(solution)/shard_map/ppermute | solution.py:433
  80.1 4.3 %collective-permute-start.26 = (f32[8,128]{1,0:T(8,128)S(1)}, f32[8,128]{1,0:T(8,128)S(1)}, u32[]{:S(2)}, u32[]{:S(2)}) collective-permute-start(f32[8,128]{1,0:T(8,128)S(1)} %add.34), channel_id=1, source_target_pairs={{0,2},{1,3},{2,0},{3,1},{4,6},{5,7},{6,4},{7,5},{8,10},{9,11},{10,... | collective-permute-start | bytes 12296 | tf_op jit(solution)/shard_map/ppermute | solution.py:433
where the time goes:
time: 86.7 us; the launch traced here: 86.8 us
  starting transfers between devices  39.9 us (46%)
  waiting for transfers between devices  30.7 us (35%)
  Pallas kernels  12.4 us (14%)
  between operations  2.53 us (3%)
  other arithmetic  1.27 us (1%)
    ppermute x4, starting transfers between devices, per_device(): backs = [lax.ppermute(grads[j], AXES, collect_pairs(j)) for j in range(4)]  11.8 us
    ppermute x4, starting transfers between devices, per_device(): gots = [lax.ppermute(sends[j], AXES, spread_pairs(j)) for j in ORDER]  11.5 us
    ppermute x6, starting transfers between devices, per_device(): part = lax.ppermute(mine, AXES, y_pairs(step))  9.38 us
    ppermute x6, waiting for transfers between devices, per_device(): part = lax.ppermute(mine, AXES, y_pairs(step))  9.3 us
    ppermute x4, waiting for transfers between devices, per_device(): gots = [lax.ppermute(sends[j], AXES, spread_pairs(j)) for j in ORDER]  5.55 us
    ppermute x4, waiting for transfers between devices, per_device(): backs = [lax.ppermute(grads[j], AXES, collect_pairs(j)) for j in range(4)]  5.48 us
    pallas_call x1, Pallas kernels, call_norm(): pl.pallas_call(norm_kernel, out_shape=jax.ShapeDtypeStruct((8, TILE), F32...  4.91 us
    ppermute x3, waiting for transfers between devices, per_device(): lax.ppermute(both, AXES, y_pairs(step))  4.38 us
  transfers between devices with their start and end apart: 29, of which 18 were waited for; matrix products, arithmetic and copies ran while one was open for 0% of the time, Pallas kernels for 2%

commit v1 on v0

--- a/solution.py
+++ b/solution.py
@@ -31,7 +31,6 @@
 BF16 = jnp.bfloat16
 AXES = ("seq", "head")
 ALL = pl.BlockSpec(memory_space=pltpu.VMEM)
-SMEM = pl.BlockSpec(memory_space=pltpu.SMEM)
 ANY = pl.BlockSpec(memory_space=pl.ANY)
 
 
@@ -57,6 +56,10 @@
     return [(target, source) for source, target in spread_pairs(j)]
 
 
+def near_pairs(sign):
+    return pairs_of(lambda y, z, x, c: ((y + sign * (1 - 2 * c)) % NY, z, x, c))
+
+
 def y_pairs(step):
     return pairs_of(lambda y, z, x, c: ((y + step) % NY, z, x, c))
 
@@ -68,6 +71,11 @@
 CORE_PAIRS = pairs_of(lambda y, z, x, c: (y, z, x, 1 - c))
 
 
+def placed():
+    seq, head = lax.axis_index("seq"), lax.axis_index("head")
+    return (lax.div(seq, NZ), lax.rem(seq, NZ), lax.rem(head, 2))
+
+
 def params(limit=VMEM_LIMIT):
     return pltpu.CompilerParams(vmem_limit_bytes=limit)
 
@@ -76,7 +84,7 @@
     return lax.dot_general(left, right, (((1,), (1,)), ((), ())), preferred_element_type=F32)
 
 
-def send_kernel(place, tq, tk, sq, sk, doc, o0, o1, o2, o3, held, docs, sems):
+def send_kernel(tq, tk, sq, sk, doc, o0, o1, o2, o3, held, docs, sems):
     copies = []
     for m, (teach, pupil) in enumerate(((tq, sq), (tq, sq), (tk, sk), (tk, sk))):
         h = m % 2
@@ -85,17 +93,19 @@
         copies.append((pupil.at[:, pl.ds(h * HDIM, HDIM)], block.at[:, pl.ds(TDIM, HDIM)]))
     copies.append((doc, docs))
     copies = [pltpu.make_async_copy(src, dst, sems.at[n]) for n, (src, dst) in enumerate(copies)]
-    for copy in copies:
+    for copy in reversed(copies):
         copy.start()
+    copies.pop().wait()
+    below = docs[...] < lax.broadcasted_iota(jnp.int32, (128, ROWS), 0)
+    counts = nt_dot(jnp.ones((16, ROWS), BF16), below.astype(F32).astype(BF16))
+    for out in (o0, o1, o2, o3):
+        out[ROWS:ROWS + 16, 0:128] = counts.astype(BF16)
+        out[ROWS:ROWS + 16, 128:WIDE] = jnp.zeros((16, 256), BF16)
     for copy in copies:
         copy.wait()
-    below = docs[...] < lax.broadcasted_iota(jnp.int32, (128, ROWS), 0)
-    counts = nt_dot(jnp.ones((16, ROWS), BF16), below.astype(F32).astype(BF16))
-    b = place[1] // 2
+    b = placed()[1] // 2
     for j, out in enumerate((o0, o1, o2, o3)):
         out[0:ROWS, :] = held[(b + j) % 4]
-        out[ROWS:ROWS + 16, 0:128] = counts.astype(BF16)
-        out[ROWS:ROWS + 16, 128:WIDE] = jnp.zeros((16, 256), BF16)
 
 
 def pack_kernel(first, second, out):
@@ -116,18 +126,18 @@
         for chunk in range(2):
             found.append((parts[other], chunk * PIECE, 0, other, chunk))
     for n, part in enumerate(parts[2:]):
-        chunk, i, other = n // 6, n % 6 // 2 + 1, n % 2
-        found.append((part, 0, i, other, chunk))
+        chunk, step, other = n // 6, (1, -1, 2)[n % 6 // 2], n % 2
+        found.append((part, 0, step, other, chunk))
     return found
 
 
-def assemble(place, parts, rows):
-    y, core = place[0], place[2]
-    m = place[1] // 2
+def assemble(parts, rows):
+    y, z, core = placed()
+    m = z // 2
     total = jnp.zeros((16, 128), F32)
-    for part, base, i, other, chunk in pieces_of(parts):
+    for part, base, step, other, chunk in pieces_of(parts):
         from_core = core if other == 0 else 1 - core
-        from_y = (y - i + NY) % NY
+        from_y = (y - step * (1 - 2 * from_core) + NY) % NY
         for k in range(2):
             b = (m - ORDER[2 * chunk + k] + 4) % 4
             at = (from_y * 8 + 2 * b + from_core) * ROWS
@@ -152,11 +162,12 @@
     return values.reshape(TILE // 8, 8, TILE)
 
 
-def norm_kernel(place, *refs):
+def norm_kernel(*refs):
     parts, out = refs[:14], refs[14]
     rows, scores_t, scores_s = refs[15:]
-    bounds = assemble(place, parts, rows)
-    r = place[0] * 2 + place[2]
+    bounds = assemble(parts, rows)
+    y, z, core = placed()
+    r = y * 2 + core
     bounds_down = jnp.transpose(jnp.broadcast_to(bounds, (128, 128)))[0:16, 0:1]
     out[...] = jnp.zeros_like(out)
     for half in range(2):
@@ -236,12 +247,12 @@
         out[4 + half:5 + half, :] = row_kl
 
 
-def grad_kernel(place, *refs):
+def grad_kernel(*refs):
     parts, packets, outs = refs[:14], refs[14:18], refs[18:22]
     rows, norms, row_norm, acc, mine = refs[22:]
-    bounds = assemble(place, parts, rows)
-    y, core = place[0], place[2]
-    m = place[1] // 2
+    bounds = assemble(parts, rows)
+    y, z, core = placed()
+    m = z // 2
     kl = jnp.zeros((1, TILE), F32)
     for i, packet in enumerate(packets):
         for other in range(2):
@@ -339,8 +350,8 @@
         outs[j][ROWS:ROWS + 16, :] = tail.astype(BF16)
 
 
-def finish_kernel(place, g0, g1, g2, g3, grad_q, grad_k, held):
-    b = place[1] // 2
+def finish_kernel(g0, g1, g2, g3, grad_q, grad_k, held):
+    b = placed()[1] // 2
     for j, got in enumerate((g0, g1, g2, g3)):
         held[(b + j) % 4] = got[0:ROWS, :]
     for m in range(4):
@@ -349,11 +360,11 @@
         out[:, h * HDIM:(h + 1) * HDIM] = held[m]
 
 
-def call_norm(place, parts):
+def call_norm(parts):
     return pl.pallas_call(
         norm_kernel,
         out_shape=jax.ShapeDtypeStruct((8, TILE), F32),
-        in_specs=[SMEM] + [ALL] * 14,
+        in_specs=[ALL] * 14,
         out_specs=ALL,
         scratch_shapes=[
             pltpu.VMEM((TOKENS, WIDE), BF16),
@@ -361,14 +372,14 @@
             pltpu.VMEM((TOKENS, TILE), F32),
         ],
         compiler_params=params(),
-    )(place, *parts)
-
-
-def call_grad(place, parts, packets):
+    )(*parts)
+
+
+def call_grad(parts, packets):
     return pl.pallas_call(
         grad_kernel,
         out_shape=[jax.ShapeDtypeStruct((ROWS + 16, HDIM), BF16)] * 4,
-        in_specs=[SMEM] + [ALL] * 18,
+        in_specs=[ALL] * 18,
         out_specs=[ALL] * 4,
         scratch_shapes=[
             pltpu.VMEM((TOKENS, WIDE), BF16),
@@ -378,18 +389,15 @@
             pltpu.VMEM((BLOCK, WIDE), BF16),
         ],
         compiler_params=params(),
-    )(place, *parts, *packets)
+    )(*parts, *packets)
 
 
 def per_device(teacher_query, teacher_key, student_query, student_key, doc_ids):
-    seq, head = lax.axis_index("seq"), lax.axis_index("head")
-    place = jnp.stack([seq // NZ, seq % NZ, head % 2]).astype(jnp.int32)
-
     block = jax.ShapeDtypeStruct((ROWS + 16, WIDE), BF16)
     sends = pl.pallas_call(
         send_kernel,
         out_shape=[block] * 4,
-        in_specs=[SMEM] + [ANY] * 5,
+        in_specs=[ANY] * 5,
         out_specs=[ALL] * 4,
         scratch_shapes=[
             pltpu.VMEM((4, ROWS, WIDE), BF16),
@@ -397,7 +405,7 @@
             pltpu.SemaphoreType.DMA((9,)),
         ],
         compiler_params=params(60 * 1024 * 1024),
-    )(place, teacher_query, teacher_key, student_query, student_key, doc_ids.reshape(1, ROWS))
+    )(teacher_query, teacher_key, student_query, student_key, doc_ids.reshape(1, ROWS))
     gots = [lax.ppermute(sends[j], AXES, spread_pairs(j)) for j in ORDER]
     piece = jax.ShapeDtypeStruct((PIECE, WIDE), BF16)
     own_a = pl.pallas_call(
@@ -418,15 +426,18 @@
         compiler_params=params(),
     )(own_a, *gots[2:4])
     parts = [own, lax.ppermute(own, AXES, CORE_PAIRS)]
-    for mine in (own_a, own_b):
-        for step in (1, 2, 3):
-            part = lax.ppermute(mine, AXES, y_pairs(step))
+    nears = [lax.ppermute(mine, AXES, near_pairs(1)) for mine in (own_a, own_b)]
+    fars = [lax.ppermute(mine, AXES, near_pairs(-1)) for mine in (own_a, own_b)]
+    opposites = [lax.ppermute(near, AXES, near_pairs(1)) for near in nears]
+    for trio in zip(nears, fars, opposites):
+        for part in trio:
             parts += [part, lax.ppermute(part, AXES, CORE_PAIRS)]
-    packet = call_norm(place, parts)
+    packet = call_norm(parts)
     both = jnp.concatenate([packet, lax.ppermute(packet, AXES, CORE_PAIRS)])
     packets = [both] + [lax.ppermute(both, AXES, y_pairs(step)) for step in (1, 2, 3)]
-    grads = call_grad(place, parts, packets)
-    backs = [lax.ppermute(grads[j], AXES, collect_pairs(j)) for j in range(4)]
+    grads = call_grad(parts, packets)
+    backs = {j: lax.ppermute(grads[j], AXES, collect_pairs(j)) for j in (2, 3, 1, 0)}
+    backs = [backs[j] for j in range(4)]
     kl = sum(back[ROWS:ROWS + 16].astype(F32) for back in backs)
     kl = jnp.sum(kl.reshape(2, 8, HDIM), axis=0)
     kl = kl + lax.ppermute(kl, AXES, CORE_PAIRS)
@@ -436,11 +447,11 @@
     grad_query, grad_key = pl.pallas_call(
         finish_kernel,
         out_shape=[half_grad, half_grad],
-        in_specs=[SMEM] + [ALL] * 4,
+        in_specs=[ALL] * 4,
         out_specs=[ALL] * 2,
         scratch_shapes=[pltpu.VMEM((4, ROWS, HDIM), BF16)],
         compiler_params=params(),
-    )(place, *backs)
+    )(*backs)
     return (kl_loss, grad_query, grad_key)
 
 

time: 86.7 us -> 84.5 us (0.975)
  starting transfers between devices: 39.9 us -> 35 us
  waiting for transfers between devices: 30.7 us -> 35 us
  Pallas kernels: 12.4 us -> 11.1 us
    ppermute x10, starting transfers between devices: 21.2 us -> 13.6 us  [the longest x4 6.79 us: per_device(): lax.ppermute(grads[j], AXES, collect_pairs(j))]
    pallas_call x1, Pallas kernels: 4.91 us -> 1.99 us  [call_norm(): pl.pallas_call(norm_kernel, out_shape=jax.ShapeDtypeStruct((8, TILE), F32...]
    pallas_call x1, Pallas kernels: 3.53 us -> 6.42 us  [call_grad(): pl.pallas_call(grad_kernel, out_shape=[jax.ShapeDtypeStruct((ROWS + 16, H...]
    ppermute x3, starting transfers between devices: 2.03 us -> 3.72 us  [per_device(): lax.ppermute(both, AXES, y_pairs(step))]
    ppermute x10, waiting for transfers between devices: 14.8 us -> 16.4 us  [the longest x2 6.26 us: per_device(): opposites = [lax.ppermute(near, AXES, near_pairs(1)) for near in nears]]
    ppermute x4, waiting for transfers between devices: 5.55 us -> 7.15 us  [per_device(): gots = [lax.ppermute(sends[j], AXES, spread_pairs(j)) for j in ORDER]]
    ppermute x6, starting transfers between devices: 0.61 us -> 1.49 us  [per_device(): parts += [part, lax.ppermute(part, AXES, CORE_PAIRS)]]
  transfers between devices with their start and end apart: 29 -> 29, of which waited for: 18 -> 15; matrix products, arithmetic and copies ran while one was open for 0% -> 0% of each run, Pallas kernels for 2% -> 1%
where the time goes in v1:
time: 84.5 us; the launch traced here: 84.2 us
  starting transfers between devices  35 us (41%)
  waiting for transfers between devices  35 us (41%)
  Pallas kernels  11.1 us (13%)
  between operations  2.5 us (3%)
    ppermute x4, starting transfers between devices, per_device(): gots = [lax.ppermute(sends[j], AXES, spread_pairs(j)) for j in ORDER]  11.5 us
    ppermute x4, waiting for transfers between devices, per_device(): gots = [lax.ppermute(sends[j], AXES, spread_pairs(j)) for j in ORDER]  7.15 us
    ppermute x4, starting transfers between devices, per_device(): lax.ppermute(grads[j], AXES, collect_pairs(j))  6.79 us
    pallas_call x1, Pallas kernels, call_grad(): pl.pallas_call(grad_kernel, out_shape=[jax.ShapeDtypeStruct((ROWS + 16, H...  6.42 us
    ppermute x2, waiting for transfers between devices, per_device(): opposites = [lax.ppermute(near, AXES, near_pairs(1)) for near in nears]  6.26 us
    ppermute x2, starting transfers between devices, per_device(): fars = [lax.ppermute(mine, AXES, near_pairs(-1)) for mine in (own_a, own_b)]  6.18 us
    ppermute x3, waiting for transfers between devices, per_device(): lax.ppermute(both, AXES, y_pairs(step))  4.95 us
    ppermute x4, waiting for transfers between devices, per_device(): lax.ppermute(grads[j], AXES, collect_pairs(j))  4.46 us
  transfers between devices with their start and end apart: 29, of which 15 were waited for; matrix products, arithmetic and copies ran while one was open for 0% of the time, Pallas kernels for 1%

profile of v1, /device:TPU:32, one launch (start us, length us, event | category | flops | bytes accessed | tf_op | source)
XLA Modules:
  0.0 84.2 jit_solution(16090064990565131651)
XLA Ops:
  0.6 1.9 %shard_map.76 = (bf16[144,384]{1,0:T(8,128)(2,1)}, bf16[144,384]{1,0:T(8,128)(2,1)}, bf16[144,384]{1,0:T(8,128)(2,1)}, bf16[144,384]{1,0:T(8,128)(2,1)}) custom-call(bf16[128,512]{1,0:T(8,128)(2,1)} %tq.1, bf16[128,512]{1,0:T(8,128)(2,1)} %tk.1, bf16[128,256]{1,0:T(8,128)(2,1)} %sq.1, bf16[128,256]{1,0:T(8,128)(2,1)} %sk.1, s32[1,128]{1,0:T(1,128)} %bitcast.3), custom_call_target="tpu_custom_call" | custom-call | tf_op jit(solution)/shard_map/pallas_call | solution.py:397
  2.6 1.9 %collective-permute-start = (bf16[144,384]{1,0:T(8,128)(2,1)}, bf16[144,384]{1,0:T(8,128)(2,1)S(1)}, u32[]{:S(2)}, u32[]{:S(2)}) collective-permute-start(bf16[144,384]{1,0:T(8,128)(2,1)} %get-tuple-element.15), channel_id=1, source_target_pairs={{0,0},{1,8},{2,2},{3,10},{4,4},{5,12},{6,6},{7,14},{8,1},{9,9},{10... | collective-permute-start | bytes 331784 | tf_op jit(solution)/shard_map/ppermute | solution.py:409
  4.5 3.6 %collective-permute-start.1 = (bf16[144,384]{1,0:T(8,128)(2,1)}, bf16[144,384]{1,0:T(8,128)(2,1)S(1)}, u32[]{:S(2)}, u32[]{:S(2)}) collective-permute-start(bf16[144,384]{1,0:T(8,128)(2,1)} %get-tuple-element.16), channel_id=1, source_target_pairs={{0,16},{1,24},{2,18},{3,26},{4,20},{5,28},{6,22},{7,30},{8,17},{9,... | collective-permute-start | bytes 331784 | tf_op jit(solution)/shard_map/ppermute | solution.py:409
  8.1 3.1 %collective-permute-start.2 = (bf16[144,384]{1,0:T(8,128)(2,1)}, bf16[144,384]{1,0:T(8,128)(2,1)S(1)}, u32[]{:S(2)}, u32[]{:S(2)}) collective-permute-start(bf16[144,384]{1,0:T(8,128)(2,1)} %get-tuple-element.17), channel_id=1, source_target_pairs={{0,48},{1,56},{2,50},{3,58},{4,52},{5,60},{6,54},{7,62},{8,49},{9,... | collective-permute-start | bytes 331784 | tf_op jit(solution)/shard_map/ppermute | solution.py:409
  11.2 2.9 %collective-permute-start.3 = (bf16[144,384]{1,0:T(8,128)(2,1)}, bf16[144,384]{1,0:T(8,128)(2,1)S(1)}, u32[]{:S(2)}, u32[]{:S(2)}) collective-permute-start(bf16[144,384]{1,0:T(8,128)(2,1)} %get-tuple-element.18), channel_id=1, source_target_pairs={{0,32},{1,40},{2,34},{3,42},{4,36},{5,44},{6,38},{7,46},{8,33},{9,... | collective-permute-start | bytes 331784 | tf_op jit(solution)/shard_map/ppermute | solution.py:409
  14.1 2.5 %collective-permute-done.1.second = bf16[144,384]{1,0:T(8,128)(2,1)S(1)} collective-permute-done((bf16[144,384]{1,0:T(8,128)(2,1)}, bf16[144,384]{1,0:T(8,128)(2,1)S(1)}, u32[]{:S(2)}, u32[]{:S(2)}) %collective-permute-start.1) | collective-permute-done | bytes 110624 | tf_op jit(solution)/shard_map/ppermute | solution.py:409
  16.6 3.1 %collective-permute-start.7 = (bf16[272,384]{1,0:T(8,128)(2,1)S(1)}, bf16[272,384]{1,0:T(8,128)(2,1)S(1)}, u32[]{:S(2)}, u32[]{:S(2)}) collective-permute-start(bf16[272,384]{1,0:T(8,128)(2,1)S(1)} %shard_map.77.before), channel_id=1, source_target_pairs={{0,192},{1,65},{2,194},{3,67},{4,196},{5,69},{6,198},{7,71},{8,200... | collective-permute-start | bytes 626696 | tf_op jit(solution)/shard_map/ppermute | solution.py:430
  19.7 4.6 %collective-permute-done.3.second = bf16[144,384]{1,0:T(8,128)(2,1)S(1)} collective-permute-done((bf16[144,384]{1,0:T(8,128)(2,1)}, bf16[144,384]{1,0:T(8,128)(2,1)S(1)}, u32[]{:S(2)}, u32[]{:S(2)}) %collective-permute-start.3) | collective-permute-done | bytes 110624 | tf_op jit(solution)/shard_map/ppermute | solution.py:409
  24.4 3.1 %collective-permute-start.13 = (bf16[272,384]{1,0:T(8,128)(2,1)S(1)}, bf16[272,384]{1,0:T(8,128)(2,1)S(1)}, u32[]{:S(2)}, u32[]{:S(2)}) collective-permute-start(bf16[272,384]{1,0:T(8,128)(2,1)S(1)} %get-tuple-element.20), channel_id=1, source_target_pairs={{0,192},{1,65},{2,194},{3,67},{4,196},{5,69},{6,198},{7,71},{8,200... | collective-permute-start | bytes 626696 | tf_op jit(solution)/shard_map/ppermute | solution.py:430
  28.6 2.2 %collective-permute-done.13.refs_10_ = bf16[272,384]{1,0:T(8,128)(2,1)S(1)} collective-permute-done((bf16[272,384]{1,0:T(8,128)(2,1)S(1)}, bf16[272,384]{1,0:T(8,128)(2,1)S(1)}, u32[]{:S(2)}, u32[]{:S(2)}) %collective-permute-start.13) | collective-permute-done | bytes 208928 | tf_op jit(solution)/shard_map/ppermute | solution.py:430
  31.1 3.5 %collective-permute-done.11.refs_8_ = bf16[272,384]{1,0:T(8,128)(2,1)S(1)} collective-permute-done((bf16[272,384]{1,0:T(8,128)(2,1)S(1)}, bf16[272,384]{1,0:T(8,128)(2,1)S(1)}, u32[]{:S(2)}, u32[]{:S(2)}) %collective-permute-start.11) | collective-permute-done | bytes 208928 | tf_op jit(solution)/shard_map/ppermute | solution.py:429
  34.8 2.0 %collective-permute-done.9.refs_6_ = bf16[272,384]{1,0:T(8,128)(2,1)S(1)} collective-permute-done((bf16[272,384]{1,0:T(8,128)(2,1)S(1)}, bf16[272,384]{1,0:T(8,128)(2,1)S(1)}, u32[]{:S(2)}, u32[]{:S(2)}) %collective-permute-start.9) | collective-permute-done | bytes 208928 | tf_op jit(solution)/shard_map/ppermute | solution.py:431
  37.3 4.3 %collective-permute-done.15.refs_12_ = bf16[272,384]{1,0:T(8,128)(2,1)S(1)} collective-permute-done((bf16[272,384]{1,0:T(8,128)(2,1)S(1)}, bf16[272,384]{1,0:T(8,128)(2,1)S(1)}, u32[]{:S(2)}, u32[]{:S(2)}) %collective-permute-start.15) | collective-permute-done | bytes 208928 | tf_op jit(solution)/shard_map/ppermute | solution.py:431
  41.6 1.4 %collective-permute-done.16.refs_13_ = bf16[272,384]{1,0:T(8,128)(2,1)S(1)} collective-permute-done((bf16[272,384]{1,0:T(8,128)(2,1)S(1)}, bf16[272,384]{1,0:T(8,128)(2,1)S(1)}, u32[]{:S(2)}, u32[]{:S(2)}) %collective-permute-start.16) | collective-permute-done | bytes 208928 | tf_op jit(solution)/shard_map/ppermute | solution.py:434
  43.0 2.0 %shard_map.79 = f32[8,256]{1,0:T(8,128)S(1)} custom-call(bf16[544,384]{1,0:T(8,128)(2,1)S(1)} %get-tuple-element.19.refs_0_, bf16[544,384]{1,0:T(8,128)(2,1)S(1)} %collective-permute-done.4.refs_1_, bf16[272,384]{1,0:T(8,128)(2,1)S(1)} %collective-permute-done.5.refs_2_, bf16[272,384]{1,0:T(8,128)(2,1)S(1)} %collective-permute-done.6.refs_3_, ...), custom_call_target="tpu_custom_call" | custom-call | tf_op jit(solution)/shard_map/pallas_call | solution.py:364
  45.0 0.6 collective-permute-start.17
  45.6 0.8 collective-permute-done.17
  46.4 2.6 %collective-permute-start.20 = (f32[16,256]{1,0:T(8,128)S(1)}, f32[16,256]{1,0:T(8,128)S(1)}, u32[]{:S(2)}, u32[]{:S(2)}) collective-permute-start(f32[16,256]{1,0:T(8,128)S(1)} %pad_maximum_fusion.refs_14_), channel_id=1, source_target_pairs={{0,192},{1,193},{2,194},{3,195},{4,196},{5,197},{6,198},{7,199},{8... | collective-permute-start | bytes 49160 | tf_op jit(solution)/shard_map/ppermute | solution.py:437
  49.1 1.1 %collective-permute-start.19 = (f32[16,256]{1,0:T(8,128)S(1)}, f32[16,256]{1,0:T(8,128)S(1)}, u32[]{:S(2)}, u32[]{:S(2)}) collective-permute-start(f32[16,256]{1,0:T(8,128)S(1)} %pad_maximum_fusion.refs_14_), channel_id=1, source_target_pairs={{0,128},{1,129},{2,130},{3,131},{4,132},{5,133},{6,134},{7,135},{8... | collective-permute-start | bytes 49160 | tf_op jit(solution)/shard_map/ppermute | solution.py:437
  50.5 3.8 %collective-permute-done.19.refs_16_ = f32[16,256]{1,0:T(8,128)S(1)} collective-permute-done((f32[16,256]{1,0:T(8,128)S(1)}, f32[16,256]{1,0:T(8,128)S(1)}, u32[]{:S(2)}, u32[]{:S(2)}) %collective-permute-start.19) | collective-permute-done | bytes 16416 | tf_op jit(solution)/shard_map/ppermute | solution.py:437
  54.3 0.8 collective-permute-done.18.refs_15_
  55.1 6.4 %shard_map.80 = (bf16[144,128]{1,0:T(8,128)(2,1)S(1)}, bf16[144,128]{1,0:T(8,128)(2,1)S(1)}, bf16[144,128]{1,0:T(8,128)(2,1)S(1)}, bf16[144,128]{1,0:T(8,128)(2,1)S(1)}) custom-call(bf16[544,384]{1,0:T(8,128)(2,1)S(1)} %get-tuple-element.19.refs_0_, bf16[544,384]{1,0:T(8,128)(2,1)S(1)} %collective-permute-done.4.refs_1_, ...), custom_call_target="tpu_custom_call" | custom-call | tf_op jit(solution)/shard_map/pallas_call | solution.py:379
  61.5 1.9 %collective-permute-start.21 = (bf16[144,128]{1,0:T(8,128)(2,1)S(1)}, bf16[144,128]{1,0:T(8,128)(2,1)S(1)}, u32[]{:S(2)}, u32[]{:S(2)}) collective-permute-start(bf16[144,128]{1,0:T(8,128)(2,1)S(1)} %get-tuple-element.21), channel_id=1, source_target_pairs={{0,0},{8,1},{2,2},{10,3},{4,4},{12,5},{6,6},{14,7},{1,8},{9,9},{3,... | collective-permute-start | bytes 110600 | tf_op jit(solution)/shard_map/ppermute | solution.py:439
  63.6 2.2 %collective-permute-start.23 = (bf16[144,128]{1,0:T(8,128)(2,1)S(1)}, bf16[144,128]{1,0:T(8,128)(2,1)S(1)}, u32[]{:S(2)}, u32[]{:S(2)}) collective-permute-start(bf16[144,128]{1,0:T(8,128)(2,1)S(1)} %get-tuple-element.23), channel_id=1, source_target_pairs={{32,0},{40,1},{34,2},{42,3},{36,4},{44,5},{38,6},{46,7},{33,8},{41... | collective-permute-start | bytes 110600 | tf_op jit(solution)/shard_map/ppermute | solution.py:439
  65.8 2.5 %collective-permute-start.24 = (bf16[144,128]{1,0:T(8,128)(2,1)S(1)}, bf16[144,128]{1,0:T(8,128)(2,1)S(1)}, u32[]{:S(2)}, u32[]{:S(2)}) collective-permute-start(bf16[144,128]{1,0:T(8,128)(2,1)S(1)} %get-tuple-element.24), channel_id=1, source_target_pairs={{48,0},{56,1},{50,2},{58,3},{52,4},{60,5},{54,6},{62,7},{49,8},{57... | collective-permute-start | bytes 110600 | tf_op jit(solution)/shard_map/ppermute | solution.py:439
  68.3 2.0 %collective-permute-done.23.g2 = bf16[144,128]{1,0:T(8,128)(2,1)S(1)} collective-permute-done((bf16[144,128]{1,0:T(8,128)(2,1)S(1)}, bf16[144,128]{1,0:T(8,128)(2,1)S(1)}, u32[]{:S(2)}, u32[]{:S(2)}) %collective-permute-start.23) | collective-permute-done | bytes 36896 | tf_op jit(solution)/shard_map/ppermute | solution.py:439
  70.4 2.4 %collective-permute-done.24.g3 = bf16[144,128]{1,0:T(8,128)(2,1)S(1)} collective-permute-done((bf16[144,128]{1,0:T(8,128)(2,1)S(1)}, bf16[144,128]{1,0:T(8,128)(2,1)S(1)}, u32[]{:S(2)}, u32[]{:S(2)}) %collective-permute-start.24) | collective-permute-done | bytes 36896 | tf_op jit(solution)/shard_map/ppermute | solution.py:439
  72.8 1.2 %collective-permute-done.25 = f32[8,128]{1,0:T(8,128)S(1)} collective-permute-done((f32[8,128]{1,0:T(8,128)S(1)}, f32[8,128]{1,0:T(8,128)S(1)}, u32[]{:S(2)}, u32[]{:S(2)}) %collective-permute-start.25) | collective-permute-done | bytes 4128 | tf_op jit(solution)/shard_map/ppermute | solution.py:443
  74.0 2.8 %collective-permute-start.28 = (f32[8,128]{1,0:T(8,128)S(1)}, f32[8,128]{1,0:T(8,128)S(1)}, u32[]{:S(2)}, u32[]{:S(2)}) collective-permute-start(f32[8,128]{1,0:T(8,128)S(1)} %add.24), channel_id=1, source_target_pairs={{0,6},{1,7},{2,4},{3,5},{4,2},{5,3},{6,0},{7,1},{8,14},{9,15},{10,... | collective-permute-start | bytes 12296 | tf_op jit(solution)/shard_map/ppermute | solution.py:444
  76.7 0.8 collective-permute-start.27
  78.1 0.7 shard_map.81
  78.8 3.1 %collective-permute-done.27 = f32[8,128]{1,0:T(8,128)S(1)} collective-permute-done((f32[8,128]{1,0:T(8,128)S(1)}, f32[8,128]{1,0:T(8,128)S(1)}, u32[]{:S(2)}, u32[]{:S(2)}) %collective-permute-start.27) | collective-permute-done | bytes 4128 | tf_op jit(solution)/shard_map/ppermute | solution.py:444
  (36 shorter events, 3.9 us)
Async XLA Ops:
  2.6 11.5 %collective-permute-start = (bf16[144,384]{1,0:T(8,128)(2,1)}, bf16[144,384]{1,0:T(8,128)(2,1)S(1)}, u32[]{:S(2)}, u32[]{:S(2)}) collective-permute-start(bf16[144,384]{1,0:T(8,128)(2,1)} %get-tuple-element.15), channel_id=1, source_target_pairs={{0,0},{1,8},{2,2},{3,10},{4,4},{5,12},{6,6},{7,14},{8,1},{9,9},{10... | collective-permute-start | bytes 331784 | tf_op jit(solution)/shard_map/ppermute | solution.py:409
  4.5 12.1 %collective-permute-start.1 = (bf16[144,384]{1,0:T(8,128)(2,1)}, bf16[144,384]{1,0:T(8,128)(2,1)S(1)}, u32[]{:S(2)}, u32[]{:S(2)}) collective-permute-start(bf16[144,384]{1,0:T(8,128)(2,1)} %get-tuple-element.16), channel_id=1, source_target_pairs={{0,16},{1,24},{2,18},{3,26},{4,20},{5,28},{6,22},{7,30},{8,17},{9,... | collective-permute-start | bytes 331784 | tf_op jit(solution)/shard_map/ppermute | solution.py:409
  8.1 11.6 %collective-permute-start.2 = (bf16[144,384]{1,0:T(8,128)(2,1)}, bf16[144,384]{1,0:T(8,128)(2,1)S(1)}, u32[]{:S(2)}, u32[]{:S(2)}) collective-permute-start(bf16[144,384]{1,0:T(8,128)(2,1)} %get-tuple-element.17), channel_id=1, source_target_pairs={{0,48},{1,56},{2,50},{3,58},{4,52},{5,60},{6,54},{7,62},{8,49},{9,... | collective-permute-start | bytes 331784 | tf_op jit(solution)/shard_map/ppermute | solution.py:409
  11.2 13.1 %collective-permute-start.3 = (bf16[144,384]{1,0:T(8,128)(2,1)}, bf16[144,384]{1,0:T(8,128)(2,1)S(1)}, u32[]{:S(2)}, u32[]{:S(2)}) collective-permute-start(bf16[144,384]{1,0:T(8,128)(2,1)} %get-tuple-element.18), channel_id=1, source_target_pairs={{0,32},{1,40},{2,34},{3,42},{4,36},{5,44},{6,38},{7,46},{8,33},{9,... | collective-permute-start | bytes 331784 | tf_op jit(solution)/shard_map/ppermute | solution.py:409
  16.6 10.9 %collective-permute-start.7 = (bf16[272,384]{1,0:T(8,128)(2,1)S(1)}, bf16[272,384]{1,0:T(8,128)(2,1)S(1)}, u32[]{:S(2)}, u32[]{:S(2)}) collective-permute-start(bf16[272,384]{1,0:T(8,128)(2,1)S(1)} %shard_map.77.before), channel_id=1, source_target_pairs={{0,192},{1,65},{2,194},{3,67},{4,196},{5,69},{6,198},{7,71},{8,200... | collective-permute-start | bytes 626696 | tf_op jit(solution)/shard_map/ppermute | solution.py:430
  19.7 8.3 %collective-permute-start.5 = (bf16[272,384]{1,0:T(8,128)(2,1)S(1)}, bf16[272,384]{1,0:T(8,128)(2,1)S(1)}, u32[]{:S(2)}, u32[]{:S(2)}) collective-permute-start(bf16[272,384]{1,0:T(8,128)(2,1)S(1)} %shard_map.77.before), channel_id=1, source_target_pairs={{0,64},{1,193},{2,66},{3,195},{4,68},{5,197},{6,70},{7,199},{8,72}... | collective-permute-start | bytes 626696 | tf_op jit(solution)/shard_map/ppermute | solution.py:429
  24.4 6.4 %collective-permute-start.13 = (bf16[272,384]{1,0:T(8,128)(2,1)S(1)}, bf16[272,384]{1,0:T(8,128)(2,1)S(1)}, u32[]{:S(2)}, u32[]{:S(2)}) collective-permute-start(bf16[272,384]{1,0:T(8,128)(2,1)S(1)} %get-tuple-element.20), channel_id=1, source_target_pairs={{0,192},{1,65},{2,194},{3,67},{4,196},{5,69},{6,198},{7,71},{8,200... | collective-permute-start | bytes 626696 | tf_op jit(solution)/shard_map/ppermute | solution.py:430
  27.5 7.0 %collective-permute-start.11 = (bf16[272,384]{1,0:T(8,128)(2,1)S(1)}, bf16[272,384]{1,0:T(8,128)(2,1)S(1)}, u32[]{:S(2)}, u32[]{:S(2)}) collective-permute-start(bf16[272,384]{1,0:T(8,128)(2,1)S(1)} %get-tuple-element.20), channel_id=1, source_target_pairs={{0,64},{1,193},{2,66},{3,195},{4,68},{5,197},{6,70},{7,199},{8,72}... | collective-permute-start | bytes 626696 | tf_op jit(solution)/shard_map/ppermute | solution.py:429
  27.5 14.0 %collective-permute-start.4 = (bf16[544,384]{1,0:T(8,128)(2,1)S(1)}, bf16[544,384]{1,0:T(8,128)(2,1)S(1)}, u32[]{:S(2)}, u32[]{:S(2)}) collective-permute-start(bf16[544,384]{1,0:T(8,128)(2,1)S(1)} %get-tuple-element.19.refs_0_), channel_id=1, source_target_pairs={{0,1},{1,0},{2,3},{3,2},{4,5},{5,4},{6,7},{7,6},{8,9},{9,8},{10,11... | collective-permute-start | bytes 1253384 | tf_op jit(solution)/shard_map/ppermute | solution.py:428
  27.5 7.0 %collective-permute-start.8 = (bf16[272,384]{1,0:T(8,128)(2,1)S(1)}, bf16[272,384]{1,0:T(8,128)(2,1)S(1)}, u32[]{:S(2)}, u32[]{:S(2)}) collective-permute-start(bf16[272,384]{1,0:T(8,128)(2,1)S(1)} %collective-permute-done.7.refs_4_), channel_id=1, source_target_pairs={{0,1},{1,0},{2,3},{3,2},{4,5},{5,4},{6,7},{7,6},{8,9},{9,8},{10,11... | collective-permute-start | bytes 626696 | tf_op jit(solution)/shard_map/ppermute | solution.py:434
  28.0 8.7 %collective-permute-start.9 = (bf16[272,384]{1,0:T(8,128)(2,1)S(1)}, bf16[272,384]{1,0:T(8,128)(2,1)S(1)}, u32[]{:S(2)}, u32[]{:S(2)}) collective-permute-start(bf16[272,384]{1,0:T(8,128)(2,1)S(1)} %collective-permute-done.5.refs_2_), channel_id=1, source_target_pairs={{0,64},{1,193},{2,66},{3,195},{4,68},{5,197},{6,70},{7,199},{8,72}... | collective-permute-start | bytes 626696 | tf_op jit(solution)/shard_map/ppermute | solution.py:431
  30.8 5.9 %collective-permute-start.6 = (bf16[272,384]{1,0:T(8,128)(2,1)S(1)}, bf16[272,384]{1,0:T(8,128)(2,1)S(1)}, u32[]{:S(2)}, u32[]{:S(2)}) collective-permute-start(bf16[272,384]{1,0:T(8,128)(2,1)S(1)} %collective-permute-done.5.refs_2_), channel_id=1, source_target_pairs={{0,1},{1,0},{2,3},{3,2},{4,5},{5,4},{6,7},{7,6},{8,9},{9,8},{10,11... | collective-permute-start | bytes 626696 | tf_op jit(solution)/shard_map/ppermute | solution.py:434
  34.5 7.0 %collective-permute-start.15 = (bf16[272,384]{1,0:T(8,128)(2,1)S(1)}, bf16[272,384]{1,0:T(8,128)(2,1)S(1)}, u32[]{:S(2)}, u32[]{:S(2)}) collective-permute-start(bf16[272,384]{1,0:T(8,128)(2,1)S(1)} %collective-permute-done.11.refs_8_), channel_id=1, source_target_pairs={{0,64},{1,193},{2,66},{3,195},{4,68},{5,197},{6,70},{7,199},{8,72}... | collective-permute-start | bytes 626696 | tf_op jit(solution)/shard_map/ppermute | solution.py:431
  34.5 7.0 %collective-permute-start.12 = (bf16[272,384]{1,0:T(8,128)(2,1)S(1)}, bf16[272,384]{1,0:T(8,128)(2,1)S(1)}, u32[]{:S(2)}, u32[]{:S(2)}) collective-permute-start(bf16[272,384]{1,0:T(8,128)(2,1)S(1)} %collective-permute-done.11.refs_8_), channel_id=1, source_target_pairs={{0,1},{1,0},{2,3},{3,2},{4,5},{5,4},{6,7},{7,6},{8,9},{9,8},{10,11... | collective-permute-start | bytes 626696 | tf_op jit(solution)/shard_map/ppermute | solution.py:434
  36.8 4.8 %collective-permute-start.14 = (bf16[272,384]{1,0:T(8,128)(2,1)S(1)}, bf16[272,384]{1,0:T(8,128)(2,1)S(1)}, u32[]{:S(2)}, u32[]{:S(2)}) collective-permute-start(bf16[272,384]{1,0:T(8,128)(2,1)S(1)} %collective-permute-done.13.refs_10_), channel_id=1, source_target_pairs={{0,1},{1,0},{2,3},{3,2},{4,5},{5,4},{6,7},{7,6},{8,9},{9,8},{10,11... | collective-permute-start | bytes 626696 | tf_op jit(solution)/shard_map/ppermute | solution.py:434
  36.8 4.8 %collective-permute-start.10 = (bf16[272,384]{1,0:T(8,128)(2,1)S(1)}, bf16[272,384]{1,0:T(8,128)(2,1)S(1)}, u32[]{:S(2)}, u32[]{:S(2)}) collective-permute-start(bf16[272,384]{1,0:T(8,128)(2,1)S(1)} %collective-permute-done.9.refs_6_), channel_id=1, source_target_pairs={{0,1},{1,0},{2,3},{3,2},{4,5},{5,4},{6,7},{7,6},{8,9},{9,8},{10,11... | collective-permute-start | bytes 626696 | tf_op jit(solution)/shard_map/ppermute | solution.py:434
  41.5 1.5 %collective-permute-start.16 = (bf16[272,384]{1,0:T(8,128)(2,1)S(1)}, bf16[272,384]{1,0:T(8,128)(2,1)S(1)}, u32[]{:S(2)}, u32[]{:S(2)}) collective-permute-start(bf16[272,384]{1,0:T(8,128)(2,1)S(1)} %collective-permute-done.15.refs_12_), channel_id=1, source_target_pairs={{0,1},{1,0},{2,3},{3,2},{4,5},{5,4},{6,7},{7,6},{8,9},{9,8},{10,11... | collective-permute-start | bytes 626696 | tf_op jit(solution)/shard_map/ppermute | solution.py:434
  45.0 1.4 %collective-permute-start.17 = (f32[8,256]{1,0:T(8,128)S(1)}, f32[8,256]{1,0:T(8,128)S(1)}, u32[]{:S(2)}, u32[]{:S(2)}) collective-permute-start(f32[8,256]{1,0:T(8,128)S(1)} %shard_map.79), channel_id=1, source_target_pairs={{0,1},{1,0},{2,3},{3,2},{4,5},{5,4},{6,7},{7,6},{8,9},{9,8},{10,11... | collective-permute-start | bytes 24584 | tf_op jit(solution)/shard_map/ppermute | solution.py:436
  46.4 4.1 %collective-permute-start.20 = (f32[16,256]{1,0:T(8,128)S(1)}, f32[16,256]{1,0:T(8,128)S(1)}, u32[]{:S(2)}, u32[]{:S(2)}) collective-permute-start(f32[16,256]{1,0:T(8,128)S(1)} %pad_maximum_fusion.refs_14_), channel_id=1, source_target_pairs={{0,192},{1,193},{2,194},{3,195},{4,196},{5,197},{6,198},{7,199},{8... | collective-permute-start | bytes 49160 | tf_op jit(solution)/shard_map/ppermute | solution.py:437
  49.1 5.2 %collective-permute-start.19 = (f32[16,256]{1,0:T(8,128)S(1)}, f32[16,256]{1,0:T(8,128)S(1)}, u32[]{:S(2)}, u32[]{:S(2)}) collective-permute-start(f32[16,256]{1,0:T(8,128)S(1)} %pad_maximum_fusion.refs_14_), channel_id=1, source_target_pairs={{0,128},{1,129},{2,130},{3,131},{4,132},{5,133},{6,134},{7,135},{8... | collective-permute-start | bytes 49160 | tf_op jit(solution)/shard_map/ppermute | solution.py:437
  50.2 4.9 %collective-permute-start.18 = (f32[16,256]{1,0:T(8,128)S(1)}, f32[16,256]{1,0:T(8,128)S(1)}, u32[]{:S(2)}, u32[]{:S(2)}) collective-permute-start(f32[16,256]{1,0:T(8,128)S(1)} %pad_maximum_fusion.refs_14_), channel_id=1, source_target_pairs={{0,64},{1,65},{2,66},{3,67},{4,68},{5,69},{6,70},{7,71},{8,72},{9,... | collective-permute-start | bytes 49160 | tf_op jit(solution)/shard_map/ppermute | solution.py:437
  61.5 6.8 %collective-permute-start.21 = (bf16[144,128]{1,0:T(8,128)(2,1)S(1)}, bf16[144,128]{1,0:T(8,128)(2,1)S(1)}, u32[]{:S(2)}, u32[]{:S(2)}) collective-permute-start(bf16[144,128]{1,0:T(8,128)(2,1)S(1)} %get-tuple-element.21), channel_id=1, source_target_pairs={{0,0},{8,1},{2,2},{10,3},{4,4},{12,5},{6,6},{14,7},{1,8},{9,9},{3,... | collective-permute-start | bytes 110600 | tf_op jit(solution)/shard_map/ppermute | solution.py:439
  63.5 4.9 %collective-permute-start.22 = (bf16[144,128]{1,0:T(8,128)(2,1)S(1)}, bf16[144,128]{1,0:T(8,128)(2,1)S(1)}, u32[]{:S(2)}, u32[]{:S(2)}) collective-permute-start(bf16[144,128]{1,0:T(8,128)(2,1)S(1)} %get-tuple-element.22), channel_id=1, source_target_pairs={{16,0},{24,1},{18,2},{26,3},{20,4},{28,5},{22,6},{30,7},{17,8},{25... | collective-permute-start | bytes 110600 | tf_op jit(solution)/shard_map/ppermute | solution.py:439
  63.6 6.8 %collective-permute-start.23 = (bf16[144,128]{1,0:T(8,128)(2,1)S(1)}, bf16[144,128]{1,0:T(8,128)(2,1)S(1)}, u32[]{:S(2)}, u32[]{:S(2)}) collective-permute-start(bf16[144,128]{1,0:T(8,128)(2,1)S(1)} %get-tuple-element.23), channel_id=1, source_target_pairs={{32,0},{40,1},{34,2},{42,3},{36,4},{44,5},{38,6},{46,7},{33,8},{41... | collective-permute-start | bytes 110600 | tf_op jit(solution)/shard_map/ppermute | solution.py:439
  65.8 7.0 %collective-permute-start.24 = (bf16[144,128]{1,0:T(8,128)(2,1)S(1)}, bf16[144,128]{1,0:T(8,128)(2,1)S(1)}, u32[]{:S(2)}, u32[]{:S(2)}) collective-permute-start(bf16[144,128]{1,0:T(8,128)(2,1)S(1)} %get-tuple-element.24), channel_id=1, source_target_pairs={{48,0},{56,1},{50,2},{58,3},{52,4},{60,5},{54,6},{62,7},{49,8},{57... | collective-permute-start | bytes 110600 | tf_op jit(solution)/shard_map/ppermute | solution.py:439
  72.8 1.2 %collective-permute-start.25 = (f32[8,128]{1,0:T(8,128)S(1)}, f32[8,128]{1,0:T(8,128)S(1)}, u32[]{:S(2)}, u32[]{:S(2)}) collective-permute-start(f32[8,128]{1,0:T(8,128)S(1)} %bitcast_reduce_fusion), channel_id=1, source_target_pairs={{0,1},{1,0},{2,3},{3,2},{4,5},{5,4},{6,7},{7,6},{8,9},{9,8},{10,11... | collective-permute-start | bytes 12296 | tf_op jit(solution)/shard_map/ppermute | solution.py:443
  74.0 4.8 %collective-permute-start.28 = (f32[8,128]{1,0:T(8,128)S(1)}, f32[8,128]{1,0:T(8,128)S(1)}, u32[]{:S(2)}, u32[]{:S(2)}) collective-permute-start(f32[8,128]{1,0:T(8,128)S(1)} %add.24), channel_id=1, source_target_pairs={{0,6},{1,7},{2,4},{3,5},{4,2},{5,3},{6,0},{7,1},{8,14},{9,15},{10,... | collective-permute-start | bytes 12296 | tf_op jit(solution)/shard_map/ppermute | solution.py:444
  76.7 5.1 %collective-permute-start.27 = (f32[8,128]{1,0:T(8,128)S(1)}, f32[8,128]{1,0:T(8,128)S(1)}, u32[]{:S(2)}, u32[]{:S(2)}) collective-permute-start(f32[8,128]{1,0:T(8,128)S(1)} %add.24), channel_id=1, source_target_pairs={{0,4},{1,5},{2,6},{3,7},{4,0},{5,1},{6,2},{7,3},{8,12},{9,13},{10,... | collective-permute-start | bytes 12296 | tf_op jit(solution)/shard_map/ppermute | solution.py:444
  77.5 4.3 %collective-permute-start.26 = (f32[8,128]{1,0:T(8,128)S(1)}, f32[8,128]{1,0:T(8,128)S(1)}, u32[]{:S(2)}, u32[]{:S(2)}) collective-permute-start(f32[8,128]{1,0:T(8,128)S(1)} %add.24), channel_id=1, source_target_pairs={{0,2},{1,3},{2,0},{3,1},{4,6},{5,7},{6,4},{7,5},{8,10},{9,11},{10,... | collective-permute-start | bytes 12296 | tf_op jit(solution)/shard_map/ppermute | solution.py:444

commit v2 on v1

--- a/solution.py
+++ b/solution.py
@@ -60,8 +60,8 @@
     return pairs_of(lambda y, z, x, c: ((y + sign * (1 - 2 * c)) % NY, z, x, c))
 
 
-def y_pairs(step):
-    return pairs_of(lambda y, z, x, c: ((y + step) % NY, z, x, c))
+def mirror_pairs(bits):
+    return pairs_of(lambda y, z, x, c: (y ^ bits, z, x, c))
 
 
 def x_pairs(bit):
@@ -120,14 +120,37 @@
     both[PIECE:2 * PIECE, :] = out[...]
 
 
+def group_kernel(*refs):
+    out = refs[-1]
+    for n, ref in enumerate(refs[:-1]):
+        out[n * PIECE:(n + 1) * PIECE, :] = ref[...]
+
+
+def group(parts):
+    return pl.pallas_call(
+        group_kernel,
+        out_shape=jax.ShapeDtypeStruct((len(parts) * PIECE, WIDE), BF16),
+        in_specs=[ALL] * len(parts),
+        out_specs=ALL,
+        compiler_params=params(),
+    )(*parts)
+
+
 def pieces_of(parts):
     found = []
     for other in range(2):
-        for chunk in range(2):
-            found.append((parts[other], chunk * PIECE, 0, other, chunk))
-    for n, part in enumerate(parts[2:]):
-        chunk, step, other = n // 6, (1, -1, 2)[n % 6 // 2], n % 2
-        found.append((part, 0, step, other, chunk))
+        own, near_a, far_a, over_a, late, over_b = parts[6 * other:6 * other + 6]
+        for part, base, step, chunk in (
+            (own, 0, 0, 0),
+            (own, 1, 0, 1),
+            (near_a, 0, 1, 0),
+            (far_a, 0, -1, 0),
+            (over_a, 0, 2, 0),
+            (late, 0, 1, 1),
+            (late, 1, -1, 1),
+            (over_b, 0, 2, 1),
+        ):
+            found.append((part, base * PIECE, step, other, chunk))
     return found
 
 
@@ -163,8 +186,8 @@
 
 
 def norm_kernel(*refs):
-    parts, out = refs[:14], refs[14]
-    rows, scores_t, scores_s = refs[15:]
+    parts, out = refs[:12], refs[12]
+    rows, scores_t, scores_s = refs[13:]
     bounds = assemble(parts, rows)
     y, z, core = placed()
     r = y * 2 + core
@@ -248,8 +271,8 @@
 
 
 def grad_kernel(*refs):
-    parts, packets, outs = refs[:14], refs[14:18], refs[18:22]
-    rows, norms, row_norm, acc, mine = refs[22:]
+    parts, packets, outs = refs[:12], refs[12:16], refs[16:20]
+    rows, norms, row_norm, acc, mine = refs[20:]
     bounds = assemble(parts, rows)
     y, z, core = placed()
     m = z // 2
@@ -257,7 +280,7 @@
     for i, packet in enumerate(packets):
         for other in range(2):
             from_core = core if other == 0 else 1 - core
-            from_r = ((y - i + NY) % NY) * 2 + from_core
+            from_r = (y ^ i) * 2 + from_core
             norms[from_r, 0:2, :] = packet[8 * other:8 * other + 2, :]
             norms[TILES - 1 - from_r, 0:2, :] = packet[8 * other + 2:8 * other + 4, :]
             kl = kl + packet[8 * other + 4:8 * other + 5, :] + packet[8 * other + 5:8 * other + 6, :]
@@ -364,7 +387,7 @@
     return pl.pallas_call(
         norm_kernel,
         out_shape=jax.ShapeDtypeStruct((8, TILE), F32),
-        in_specs=[ALL] * 14,
+        in_specs=[ALL] * 12,
         out_specs=ALL,
         scratch_shapes=[
             pltpu.VMEM((TOKENS, WIDE), BF16),
@@ -379,7 +402,7 @@
     return pl.pallas_call(
         grad_kernel,
         out_shape=[jax.ShapeDtypeStruct((ROWS + 16, HDIM), BF16)] * 4,
-        in_specs=[ALL] * 18,
+        in_specs=[ALL] * 16,
         out_specs=[ALL] * 4,
         scratch_shapes=[
             pltpu.VMEM((TOKENS, WIDE), BF16),
@@ -425,16 +448,15 @@
         out_specs=[ALL] * 2,
         compiler_params=params(),
     )(own_a, *gots[2:4])
-    parts = [own, lax.ppermute(own, AXES, CORE_PAIRS)]
-    nears = [lax.ppermute(mine, AXES, near_pairs(1)) for mine in (own_a, own_b)]
-    fars = [lax.ppermute(mine, AXES, near_pairs(-1)) for mine in (own_a, own_b)]
-    opposites = [lax.ppermute(near, AXES, near_pairs(1)) for near in nears]
-    for trio in zip(nears, fars, opposites):
-        for part in trio:
-            parts += [part, lax.ppermute(part, AXES, CORE_PAIRS)]
+    near_a, near_b = (lax.ppermute(mine, AXES, near_pairs(1)) for mine in (own_a, own_b))
+    far_a, far_b = (lax.ppermute(mine, AXES, near_pairs(-1)) for mine in (own_a, own_b))
+    over_a, over_b = (lax.ppermute(near, AXES, near_pairs(1)) for near in (near_a, near_b))
+    parts = [own, near_a, far_a, over_a, group([near_b, far_b]), over_b]
+    parts += [lax.ppermute(part, AXES, CORE_PAIRS) for part in parts]
     packet = call_norm(parts)
     both = jnp.concatenate([packet, lax.ppermute(packet, AXES, CORE_PAIRS)])
-    packets = [both] + [lax.ppermute(both, AXES, y_pairs(step)) for step in (1, 2, 3)]
+    others = {step: lax.ppermute(both, AXES, mirror_pairs(step)) for step in (2, 1, 3)}
+    packets = [both] + [others[step] for step in (1, 2, 3)]
     grads = call_grad(parts, packets)
     backs = {j: lax.ppermute(grads[j], AXES, collect_pairs(j)) for j in (2, 3, 1, 0)}
     backs = [backs[j] for j in range(4)]

time: 84.5 us -> 82.7 us (0.979)
  waiting for transfers between devices: 35 us -> 30.6 us
  starting transfers between devices: 35 us -> 37.4 us
    ppermute x16 -> x15, waiting for transfers between devices: 18.3 us -> 14 us  [the longest x2 6.36 us: per_device(): lax.ppermute(near, AXES, near_pairs(1))]
    ppermute x1, starting transfers between devices: 0.61 us -> 3 us  [per_device(): both = jnp.concatenate([packet, lax.ppermute(packet, AXES, CORE_PAIRS)])]
    ppermute x16 -> x15, starting transfers between devices: 12 us -> 12 us  [the longest x2 4.75 us: per_device(): lax.ppermute(mine, AXES, near_pairs(-1))]
  transfers between devices with their start and end apart: 29 -> 28, of which waited for: 15 -> 14; matrix products, arithmetic and copies ran while one was open for 0% -> 0% of each run, Pallas kernels for 1% -> 1%
where the time goes in v2:
time: 82.7 us; the launch traced here: 82.8 us
  starting transfers between devices  37.4 us (45%)
  waiting for transfers between devices  30.6 us (37%)
  Pallas kernels  11.6 us (14%)
  between operations  2.51 us (3%)
    ppermute x4, starting transfers between devices, per_device(): gots = [lax.ppermute(sends[j], AXES, spread_pairs(j)) for j in ORDER]  11.5 us
    ppermute x4, waiting for transfers between devices, per_device(): gots = [lax.ppermute(sends[j], AXES, spread_pairs(j)) for j in ORDER]  7.15 us
    pallas_call x1, Pallas kernels, call_grad(): pl.pallas_call(grad_kernel, out_shape=[jax.ShapeDtypeStruct((ROWS + 16, H...  6.92 us
    ppermute x4, starting transfers between devices, per_device(): lax.ppermute(grads[j], AXES, collect_pairs(j))  6.82 us
    ppermute x2, waiting for transfers between devices, per_device(): lax.ppermute(near, AXES, near_pairs(1))  6.36 us
    ppermute x2, starting transfers between devices, per_device(): lax.ppermute(mine, AXES, near_pairs(-1))  4.75 us
    ppermute x4, waiting for transfers between devices, per_device(): lax.ppermute(grads[j], AXES, collect_pairs(j))  4.39 us
    ppermute x2, waiting for transfers between devices, per_device(): lax.ppermute(mine, AXES, near_pairs(1))  4.29 us
  transfers between devices with their start and end apart: 28, of which 14 were waited for; matrix products, arithmetic and copies ran while one was open for 0% of the time, Pallas kernels for 1%

profile of v2, /device:TPU:32, one launch (start us, length us, event | category | flops | bytes accessed | tf_op | source)
XLA Modules:
  0.0 82.8 jit_solution(18076342527095375250)
XLA Ops:
  0.6 1.9 %shard_map.76 = (bf16[144,384]{1,0:T(8,128)(2,1)}, bf16[144,384]{1,0:T(8,128)(2,1)}, bf16[144,384]{1,0:T(8,128)(2,1)}, bf16[144,384]{1,0:T(8,128)(2,1)}) custom-call(bf16[128,512]{1,0:T(8,128)(2,1)} %tq.1, bf16[128,512]{1,0:T(8,128)(2,1)} %tk.1, bf16[128,256]{1,0:T(8,128)(2,1)} %sq.1, bf16[128,256]{1,0:T(8,128)(2,1)} %sk.1, s32[1,128]{1,0:T(1,128)} %bitcast.3), custom_call_target="tpu_custom_call" | custom-call | tf_op jit(solution)/shard_map/pallas_call | solution.py:420
  2.6 1.9 %collective-permute-start = (bf16[144,384]{1,0:T(8,128)(2,1)}, bf16[144,384]{1,0:T(8,128)(2,1)S(1)}, u32[]{:S(2)}, u32[]{:S(2)}) collective-permute-start(bf16[144,384]{1,0:T(8,128)(2,1)} %get-tuple-element.15), channel_id=1, source_target_pairs={{0,0},{1,8},{2,2},{3,10},{4,4},{5,12},{6,6},{7,14},{8,1},{9,9},{10... | collective-permute-start | bytes 331784 | tf_op jit(solution)/shard_map/ppermute | solution.py:432
  4.5 3.6 %collective-permute-start.1 = (bf16[144,384]{1,0:T(8,128)(2,1)}, bf16[144,384]{1,0:T(8,128)(2,1)S(1)}, u32[]{:S(2)}, u32[]{:S(2)}) collective-permute-start(bf16[144,384]{1,0:T(8,128)(2,1)} %get-tuple-element.16), channel_id=1, source_target_pairs={{0,16},{1,24},{2,18},{3,26},{4,20},{5,28},{6,22},{7,30},{8,17},{9,... | collective-permute-start | bytes 331784 | tf_op jit(solution)/shard_map/ppermute | solution.py:432
  8.1 3.1 %collective-permute-start.2 = (bf16[144,384]{1,0:T(8,128)(2,1)}, bf16[144,384]{1,0:T(8,128)(2,1)S(1)}, u32[]{:S(2)}, u32[]{:S(2)}) collective-permute-start(bf16[144,384]{1,0:T(8,128)(2,1)} %get-tuple-element.17), channel_id=1, source_target_pairs={{0,48},{1,56},{2,50},{3,58},{4,52},{5,60},{6,54},{7,62},{8,49},{9,... | collective-permute-start | bytes 331784 | tf_op jit(solution)/shard_map/ppermute | solution.py:432
  11.2 2.9 %collective-permute-start.3 = (bf16[144,384]{1,0:T(8,128)(2,1)}, bf16[144,384]{1,0:T(8,128)(2,1)S(1)}, u32[]{:S(2)}, u32[]{:S(2)}) collective-permute-start(bf16[144,384]{1,0:T(8,128)(2,1)} %get-tuple-element.18), channel_id=1, source_target_pairs={{0,32},{1,40},{2,34},{3,42},{4,36},{5,44},{6,38},{7,46},{8,33},{9,... | collective-permute-start | bytes 331784 | tf_op jit(solution)/shard_map/ppermute | solution.py:432
  14.1 2.5 %collective-permute-done.1.second = bf16[144,384]{1,0:T(8,128)(2,1)S(1)} collective-permute-done((bf16[144,384]{1,0:T(8,128)(2,1)}, bf16[144,384]{1,0:T(8,128)(2,1)S(1)}, u32[]{:S(2)}, u32[]{:S(2)}) %collective-permute-start.1) | collective-permute-done | bytes 110624 | tf_op jit(solution)/shard_map/ppermute | solution.py:432
  16.6 3.1 %collective-permute-start.5 = (bf16[272,384]{1,0:T(8,128)(2,1)S(1)}, bf16[272,384]{1,0:T(8,128)(2,1)S(1)}, u32[]{:S(2)}, u32[]{:S(2)}) collective-permute-start(bf16[272,384]{1,0:T(8,128)(2,1)S(1)} %shard_map.77.before), channel_id=1, source_target_pairs={{0,192},{1,65},{2,194},{3,67},{4,196},{5,69},{6,198},{7,71},{8,200... | collective-permute-start | bytes 626696 | tf_op jit(solution)/shard_map/ppermute | solution.py:452
  19.7 4.6 %collective-permute-done.3.second = bf16[144,384]{1,0:T(8,128)(2,1)S(1)} collective-permute-done((bf16[144,384]{1,0:T(8,128)(2,1)}, bf16[144,384]{1,0:T(8,128)(2,1)S(1)}, u32[]{:S(2)}, u32[]{:S(2)}) %collective-permute-start.3) | collective-permute-done | bytes 110624 | tf_op jit(solution)/shard_map/ppermute | solution.py:432
  24.4 1.7 %collective-permute-start.7 = (bf16[272,384]{1,0:T(8,128)(2,1)S(1)}, bf16[272,384]{1,0:T(8,128)(2,1)S(1)}, u32[]{:S(2)}, u32[]{:S(2)}) collective-permute-start(bf16[272,384]{1,0:T(8,128)(2,1)S(1)} %get-tuple-element.20), channel_id=1, source_target_pairs={{0,64},{1,193},{2,66},{3,195},{4,68},{5,197},{6,70},{7,199},{8,72}... | collective-permute-start | bytes 626696 | tf_op jit(solution)/shard_map/ppermute | solution.py:451
  26.1 1.7 %collective-permute-start.8 = (bf16[272,384]{1,0:T(8,128)(2,1)S(1)}, bf16[272,384]{1,0:T(8,128)(2,1)S(1)}, u32[]{:S(2)}, u32[]{:S(2)}) collective-permute-start(bf16[272,384]{1,0:T(8,128)(2,1)S(1)} %get-tuple-element.20), channel_id=1, source_target_pairs={{0,192},{1,65},{2,194},{3,67},{4,196},{5,69},{6,198},{7,71},{8,200... | collective-permute-start | bytes 626696 | tf_op jit(solution)/shard_map/ppermute | solution.py:452
  28.6 4.3 %collective-permute-done.7.refs_0_ = bf16[272,384]{1,0:T(8,128)(2,1)S(1)} collective-permute-done((bf16[272,384]{1,0:T(8,128)(2,1)S(1)}, bf16[272,384]{1,0:T(8,128)(2,1)S(1)}, u32[]{:S(2)}, u32[]{:S(2)}) %collective-permute-start.7) | collective-permute-done | bytes 208928 | tf_op jit(solution)/shard_map/ppermute | solution.py:451
  33.6 1.7 %collective-permute-done.6.refs_3_ = bf16[272,384]{1,0:T(8,128)(2,1)S(1)} collective-permute-done((bf16[272,384]{1,0:T(8,128)(2,1)S(1)}, bf16[272,384]{1,0:T(8,128)(2,1)S(1)}, u32[]{:S(2)}, u32[]{:S(2)}) %collective-permute-start.6) | collective-permute-done | bytes 208928 | tf_op jit(solution)/shard_map/ppermute | solution.py:453
  35.3 4.6 %collective-permute-done.9.refs_5_ = bf16[272,384]{1,0:T(8,128)(2,1)S(1)} collective-permute-done((bf16[272,384]{1,0:T(8,128)(2,1)S(1)}, bf16[272,384]{1,0:T(8,128)(2,1)S(1)}, u32[]{:S(2)}, u32[]{:S(2)}) %collective-permute-start.9) | collective-permute-done | bytes 208928 | tf_op jit(solution)/shard_map/ppermute | solution.py:453
  39.9 1.4 %collective-permute-done.15.refs_11_ = bf16[272,384]{1,0:T(8,128)(2,1)S(1)} collective-permute-done((bf16[272,384]{1,0:T(8,128)(2,1)S(1)}, bf16[272,384]{1,0:T(8,128)(2,1)S(1)}, u32[]{:S(2)}, u32[]{:S(2)}) %collective-permute-start.15) | collective-permute-done | bytes 208928 | tf_op jit(solution)/shard_map/ppermute | solution.py:455
  41.4 2.0 %shard_map.80 = f32[8,256]{1,0:T(8,128)S(1)} custom-call(bf16[544,384]{1,0:T(8,128)(2,1)S(1)} %get-tuple-element.19.refs_0_, bf16[272,384]{1,0:T(8,128)(2,1)S(1)} %collective-permute-done.4.refs_1_, bf16[272,384]{1,0:T(8,128)(2,1)S(1)} %collective-permute-done.5.refs_2_, bf16[272,384]{1,0:T(8,128)(2,1)S(1)} %collective-permute-done.6.refs_3_, ...), custom_call_target="tpu_custom_call" | custom-call | tf_op jit(solution)/shard_map/pallas_call | solution.py:387
  43.4 3.0 %collective-permute-start.16 = (f32[8,256]{1,0:T(8,128)S(1)}, f32[8,256]{1,0:T(8,128)S(1)}, u32[]{:S(2)}, u32[]{:S(2)}) collective-permute-start(f32[8,256]{1,0:T(8,128)S(1)} %shard_map.80), channel_id=1, source_target_pairs={{0,1},{1,0},{2,3},{3,2},{4,5},{5,4},{6,7},{7,6},{8,9},{9,8},{10,11... | collective-permute-start | bytes 24584 | tf_op jit(solution)/shard_map/ppermute | solution.py:457
  46.4 0.8 %collective-permute-done.16 = f32[8,256]{1,0:T(8,128)S(1)} collective-permute-done((f32[8,256]{1,0:T(8,128)S(1)}, f32[8,256]{1,0:T(8,128)S(1)}, u32[]{:S(2)}, u32[]{:S(2)}) %collective-permute-start.16) | collective-permute-done | bytes 8224 | tf_op jit(solution)/shard_map/ppermute | solution.py:457
  47.2 0.9 %collective-permute-start.18 = (f32[16,256]{1,0:T(8,128)S(1)}, f32[16,256]{1,0:T(8,128)S(1)}, u32[]{:S(2)}, u32[]{:S(2)}) collective-permute-start(f32[16,256]{1,0:T(8,128)S(1)} %pad_maximum_fusion.refs_12_), channel_id=1, source_target_pairs={{0,128},{1,129},{2,130},{3,131},{4,132},{5,133},{6,134},{7,135},{8... | collective-permute-start | bytes 49160 | tf_op jit(solution)/shard_map/ppermute | solution.py:458
  48.0 3.2 %collective-permute-start.17 = (f32[16,256]{1,0:T(8,128)S(1)}, f32[16,256]{1,0:T(8,128)S(1)}, u32[]{:S(2)}, u32[]{:S(2)}) collective-permute-start(f32[16,256]{1,0:T(8,128)S(1)} %pad_maximum_fusion.refs_12_), channel_id=1, source_target_pairs={{0,64},{1,65},{2,66},{3,67},{4,68},{5,69},{6,70},{7,71},{8,72},{9,... | collective-permute-start | bytes 49160 | tf_op jit(solution)/shard_map/ppermute | solution.py:458
  51.3 0.9 %collective-permute-done.19.refs_15_ = f32[16,256]{1,0:T(8,128)S(1)} collective-permute-done((f32[16,256]{1,0:T(8,128)S(1)}, f32[16,256]{1,0:T(8,128)S(1)}, u32[]{:S(2)}, u32[]{:S(2)}) %collective-permute-start.19) | collective-permute-done | bytes 16416 | tf_op jit(solution)/shard_map/ppermute | solution.py:458
  52.4 0.7 collective-permute-done.17.refs_13_
  53.2 6.9 %shard_map.81 = (bf16[144,128]{1,0:T(8,128)(2,1)S(1)}, bf16[144,128]{1,0:T(8,128)(2,1)S(1)}, bf16[144,128]{1,0:T(8,128)(2,1)S(1)}, bf16[144,128]{1,0:T(8,128)(2,1)S(1)}) custom-call(bf16[544,384]{1,0:T(8,128)(2,1)S(1)} %get-tuple-element.19.refs_0_, bf16[272,384]{1,0:T(8,128)(2,1)S(1)} %collective-permute-done.4.refs_1_, ...), custom_call_target="tpu_custom_call" | custom-call | tf_op jit(solution)/shard_map/pallas_call | solution.py:402
  60.1 2.1 %collective-permute-start.20 = (bf16[144,128]{1,0:T(8,128)(2,1)S(1)}, bf16[144,128]{1,0:T(8,128)(2,1)S(1)}, u32[]{:S(2)}, u32[]{:S(2)}) collective-permute-start(bf16[144,128]{1,0:T(8,128)(2,1)S(1)} %get-tuple-element.21), channel_id=1, source_target_pairs={{0,0},{8,1},{2,2},{10,3},{4,4},{12,5},{6,6},{14,7},{1,8},{9,9},{3,... | collective-permute-start | bytes 110600 | tf_op jit(solution)/shard_map/ppermute | solution.py:461
  62.2 1.0 %collective-permute-start.21 = (bf16[144,128]{1,0:T(8,128)(2,1)S(1)}, bf16[144,128]{1,0:T(8,128)(2,1)S(1)}, u32[]{:S(2)}, u32[]{:S(2)}) collective-permute-start(bf16[144,128]{1,0:T(8,128)(2,1)S(1)} %get-tuple-element.22), channel_id=1, source_target_pairs={{16,0},{24,1},{18,2},{26,3},{20,4},{28,5},{22,6},{30,7},{17,8},{25... | collective-permute-start | bytes 110600 | tf_op jit(solution)/shard_map/ppermute | solution.py:461
  63.2 1.2 %collective-permute-start.22 = (bf16[144,128]{1,0:T(8,128)(2,1)S(1)}, bf16[144,128]{1,0:T(8,128)(2,1)S(1)}, u32[]{:S(2)}, u32[]{:S(2)}) collective-permute-start(bf16[144,128]{1,0:T(8,128)(2,1)S(1)} %get-tuple-element.23), channel_id=1, source_target_pairs={{32,0},{40,1},{34,2},{42,3},{36,4},{44,5},{38,6},{46,7},{33,8},{41... | collective-permute-start | bytes 110600 | tf_op jit(solution)/shard_map/ppermute | solution.py:461
  64.4 2.5 %collective-permute-start.23 = (bf16[144,128]{1,0:T(8,128)(2,1)S(1)}, bf16[144,128]{1,0:T(8,128)(2,1)S(1)}, u32[]{:S(2)}, u32[]{:S(2)}) collective-permute-start(bf16[144,128]{1,0:T(8,128)(2,1)S(1)} %get-tuple-element.24), channel_id=1, source_target_pairs={{48,0},{56,1},{50,2},{58,3},{52,4},{60,5},{54,6},{62,7},{49,8},{57... | collective-permute-start | bytes 110600 | tf_op jit(solution)/shard_map/ppermute | solution.py:461
  66.9 2.9 %collective-permute-done.22.g2 = bf16[144,128]{1,0:T(8,128)(2,1)S(1)} collective-permute-done((bf16[144,128]{1,0:T(8,128)(2,1)S(1)}, bf16[144,128]{1,0:T(8,128)(2,1)S(1)}, u32[]{:S(2)}, u32[]{:S(2)}) %collective-permute-start.22) | collective-permute-done | bytes 36896 | tf_op jit(solution)/shard_map/ppermute | solution.py:461
  69.9 1.5 %collective-permute-done.23.g3 = bf16[144,128]{1,0:T(8,128)(2,1)S(1)} collective-permute-done((bf16[144,128]{1,0:T(8,128)(2,1)S(1)}, bf16[144,128]{1,0:T(8,128)(2,1)S(1)}, u32[]{:S(2)}, u32[]{:S(2)}) %collective-permute-start.23) | collective-permute-done | bytes 36896 | tf_op jit(solution)/shard_map/ppermute | solution.py:461
  71.3 1.2 %collective-permute-done.24 = f32[8,128]{1,0:T(8,128)S(1)} collective-permute-done((f32[8,128]{1,0:T(8,128)S(1)}, f32[8,128]{1,0:T(8,128)S(1)}, u32[]{:S(2)}, u32[]{:S(2)}) %collective-permute-start.24) | collective-permute-done | bytes 4128 | tf_op jit(solution)/shard_map/ppermute | solution.py:465
  72.5 2.8 %collective-permute-start.27 = (f32[8,128]{1,0:T(8,128)S(1)}, f32[8,128]{1,0:T(8,128)S(1)}, u32[]{:S(2)}, u32[]{:S(2)}) collective-permute-start(f32[8,128]{1,0:T(8,128)S(1)} %add.24), channel_id=1, source_target_pairs={{0,6},{1,7},{2,4},{3,5},{4,2},{5,3},{6,0},{7,1},{8,14},{9,15},{10,... | collective-permute-start | bytes 12296 | tf_op jit(solution)/shard_map/ppermute | solution.py:466
  75.3 0.8 collective-permute-start.26
  77.3 3.0 %collective-permute-done.26 = f32[8,128]{1,0:T(8,128)S(1)} collective-permute-done((f32[8,128]{1,0:T(8,128)S(1)}, f32[8,128]{1,0:T(8,128)S(1)}, u32[]{:S(2)}, u32[]{:S(2)}) %collective-permute-start.26) | collective-permute-done | bytes 4128 | tf_op jit(solution)/shard_map/ppermute | solution.py:466
  (35 shorter events, 3.8 us)
Async XLA Ops:
  2.6 11.5 %collective-permute-start = (bf16[144,384]{1,0:T(8,128)(2,1)}, bf16[144,384]{1,0:T(8,128)(2,1)S(1)}, u32[]{:S(2)}, u32[]{:S(2)}) collective-permute-start(bf16[144,384]{1,0:T(8,128)(2,1)} %get-tuple-element.15), channel_id=1, source_target_pairs={{0,0},{1,8},{2,2},{3,10},{4,4},{5,12},{6,6},{7,14},{8,1},{9,9},{10... | collective-permute-start | bytes 331784 | tf_op jit(solution)/shard_map/ppermute | solution.py:432
  4.5 12.1 %collective-permute-start.1 = (bf16[144,384]{1,0:T(8,128)(2,1)}, bf16[144,384]{1,0:T(8,128)(2,1)S(1)}, u32[]{:S(2)}, u32[]{:S(2)}) collective-permute-start(bf16[144,384]{1,0:T(8,128)(2,1)} %get-tuple-element.16), channel_id=1, source_target_pairs={{0,16},{1,24},{2,18},{3,26},{4,20},{5,28},{6,22},{7,30},{8,17},{9,... | collective-permute-start | bytes 331784 | tf_op jit(solution)/shard_map/ppermute | solution.py:432
  8.1 11.6 %collective-permute-start.2 = (bf16[144,384]{1,0:T(8,128)(2,1)}, bf16[144,384]{1,0:T(8,128)(2,1)S(1)}, u32[]{:S(2)}, u32[]{:S(2)}) collective-permute-start(bf16[144,384]{1,0:T(8,128)(2,1)} %get-tuple-element.17), channel_id=1, source_target_pairs={{0,48},{1,56},{2,50},{3,58},{4,52},{5,60},{6,54},{7,62},{8,49},{9,... | collective-permute-start | bytes 331784 | tf_op jit(solution)/shard_map/ppermute | solution.py:432
  11.2 13.1 %collective-permute-start.3 = (bf16[144,384]{1,0:T(8,128)(2,1)}, bf16[144,384]{1,0:T(8,128)(2,1)S(1)}, u32[]{:S(2)}, u32[]{:S(2)}) collective-permute-start(bf16[144,384]{1,0:T(8,128)(2,1)} %get-tuple-element.18), channel_id=1, source_target_pairs={{0,32},{1,40},{2,34},{3,42},{4,36},{5,44},{6,38},{7,46},{8,33},{9,... | collective-permute-start | bytes 331784 | tf_op jit(solution)/shard_map/ppermute | solution.py:432
  16.6 11.1 %collective-permute-start.5 = (bf16[272,384]{1,0:T(8,128)(2,1)S(1)}, bf16[272,384]{1,0:T(8,128)(2,1)S(1)}, u32[]{:S(2)}, u32[]{:S(2)}) collective-permute-start(bf16[272,384]{1,0:T(8,128)(2,1)S(1)} %shard_map.77.before), channel_id=1, source_target_pairs={{0,192},{1,65},{2,194},{3,67},{4,196},{5,69},{6,198},{7,71},{8,200... | collective-permute-start | bytes 626696 | tf_op jit(solution)/shard_map/ppermute | solution.py:452
  19.7 8.5 %collective-permute-start.4 = (bf16[272,384]{1,0:T(8,128)(2,1)S(1)}, bf16[272,384]{1,0:T(8,128)(2,1)S(1)}, u32[]{:S(2)}, u32[]{:S(2)}) collective-permute-start(bf16[272,384]{1,0:T(8,128)(2,1)S(1)} %shard_map.77.before), channel_id=1, source_target_pairs={{0,64},{1,193},{2,66},{3,195},{4,68},{5,197},{6,70},{7,199},{8,72}... | collective-permute-start | bytes 626696 | tf_op jit(solution)/shard_map/ppermute | solution.py:451
  24.4 8.5 %collective-permute-start.7 = (bf16[272,384]{1,0:T(8,128)(2,1)S(1)}, bf16[272,384]{1,0:T(8,128)(2,1)S(1)}, u32[]{:S(2)}, u32[]{:S(2)}) collective-permute-start(bf16[272,384]{1,0:T(8,128)(2,1)S(1)} %get-tuple-element.20), channel_id=1, source_target_pairs={{0,64},{1,193},{2,66},{3,195},{4,68},{5,197},{6,70},{7,199},{8,72}... | collective-permute-start | bytes 626696 | tf_op jit(solution)/shard_map/ppermute | solution.py:451
  26.1 6.8 %collective-permute-start.8 = (bf16[272,384]{1,0:T(8,128)(2,1)S(1)}, bf16[272,384]{1,0:T(8,128)(2,1)S(1)}, u32[]{:S(2)}, u32[]{:S(2)}) collective-permute-start(bf16[272,384]{1,0:T(8,128)(2,1)S(1)} %get-tuple-element.20), channel_id=1, source_target_pairs={{0,192},{1,65},{2,194},{3,67},{4,196},{5,69},{6,198},{7,71},{8,200... | collective-permute-start | bytes 626696 | tf_op jit(solution)/shard_map/ppermute | solution.py:452
  27.7 12.2 %collective-permute-start.10 = (bf16[544,384]{1,0:T(8,128)(2,1)S(1)}, bf16[544,384]{1,0:T(8,128)(2,1)S(1)}, u32[]{:S(2)}, u32[]{:S(2)}) collective-permute-start(bf16[544,384]{1,0:T(8,128)(2,1)S(1)} %get-tuple-element.19.refs_0_), channel_id=1, source_target_pairs={{0,1},{1,0},{2,3},{3,2},{4,5},{5,4},{6,7},{7,6},{8,9},{9,8},{10,11... | collective-permute-start | bytes 1253384 | tf_op jit(solution)/shard_map/ppermute | solution.py:455
  27.7 5.3 %collective-permute-start.12 = (bf16[272,384]{1,0:T(8,128)(2,1)S(1)}, bf16[272,384]{1,0:T(8,128)(2,1)S(1)}, u32[]{:S(2)}, u32[]{:S(2)}) collective-permute-start(bf16[272,384]{1,0:T(8,128)(2,1)S(1)} %collective-permute-done.5.refs_2_), channel_id=1, source_target_pairs={{0,1},{1,0},{2,3},{3,2},{4,5},{5,4},{6,7},{7,6},{8,9},{9,8},{10,11... | collective-permute-start | bytes 626696 | tf_op jit(solution)/shard_map/ppermute | solution.py:455
  28.2 7.0 %collective-permute-start.6 = (bf16[272,384]{1,0:T(8,128)(2,1)S(1)}, bf16[272,384]{1,0:T(8,128)(2,1)S(1)}, u32[]{:S(2)}, u32[]{:S(2)}) collective-permute-start(bf16[272,384]{1,0:T(8,128)(2,1)S(1)} %collective-permute-done.4.refs_1_), channel_id=1, source_target_pairs={{0,64},{1,193},{2,66},{3,195},{4,68},{5,197},{6,70},{7,199},{8,72}... | collective-permute-start | bytes 626696 | tf_op jit(solution)/shard_map/ppermute | solution.py:453
  32.9 7.0 %collective-permute-start.9 = (bf16[272,384]{1,0:T(8,128)(2,1)S(1)}, bf16[272,384]{1,0:T(8,128)(2,1)S(1)}, u32[]{:S(2)}, u32[]{:S(2)}) collective-permute-start(bf16[272,384]{1,0:T(8,128)(2,1)S(1)} %collective-permute-done.7.refs_0_), channel_id=1, source_target_pairs={{0,64},{1,193},{2,66},{3,195},{4,68},{5,197},{6,70},{7,199},{8,72}... | collective-permute-start | bytes 626696 | tf_op jit(solution)/shard_map/ppermute | solution.py:453
  32.9 8.4 %collective-permute-start.14 = (bf16[544,384]{1,0:T(8,128)(2,1)S(1)}, bf16[544,384]{1,0:T(8,128)(2,1)S(1)}, u32[]{:S(2)}, u32[]{:S(2)}) collective-permute-start(bf16[544,384]{1,0:T(8,128)(2,1)S(1)} %shard_map.79.refs_4_), channel_id=1, source_target_pairs={{0,1},{1,0},{2,3},{3,2},{4,5},{5,4},{6,7},{7,6},{8,9},{9,8},{10,11... | collective-permute-start | bytes 1253384 | tf_op jit(solution)/shard_map/ppermute | solution.py:455
  33.1 6.9 %collective-permute-start.11 = (bf16[272,384]{1,0:T(8,128)(2,1)S(1)}, bf16[272,384]{1,0:T(8,128)(2,1)S(1)}, u32[]{:S(2)}, u32[]{:S(2)}) collective-permute-start(bf16[272,384]{1,0:T(8,128)(2,1)S(1)} %collective-permute-done.4.refs_1_), channel_id=1, source_target_pairs={{0,1},{1,0},{2,3},{3,2},{4,5},{5,4},{6,7},{7,6},{8,9},{9,8},{10,11... | collective-permute-start | bytes 626696 | tf_op jit(solution)/shard_map/ppermute | solution.py:455
  35.3 4.7 %collective-permute-start.13 = (bf16[272,384]{1,0:T(8,128)(2,1)S(1)}, bf16[272,384]{1,0:T(8,128)(2,1)S(1)}, u32[]{:S(2)}, u32[]{:S(2)}) collective-permute-start(bf16[272,384]{1,0:T(8,128)(2,1)S(1)} %collective-permute-done.6.refs_3_), channel_id=1, source_target_pairs={{0,1},{1,0},{2,3},{3,2},{4,5},{5,4},{6,7},{7,6},{8,9},{9,8},{10,11... | collective-permute-start | bytes 626696 | tf_op jit(solution)/shard_map/ppermute | solution.py:455
  39.9 1.5 %collective-permute-start.15 = (bf16[272,384]{1,0:T(8,128)(2,1)S(1)}, bf16[272,384]{1,0:T(8,128)(2,1)S(1)}, u32[]{:S(2)}, u32[]{:S(2)}) collective-permute-start(bf16[272,384]{1,0:T(8,128)(2,1)S(1)} %collective-permute-done.9.refs_5_), channel_id=1, source_target_pairs={{0,1},{1,0},{2,3},{3,2},{4,5},{5,4},{6,7},{7,6},{8,9},{9,8},{10,11... | collective-permute-start | bytes 626696 | tf_op jit(solution)/shard_map/ppermute | solution.py:455
  43.4 3.8 %collective-permute-start.16 = (f32[8,256]{1,0:T(8,128)S(1)}, f32[8,256]{1,0:T(8,128)S(1)}, u32[]{:S(2)}, u32[]{:S(2)}) collective-permute-start(f32[8,256]{1,0:T(8,128)S(1)} %shard_map.80), channel_id=1, source_target_pairs={{0,1},{1,0},{2,3},{3,2},{4,5},{5,4},{6,7},{7,6},{8,9},{9,8},{10,11... | collective-permute-start | bytes 24584 | tf_op jit(solution)/shard_map/ppermute | solution.py:457
  47.2 4.9 %collective-permute-start.19 = (f32[16,256]{1,0:T(8,128)S(1)}, f32[16,256]{1,0:T(8,128)S(1)}, u32[]{:S(2)}, u32[]{:S(2)}) collective-permute-start(f32[16,256]{1,0:T(8,128)S(1)} %pad_maximum_fusion.refs_12_), channel_id=1, source_target_pairs={{0,192},{1,193},{2,194},{3,195},{4,196},{5,197},{6,198},{7,199},{8... | collective-permute-start | bytes 49160 | tf_op jit(solution)/shard_map/ppermute | solution.py:458
  47.2 5.2 %collective-permute-start.18 = (f32[16,256]{1,0:T(8,128)S(1)}, f32[16,256]{1,0:T(8,128)S(1)}, u32[]{:S(2)}, u32[]{:S(2)}) collective-permute-start(f32[16,256]{1,0:T(8,128)S(1)} %pad_maximum_fusion.refs_12_), channel_id=1, source_target_pairs={{0,128},{1,129},{2,130},{3,131},{4,132},{5,133},{6,134},{7,135},{8... | collective-permute-start | bytes 49160 | tf_op jit(solution)/shard_map/ppermute | solution.py:458
  48.0 5.1 %collective-permute-start.17 = (f32[16,256]{1,0:T(8,128)S(1)}, f32[16,256]{1,0:T(8,128)S(1)}, u32[]{:S(2)}, u32[]{:S(2)}) collective-permute-start(f32[16,256]{1,0:T(8,128)S(1)} %pad_maximum_fusion.refs_12_), channel_id=1, source_target_pairs={{0,64},{1,65},{2,66},{3,67},{4,68},{5,69},{6,70},{7,71},{8,72},{9,... | collective-permute-start | bytes 49160 | tf_op jit(solution)/shard_map/ppermute | solution.py:458
  60.1 6.8 %collective-permute-start.20 = (bf16[144,128]{1,0:T(8,128)(2,1)S(1)}, bf16[144,128]{1,0:T(8,128)(2,1)S(1)}, u32[]{:S(2)}, u32[]{:S(2)}) collective-permute-start(bf16[144,128]{1,0:T(8,128)(2,1)S(1)} %get-tuple-element.21), channel_id=1, source_target_pairs={{0,0},{8,1},{2,2},{10,3},{4,4},{12,5},{6,6},{14,7},{1,8},{9,9},{3,... | collective-permute-start | bytes 110600 | tf_op jit(solution)/shard_map/ppermute | solution.py:461
  62.2 4.7 %collective-permute-start.21 = (bf16[144,128]{1,0:T(8,128)(2,1)S(1)}, bf16[144,128]{1,0:T(8,128)(2,1)S(1)}, u32[]{:S(2)}, u32[]{:S(2)}) collective-permute-start(bf16[144,128]{1,0:T(8,128)(2,1)S(1)} %get-tuple-element.22), channel_id=1, source_target_pairs={{16,0},{24,1},{18,2},{26,3},{20,4},{28,5},{22,6},{30,7},{17,8},{25... | collective-permute-start | bytes 110600 | tf_op jit(solution)/shard_map/ppermute | solution.py:461
  63.2 6.7 %collective-permute-start.22 = (bf16[144,128]{1,0:T(8,128)(2,1)S(1)}, bf16[144,128]{1,0:T(8,128)(2,1)S(1)}, u32[]{:S(2)}, u32[]{:S(2)}) collective-permute-start(bf16[144,128]{1,0:T(8,128)(2,1)S(1)} %get-tuple-element.23), channel_id=1, source_target_pairs={{32,0},{40,1},{34,2},{42,3},{36,4},{44,5},{38,6},{46,7},{33,8},{41... | collective-permute-start | bytes 110600 | tf_op jit(solution)/shard_map/ppermute | solution.py:461
  64.4 6.9 %collective-permute-start.23 = (bf16[144,128]{1,0:T(8,128)(2,1)S(1)}, bf16[144,128]{1,0:T(8,128)(2,1)S(1)}, u32[]{:S(2)}, u32[]{:S(2)}) collective-permute-start(bf16[144,128]{1,0:T(8,128)(2,1)S(1)} %get-tuple-element.24), channel_id=1, source_target_pairs={{48,0},{56,1},{50,2},{58,3},{52,4},{60,5},{54,6},{62,7},{49,8},{57... | collective-permute-start | bytes 110600 | tf_op jit(solution)/shard_map/ppermute | solution.py:461
  71.3 1.2 %collective-permute-start.24 = (f32[8,128]{1,0:T(8,128)S(1)}, f32[8,128]{1,0:T(8,128)S(1)}, u32[]{:S(2)}, u32[]{:S(2)}) collective-permute-start(f32[8,128]{1,0:T(8,128)S(1)} %bitcast_reduce_fusion), channel_id=1, source_target_pairs={{0,1},{1,0},{2,3},{3,2},{4,5},{5,4},{6,7},{7,6},{8,9},{9,8},{10,11... | collective-permute-start | bytes 12296 | tf_op jit(solution)/shard_map/ppermute | solution.py:465
  72.5 4.8 %collective-permute-start.27 = (f32[8,128]{1,0:T(8,128)S(1)}, f32[8,128]{1,0:T(8,128)S(1)}, u32[]{:S(2)}, u32[]{:S(2)}) collective-permute-start(f32[8,128]{1,0:T(8,128)S(1)} %add.24), channel_id=1, source_target_pairs={{0,6},{1,7},{2,4},{3,5},{4,2},{5,3},{6,0},{7,1},{8,14},{9,15},{10,... | collective-permute-start | bytes 12296 | tf_op jit(solution)/shard_map/ppermute | solution.py:466
  75.3 5.1 %collective-permute-start.26 = (f32[8,128]{1,0:T(8,128)S(1)}, f32[8,128]{1,0:T(8,128)S(1)}, u32[]{:S(2)}, u32[]{:S(2)}) collective-permute-start(f32[8,128]{1,0:T(8,128)S(1)} %add.24), channel_id=1, source_target_pairs={{0,4},{1,5},{2,6},{3,7},{4,0},{5,1},{6,2},{7,3},{8,12},{9,13},{10,... | collective-permute-start | bytes 12296 | tf_op jit(solution)/shard_map/ppermute | solution.py:466
  76.1 4.3 %collective-permute-start.25 = (f32[8,128]{1,0:T(8,128)S(1)}, f32[8,128]{1,0:T(8,128)S(1)}, u32[]{:S(2)}, u32[]{:S(2)}) collective-permute-start(f32[8,128]{1,0:T(8,128)S(1)} %add.24), channel_id=1, source_target_pairs={{0,2},{1,3},{2,0},{3,1},{4,6},{5,7},{6,4},{7,5},{8,10},{9,11},{10,... | collective-permute-start | bytes 12296 | tf_op jit(solution)/shard_map/ppermute | solution.py:466

commit v3 on v2

--- a/solution.py
+++ b/solution.py
@@ -26,6 +26,8 @@
 ORDER = (0, 1, 3, 2)
 PIECE = 2 * ROWS + 16
 UNROLL = 2
+STEP = 1
+SPANS = (4, 2, 1)
 PACK_FLOPS = 20_000_000_000
 F32 = jnp.float32
 BF16 = jnp.bfloat16
@@ -181,23 +183,24 @@
     return pl.ds(pl.multiple_of(t * TILE, TILE), TILE)
 
 
-def folded(values):
-    return values.reshape(TILE // 8, 8, TILE)
+def bounds_in_rows(bounds):
+    return jnp.transpose(jnp.broadcast_to(bounds, (128, 128)))[0:16, 0:1]
+
+
+def eights(values):
+    return values.reshape(values.shape[0] // 8, 8, TILE)
 
 
 def norm_kernel(*refs):
-    parts, out = refs[:12], refs[12]
-    rows, scores_t, scores_s = refs[13:]
+    parts, out, rows = refs[:12], refs[12], refs[13]
     bounds = assemble(parts, rows)
     y, z, core = placed()
     r = y * 2 + core
-    bounds_down = jnp.transpose(jnp.broadcast_to(bounds, (128, 128)))[0:16, 0:1]
+    bounds_down = bounds_in_rows(bounds)
     out[...] = jnp.zeros_like(out)
     for half in range(2):
         t = r if half == 0 else TILES - 1 - r
         first = t * TILE
-        mine_t = rows[tile_rows(t), 0:TDIM]
-        mine_s = rows[tile_rows(t), TDIM:WIDE]
         low = start_of(bounds, first.astype(F32)).astype(jnp.int32)
         high = start_of(bounds, (first + TILE - 1).astype(F32)).astype(jnp.int32)
         my_pos = first + lax.broadcasted_iota(jnp.int32, (1, TILE), 1)
@@ -205,61 +208,55 @@
             jnp.where(bounds_down <= my_pos.astype(F32), bounds_down, 0.0), axis=0, keepdims=True
         ).astype(jnp.int32)
 
-        def span(c, n):
-            return pl.ds(pl.multiple_of(c * TILE, TILE), n * TILE)
-
-        def eights(values):
-            return values.reshape(values.shape[0] // 8, 8, TILE)
-
-        def score(c, tops, n, masked):
-            t_tile = nt_dot(rows[span(c, n), 0:TDIM], mine_t) * KT
-            s_tile = nt_dot(rows[span(c, n), TDIM:WIDE], mine_s) * KS
+        def online(c, state, n, masked):
+            top_t, top_s, sum_t, sum_s, cross = state
+            span = pl.ds(pl.multiple_of(c * TILE, TILE), n * TILE)
+            t_tile = nt_dot(rows[span, 0:TDIM], rows[tile_rows(t), 0:TDIM]) * KT
+            s_tile = nt_dot(rows[span, TDIM:WIDE], rows[tile_rows(t), TDIM:WIDE]) * KS
             if masked:
                 pos = c * TILE + lax.broadcasted_iota(jnp.int32, (n * TILE, TILE), 0)
                 seen = (pos <= my_pos) & (pos >= my_start)
                 t_tile = jnp.where(seen, t_tile, NEG)
                 s_tile = jnp.where(seen, s_tile, NEG)
-            scores_t[span(c, n), :] = t_tile
-            scores_s[span(c, n), :] = s_tile
+            new_t = jnp.maximum(top_t, jnp.max(jnp.max(eights(t_tile), axis=0), axis=0, keepdims=True))
+            new_s = jnp.maximum(top_s, jnp.max(jnp.max(eights(s_tile), axis=0), axis=0, keepdims=True))
+            p = jnp.exp2(t_tile - new_t)
+            q = jnp.exp2(s_tile - new_s)
+            decay_t = jnp.exp2(top_t - new_t)
+            decay_s = jnp.exp2(top_s - new_s)
             return (
-                jnp.maximum(tops[0], jnp.max(eights(t_tile), axis=0)),
-                jnp.maximum(tops[1], jnp.max(eights(s_tile), axis=0)),
+                new_t,
+                new_s,
+                sum_t * decay_t + jnp.sum(eights(p), axis=0),
+                sum_s * decay_s + jnp.sum(eights(q), axis=0),
+                cross * decay_t + jnp.sum(eights(p * (t_tile - s_tile)), axis=0),
             )
 
-        def run(begin, stop, carry, body, n=1):
-            return lax.fori_loop(0, (stop - begin) // n, lambda i, v: body(begin + n * i, v, n), carry)
-
-        def run_all(begin, stop, carry, body):
-            for n in (4, 2, 1):
+        def several(c, state, n, masked):
+            for part in range(0, n, STEP):
+                state = online(c + part, state, min(n, STEP), masked)
+            return state
+
+        def run_all(begin, stop, state, masked):
+            for n in SPANS:
                 middle = stop - (stop - begin) % n
-                carry = run(begin, middle, carry, body, n)
+                state = lax.fori_loop(
+                    0,
+                    (middle - begin) // n,
+                    lambda i, v: several(begin + n * i, v, n, masked),
+                    state,
+                )
                 begin = middle
-            return carry
+            return state
 
         from_tile = low // TILE
         plain_tile = jnp.minimum((high + TILE - 1) // TILE, t)
-        tops = (jnp.full((8, TILE), NEG, F32), jnp.full((8, TILE), NEG, F32))
-        tops = run_all(from_tile, plain_tile, tops, functools.partial(score, masked=True))
-        tops = run_all(plain_tile, t, tops, functools.partial(score, masked=False))
-        tops = score(t, tops, 1, True)
-        top_t = jnp.max(tops[0], axis=0, keepdims=True)
-        top_s = jnp.max(tops[1], axis=0, keepdims=True)
-
-        def add(c, sums, n):
-            sum_t, sum_s, cross = sums
-            t_tile = scores_t[span(c, n), :]
-            s_tile = scores_s[span(c, n), :]
-            p = jnp.exp2(t_tile - top_t)
-            q = jnp.exp2(s_tile - top_s)
-            return (
-                sum_t + jnp.sum(eights(p), axis=0),
-                sum_s + jnp.sum(eights(q), axis=0),
-                cross + jnp.sum(eights(p * (t_tile - s_tile)), axis=0),
-            )
-
-        zero = jnp.zeros((8, TILE), F32)
-        sums = run_all(from_tile, t + 1, (zero, zero, zero), add)
-        sum_t, sum_s, cross = (jnp.sum(v, axis=0, keepdims=True) for v in sums)
+        none, zero = jnp.full((1, TILE), NEG, F32), jnp.zeros((8, TILE), F32)
+        state = online(t, (none, none, zero, zero, zero), 1, True)
+        state = run_all(from_tile, plain_tile, state, True)
+        state = run_all(plain_tile, t, state, False)
+        top_t, top_s = state[:2]
+        sum_t, sum_s, cross = (jnp.sum(v, axis=0, keepdims=True) for v in state[2:])
         lse_t = top_t * LN2 + jnp.log(sum_t)
         lse_s = top_s * LN2 + jnp.log(sum_s)
         row_kl = cross * LN2 / sum_t - lse_t + lse_s
@@ -339,24 +336,15 @@
 
         lax.fori_loop(0, (stop - begin) // n, body, 0)
 
+    wide = UNROLL * TILE
     diag = 4 * y
-    plain = jnp.minimum((start_high + TILE - 1) // TILE, diag)
-    begin = start_low // TILE
-    odd = plain - (plain - begin) % UNROLL
-    run(begin, odd, "below", True, UNROLL)
-    run(odd, plain, "below", True)
-    odd = plain + (diag - plain) % UNROLL
-    run(plain, odd, "below", False)
-    run(odd, diag, "below", False, UNROLL)
-    run(diag, diag + 4, "diagonal", True, 2)
-    plain = jnp.maximum(end_low // TILE, diag + 4)
-    odd = diag + 4 + (plain - diag - 4) % UNROLL
-    run(diag + 4, odd, "above", False)
-    run(odd, plain, "above", False, UNROLL)
-    stop = (end_high + TILE - 1) // TILE
-    odd = plain + (stop - plain) % UNROLL
-    run(plain, odd, "above", True)
-    run(odd, stop, "above", True, UNROLL)
+    plain = jnp.minimum((start_high + wide - 1) // wide * UNROLL, diag)
+    run(start_low // wide * UNROLL, plain, "below", True, UNROLL)
+    run(plain, diag, "below", False, UNROLL)
+    run(diag, diag + 4, "diagonal", True, UNROLL)
+    plain = jnp.maximum(end_low // wide * UNROLL, diag + 4)
+    run(diag + 4, plain, "above", False, UNROLL)
+    run(plain, (end_high + wide - 1) // wide * UNROLL, "above", True, UNROLL)
     for b in range(4):
         for j in range(4):
 
@@ -391,8 +379,6 @@
         out_specs=ALL,
         scratch_shapes=[
             pltpu.VMEM((TOKENS, WIDE), BF16),
-            pltpu.VMEM((TOKENS, TILE), F32),
-            pltpu.VMEM((TOKENS, TILE), F32),
         ],
         compiler_params=params(),
     )(*parts)
@@ -455,7 +441,7 @@
     parts += [lax.ppermute(part, AXES, CORE_PAIRS) for part in parts]
     packet = call_norm(parts)
     both = jnp.concatenate([packet, lax.ppermute(packet, AXES, CORE_PAIRS)])
-    others = {step: lax.ppermute(both, AXES, mirror_pairs(step)) for step in (2, 1, 3)}
+    others = {step: lax.ppermute(both, AXES, mirror_pairs(step)) for step in (3, 1, 2)}
     packets = [both] + [others[step] for step in (1, 2, 3)]
     grads = call_grad(parts, packets)
     backs = {j: lax.ppermute(grads[j], AXES, collect_pairs(j)) for j in (2, 3, 1, 0)}

time: 82.7 us -> 82.3 us (level); the launches traced: 82.8 us -> 81.3 us
  starting transfers between devices: 37.4 us -> 35.6 us
  waiting for transfers between devices: 30.6 us -> 31.8 us
  Pallas kernels: 11.6 us -> 10.7 us
    ppermute x1, starting transfers between devices: 3 us -> 0.58 us  [per_device(): both = jnp.concatenate([packet, lax.ppermute(packet, AXES, CORE_PAIRS)])]
    ppermute x3, waiting for transfers between devices: 1.89 us -> 3.55 us  [per_device(): lax.ppermute(both, AXES, mirror_pairs(step))]
  transfers between devices with their start and end apart: 28 -> 28, of which waited for: 14 -> 13; matrix products, arithmetic and copies ran while one was open for 0% -> 0% of each run, Pallas kernels for 1% -> 1%
where the time goes in v3:
time: 82.3 us; the launch traced here: 81.3 us
  starting transfers between devices  35.6 us (43%)
  waiting for transfers between devices  31.8 us (39%)
  Pallas kernels  10.7 us (13%)
  between operations  2.51 us (3%)
    ppermute x4, starting transfers between devices, per_device(): gots = [lax.ppermute(sends[j], AXES, spread_pairs(j)) for j in ORDER]  11.5 us
    ppermute x4, starting transfers between devices, per_device(): lax.ppermute(grads[j], AXES, collect_pairs(j))  7.49 us
    ppermute x4, waiting for transfers between devices, per_device(): gots = [lax.ppermute(sends[j], AXES, spread_pairs(j)) for j in ORDER]  7.15 us
    ppermute x2, waiting for transfers between devices, per_device(): lax.ppermute(near, AXES, near_pairs(1))  6.36 us
    pallas_call x1, Pallas kernels, call_grad(): pl.pallas_call(grad_kernel, out_shape=[jax.ShapeDtypeStruct((ROWS + 16, H...  6.3 us
    ppermute x2, starting transfers between devices, per_device(): lax.ppermute(mine, AXES, near_pairs(-1))  4.75 us
    ppermute x2, waiting for transfers between devices, per_device(): lax.ppermute(mine, AXES, near_pairs(1))  4.29 us
    ppermute x3, starting transfers between devices, per_device(): lax.ppermute(both, AXES, mirror_pairs(step))  4.09 us
  transfers between devices with their start and end apart: 28, of which 13 were waited for; matrix products, arithmetic and copies ran while one was open for 0% of the time, Pallas kernels for 1%

profile of v3, /device:TPU:32, one launch (start us, length us, event | category | flops | bytes accessed | tf_op | source)
XLA Modules:
  0.0 81.3 jit_solution(10726218518935349813)
XLA Ops:
  0.6 1.9 %shard_map.76 = (bf16[144,384]{1,0:T(8,128)(2,1)}, bf16[144,384]{1,0:T(8,128)(2,1)}, bf16[144,384]{1,0:T(8,128)(2,1)}, bf16[144,384]{1,0:T(8,128)(2,1)}) custom-call(bf16[128,512]{1,0:T(8,128)(2,1)} %tq.1, bf16[128,512]{1,0:T(8,128)(2,1)} %tk.1, bf16[128,256]{1,0:T(8,128)(2,1)} %sq.1, bf16[128,256]{1,0:T(8,128)(2,1)} %sk.1, s32[1,128]{1,0:T(1,128)} %bitcast.3), custom_call_target="tpu_custom_call" | custom-call | tf_op jit(solution)/shard_map/pallas_call | solution.py:406
  2.6 1.9 %collective-permute-start = (bf16[144,384]{1,0:T(8,128)(2,1)}, bf16[144,384]{1,0:T(8,128)(2,1)S(1)}, u32[]{:S(2)}, u32[]{:S(2)}) collective-permute-start(bf16[144,384]{1,0:T(8,128)(2,1)} %get-tuple-element.15), channel_id=1, source_target_pairs={{0,0},{1,8},{2,2},{3,10},{4,4},{5,12},{6,6},{7,14},{8,1},{9,9},{10... | collective-permute-start | bytes 331784 | tf_op jit(solution)/shard_map/ppermute | solution.py:418
  4.5 3.6 %collective-permute-start.1 = (bf16[144,384]{1,0:T(8,128)(2,1)}, bf16[144,384]{1,0:T(8,128)(2,1)S(1)}, u32[]{:S(2)}, u32[]{:S(2)}) collective-permute-start(bf16[144,384]{1,0:T(8,128)(2,1)} %get-tuple-element.16), channel_id=1, source_target_pairs={{0,16},{1,24},{2,18},{3,26},{4,20},{5,28},{6,22},{7,30},{8,17},{9,... | collective-permute-start | bytes 331784 | tf_op jit(solution)/shard_map/ppermute | solution.py:418
  8.1 3.1 %collective-permute-start.2 = (bf16[144,384]{1,0:T(8,128)(2,1)}, bf16[144,384]{1,0:T(8,128)(2,1)S(1)}, u32[]{:S(2)}, u32[]{:S(2)}) collective-permute-start(bf16[144,384]{1,0:T(8,128)(2,1)} %get-tuple-element.17), channel_id=1, source_target_pairs={{0,48},{1,56},{2,50},{3,58},{4,52},{5,60},{6,54},{7,62},{8,49},{9,... | collective-permute-start | bytes 331784 | tf_op jit(solution)/shard_map/ppermute | solution.py:418
  11.2 2.9 %collective-permute-start.3 = (bf16[144,384]{1,0:T(8,128)(2,1)}, bf16[144,384]{1,0:T(8,128)(2,1)S(1)}, u32[]{:S(2)}, u32[]{:S(2)}) collective-permute-start(bf16[144,384]{1,0:T(8,128)(2,1)} %get-tuple-element.18), channel_id=1, source_target_pairs={{0,32},{1,40},{2,34},{3,42},{4,36},{5,44},{6,38},{7,46},{8,33},{9,... | collective-permute-start | bytes 331784 | tf_op jit(solution)/shard_map/ppermute | solution.py:418
  14.1 2.5 %collective-permute-done.1.second = bf16[144,384]{1,0:T(8,128)(2,1)S(1)} collective-permute-done((bf16[144,384]{1,0:T(8,128)(2,1)}, bf16[144,384]{1,0:T(8,128)(2,1)S(1)}, u32[]{:S(2)}, u32[]{:S(2)}) %collective-permute-start.1) | collective-permute-done | bytes 110624 | tf_op jit(solution)/shard_map/ppermute | solution.py:418
  16.6 3.1 %collective-permute-start.5 = (bf16[272,384]{1,0:T(8,128)(2,1)S(1)}, bf16[272,384]{1,0:T(8,128)(2,1)S(1)}, u32[]{:S(2)}, u32[]{:S(2)}) collective-permute-start(bf16[272,384]{1,0:T(8,128)(2,1)S(1)} %shard_map.77.before), channel_id=1, source_target_pairs={{0,192},{1,65},{2,194},{3,67},{4,196},{5,69},{6,198},{7,71},{8,200... | collective-permute-start | bytes 626696 | tf_op jit(solution)/shard_map/ppermute | solution.py:438
  19.7 4.6 %collective-permute-done.3.second = bf16[144,384]{1,0:T(8,128)(2,1)S(1)} collective-permute-done((bf16[144,384]{1,0:T(8,128)(2,1)}, bf16[144,384]{1,0:T(8,128)(2,1)S(1)}, u32[]{:S(2)}, u32[]{:S(2)}) %collective-permute-start.3) | collective-permute-done | bytes 110624 | tf_op jit(solution)/shard_map/ppermute | solution.py:418
  24.4 1.7 %collective-permute-start.7 = (bf16[272,384]{1,0:T(8,128)(2,1)S(1)}, bf16[272,384]{1,0:T(8,128)(2,1)S(1)}, u32[]{:S(2)}, u32[]{:S(2)}) collective-permute-start(bf16[272,384]{1,0:T(8,128)(2,1)S(1)} %get-tuple-element.20), channel_id=1, source_target_pairs={{0,64},{1,193},{2,66},{3,195},{4,68},{5,197},{6,70},{7,199},{8,72}... | collective-permute-start | bytes 626696 | tf_op jit(solution)/shard_map/ppermute | solution.py:437
  26.1 1.7 %collective-permute-start.8 = (bf16[272,384]{1,0:T(8,128)(2,1)S(1)}, bf16[272,384]{1,0:T(8,128)(2,1)S(1)}, u32[]{:S(2)}, u32[]{:S(2)}) collective-permute-start(bf16[272,384]{1,0:T(8,128)(2,1)S(1)} %get-tuple-element.20), channel_id=1, source_target_pairs={{0,192},{1,65},{2,194},{3,67},{4,196},{5,69},{6,198},{7,71},{8,200... | collective-permute-start | bytes 626696 | tf_op jit(solution)/shard_map/ppermute | solution.py:438
  28.6 4.3 %collective-permute-done.7.refs_0_ = bf16[272,384]{1,0:T(8,128)(2,1)S(1)} collective-permute-done((bf16[272,384]{1,0:T(8,128)(2,1)S(1)}, bf16[272,384]{1,0:T(8,128)(2,1)S(1)}, u32[]{:S(2)}, u32[]{:S(2)}) %collective-permute-start.7) | collective-permute-done | bytes 208928 | tf_op jit(solution)/shard_map/ppermute | solution.py:437
  33.6 1.7 %collective-permute-done.6.refs_3_ = bf16[272,384]{1,0:T(8,128)(2,1)S(1)} collective-permute-done((bf16[272,384]{1,0:T(8,128)(2,1)S(1)}, bf16[272,384]{1,0:T(8,128)(2,1)S(1)}, u32[]{:S(2)}, u32[]{:S(2)}) %collective-permute-start.6) | collective-permute-done | bytes 208928 | tf_op jit(solution)/shard_map/ppermute | solution.py:439
  35.3 4.6 %collective-permute-done.9.refs_5_ = bf16[272,384]{1,0:T(8,128)(2,1)S(1)} collective-permute-done((bf16[272,384]{1,0:T(8,128)(2,1)S(1)}, bf16[272,384]{1,0:T(8,128)(2,1)S(1)}, u32[]{:S(2)}, u32[]{:S(2)}) %collective-permute-start.9) | collective-permute-done | bytes 208928 | tf_op jit(solution)/shard_map/ppermute | solution.py:439
  39.9 1.4 %collective-permute-done.15.refs_11_ = bf16[272,384]{1,0:T(8,128)(2,1)S(1)} collective-permute-done((bf16[272,384]{1,0:T(8,128)(2,1)S(1)}, bf16[272,384]{1,0:T(8,128)(2,1)S(1)}, u32[]{:S(2)}, u32[]{:S(2)}) %collective-permute-start.15) | collective-permute-done | bytes 208928 | tf_op jit(solution)/shard_map/ppermute | solution.py:441
  41.4 1.7 %shard_map.80 = f32[8,256]{1,0:T(8,128)S(1)} custom-call(bf16[544,384]{1,0:T(8,128)(2,1)S(1)} %get-tuple-element.19.refs_0_, bf16[272,384]{1,0:T(8,128)(2,1)S(1)} %collective-permute-done.4.refs_1_, bf16[272,384]{1,0:T(8,128)(2,1)S(1)} %collective-permute-done.5.refs_2_, bf16[272,384]{1,0:T(8,128)(2,1)S(1)} %collective-permute-done.6.refs_3_, ...), custom_call_target="tpu_custom_call" | custom-call | tf_op jit(solution)/shard_map/pallas_call | solution.py:375
  43.7 0.8 %collective-permute-done.16 = f32[8,256]{1,0:T(8,128)S(1)} collective-permute-done((f32[8,256]{1,0:T(8,128)S(1)}, f32[8,256]{1,0:T(8,128)S(1)}, u32[]{:S(2)}, u32[]{:S(2)}) %collective-permute-start.16) | collective-permute-done | bytes 8224 | tf_op jit(solution)/shard_map/ppermute | solution.py:443
  44.5 2.4 %collective-permute-start.19 = (f32[16,256]{1,0:T(8,128)S(1)}, f32[16,256]{1,0:T(8,128)S(1)}, u32[]{:S(2)}, u32[]{:S(2)}) collective-permute-start(f32[16,256]{1,0:T(8,128)S(1)} %pad_maximum_fusion.refs_12_), channel_id=1, source_target_pairs={{0,192},{1,193},{2,194},{3,195},{4,196},{5,197},{6,198},{7,199},{8... | collective-permute-start | bytes 49160 | tf_op jit(solution)/shard_map/ppermute | solution.py:444
  46.9 1.2 %collective-permute-start.18 = (f32[16,256]{1,0:T(8,128)S(1)}, f32[16,256]{1,0:T(8,128)S(1)}, u32[]{:S(2)}, u32[]{:S(2)}) collective-permute-start(f32[16,256]{1,0:T(8,128)S(1)} %pad_maximum_fusion.refs_12_), channel_id=1, source_target_pairs={{0,128},{1,129},{2,130},{3,131},{4,132},{5,133},{6,134},{7,135},{8... | collective-permute-start | bytes 49160 | tf_op jit(solution)/shard_map/ppermute | solution.py:444
  48.6 0.9 %collective-permute-done.19.refs_15_ = f32[16,256]{1,0:T(8,128)S(1)} collective-permute-done((f32[16,256]{1,0:T(8,128)S(1)}, f32[16,256]{1,0:T(8,128)S(1)}, u32[]{:S(2)}, u32[]{:S(2)}) %collective-permute-start.19) | collective-permute-done | bytes 16416 | tf_op jit(solution)/shard_map/ppermute | solution.py:444
  49.5 2.7 %collective-permute-done.18.refs_14_ = f32[16,256]{1,0:T(8,128)S(1)} collective-permute-done((f32[16,256]{1,0:T(8,128)S(1)}, f32[16,256]{1,0:T(8,128)S(1)}, u32[]{:S(2)}, u32[]{:S(2)}) %collective-permute-start.18) | collective-permute-done | bytes 16416 | tf_op jit(solution)/shard_map/ppermute | solution.py:444
  52.2 6.3 %shard_map.81 = (bf16[144,128]{1,0:T(8,128)(2,1)S(1)}, bf16[144,128]{1,0:T(8,128)(2,1)S(1)}, bf16[144,128]{1,0:T(8,128)(2,1)S(1)}, bf16[144,128]{1,0:T(8,128)(2,1)S(1)}) custom-call(bf16[544,384]{1,0:T(8,128)(2,1)S(1)} %get-tuple-element.19.refs_0_, bf16[272,384]{1,0:T(8,128)(2,1)S(1)} %collective-permute-done.4.refs_1_, ...), custom_call_target="tpu_custom_call" | custom-call | tf_op jit(solution)/shard_map/pallas_call | solution.py:388
  58.5 2.1 %collective-permute-start.20 = (bf16[144,128]{1,0:T(8,128)(2,1)S(1)}, bf16[144,128]{1,0:T(8,128)(2,1)S(1)}, u32[]{:S(2)}, u32[]{:S(2)}) collective-permute-start(bf16[144,128]{1,0:T(8,128)(2,1)S(1)} %get-tuple-element.21), channel_id=1, source_target_pairs={{0,0},{8,1},{2,2},{10,3},{4,4},{12,5},{6,6},{14,7},{1,8},{9,9},{3,... | collective-permute-start | bytes 110600 | tf_op jit(solution)/shard_map/ppermute | solution.py:447
  60.6 1.4 %collective-permute-start.21 = (bf16[144,128]{1,0:T(8,128)(2,1)S(1)}, bf16[144,128]{1,0:T(8,128)(2,1)S(1)}, u32[]{:S(2)}, u32[]{:S(2)}) collective-permute-start(bf16[144,128]{1,0:T(8,128)(2,1)S(1)} %get-tuple-element.22), channel_id=1, source_target_pairs={{16,0},{24,1},{18,2},{26,3},{20,4},{28,5},{22,6},{30,7},{17,8},{25... | collective-permute-start | bytes 110600 | tf_op jit(solution)/shard_map/ppermute | solution.py:447
  62.0 1.4 %collective-permute-start.22 = (bf16[144,128]{1,0:T(8,128)(2,1)S(1)}, bf16[144,128]{1,0:T(8,128)(2,1)S(1)}, u32[]{:S(2)}, u32[]{:S(2)}) collective-permute-start(bf16[144,128]{1,0:T(8,128)(2,1)S(1)} %get-tuple-element.23), channel_id=1, source_target_pairs={{32,0},{40,1},{34,2},{42,3},{36,4},{44,5},{38,6},{46,7},{33,8},{41... | collective-permute-start | bytes 110600 | tf_op jit(solution)/shard_map/ppermute | solution.py:447
  63.4 2.5 %collective-permute-start.23 = (bf16[144,128]{1,0:T(8,128)(2,1)S(1)}, bf16[144,128]{1,0:T(8,128)(2,1)S(1)}, u32[]{:S(2)}, u32[]{:S(2)}) collective-permute-start(bf16[144,128]{1,0:T(8,128)(2,1)S(1)} %get-tuple-element.24), channel_id=1, source_target_pairs={{48,0},{56,1},{50,2},{58,3},{52,4},{60,5},{54,6},{62,7},{49,8},{57... | collective-permute-start | bytes 110600 | tf_op jit(solution)/shard_map/ppermute | solution.py:447
  66.0 2.5 %collective-permute-done.22.g2 = bf16[144,128]{1,0:T(8,128)(2,1)S(1)} collective-permute-done((bf16[144,128]{1,0:T(8,128)(2,1)S(1)}, bf16[144,128]{1,0:T(8,128)(2,1)S(1)}, u32[]{:S(2)}, u32[]{:S(2)}) %collective-permute-start.22) | collective-permute-done | bytes 36896 | tf_op jit(solution)/shard_map/ppermute | solution.py:447
  68.4 1.4 %collective-permute-done.23.g3 = bf16[144,128]{1,0:T(8,128)(2,1)S(1)} collective-permute-done((bf16[144,128]{1,0:T(8,128)(2,1)S(1)}, bf16[144,128]{1,0:T(8,128)(2,1)S(1)}, u32[]{:S(2)}, u32[]{:S(2)}) %collective-permute-start.23) | collective-permute-done | bytes 36896 | tf_op jit(solution)/shard_map/ppermute | solution.py:447
  69.9 1.2 %collective-permute-done.24 = f32[8,128]{1,0:T(8,128)S(1)} collective-permute-done((f32[8,128]{1,0:T(8,128)S(1)}, f32[8,128]{1,0:T(8,128)S(1)}, u32[]{:S(2)}, u32[]{:S(2)}) %collective-permute-start.24) | collective-permute-done | bytes 4128 | tf_op jit(solution)/shard_map/ppermute | solution.py:451
  71.0 2.8 %collective-permute-start.27 = (f32[8,128]{1,0:T(8,128)S(1)}, f32[8,128]{1,0:T(8,128)S(1)}, u32[]{:S(2)}, u32[]{:S(2)}) collective-permute-start(f32[8,128]{1,0:T(8,128)S(1)} %add.24), channel_id=1, source_target_pairs={{0,6},{1,7},{2,4},{3,5},{4,2},{5,3},{6,0},{7,1},{8,14},{9,15},{10,... | collective-permute-start | bytes 12296 | tf_op jit(solution)/shard_map/ppermute | solution.py:452
  73.8 0.8 collective-permute-start.26
  75.1 0.7 shard_map.82
  75.8 3.1 %collective-permute-done.26 = f32[8,128]{1,0:T(8,128)S(1)} collective-permute-done((f32[8,128]{1,0:T(8,128)S(1)}, f32[8,128]{1,0:T(8,128)S(1)}, u32[]{:S(2)}, u32[]{:S(2)}) %collective-permute-start.26) | collective-permute-done | bytes 4128 | tf_op jit(solution)/shard_map/ppermute | solution.py:452
  (35 shorter events, 3.8 us)
Async XLA Ops:
  2.6 11.5 %collective-permute-start = (bf16[144,384]{1,0:T(8,128)(2,1)}, bf16[144,384]{1,0:T(8,128)(2,1)S(1)}, u32[]{:S(2)}, u32[]{:S(2)}) collective-permute-start(bf16[144,384]{1,0:T(8,128)(2,1)} %get-tuple-element.15), channel_id=1, source_target_pairs={{0,0},{1,8},{2,2},{3,10},{4,4},{5,12},{6,6},{7,14},{8,1},{9,9},{10... | collective-permute-start | bytes 331784 | tf_op jit(solution)/shard_map/ppermute | solution.py:418
  4.5 12.1 %collective-permute-start.1 = (bf16[144,384]{1,0:T(8,128)(2,1)}, bf16[144,384]{1,0:T(8,128)(2,1)S(1)}, u32[]{:S(2)}, u32[]{:S(2)}) collective-permute-start(bf16[144,384]{1,0:T(8,128)(2,1)} %get-tuple-element.16), channel_id=1, source_target_pairs={{0,16},{1,24},{2,18},{3,26},{4,20},{5,28},{6,22},{7,30},{8,17},{9,... | collective-permute-start | bytes 331784 | tf_op jit(solution)/shard_map/ppermute | solution.py:418
  8.1 11.6 %collective-permute-start.2 = (bf16[144,384]{1,0:T(8,128)(2,1)}, bf16[144,384]{1,0:T(8,128)(2,1)S(1)}, u32[]{:S(2)}, u32[]{:S(2)}) collective-permute-start(bf16[144,384]{1,0:T(8,128)(2,1)} %get-tuple-element.17), channel_id=1, source_target_pairs={{0,48},{1,56},{2,50},{3,58},{4,52},{5,60},{6,54},{7,62},{8,49},{9,... | collective-permute-start | bytes 331784 | tf_op jit(solution)/shard_map/ppermute | solution.py:418
  11.2 13.1 %collective-permute-start.3 = (bf16[144,384]{1,0:T(8,128)(2,1)}, bf16[144,384]{1,0:T(8,128)(2,1)S(1)}, u32[]{:S(2)}, u32[]{:S(2)}) collective-permute-start(bf16[144,384]{1,0:T(8,128)(2,1)} %get-tuple-element.18), channel_id=1, source_target_pairs={{0,32},{1,40},{2,34},{3,42},{4,36},{5,44},{6,38},{7,46},{8,33},{9,... | collective-permute-start | bytes 331784 | tf_op jit(solution)/shard_map/ppermute | solution.py:418
  16.6 11.1 %collective-permute-start.5 = (bf16[272,384]{1,0:T(8,128)(2,1)S(1)}, bf16[272,384]{1,0:T(8,128)(2,1)S(1)}, u32[]{:S(2)}, u32[]{:S(2)}) collective-permute-start(bf16[272,384]{1,0:T(8,128)(2,1)S(1)} %shard_map.77.before), channel_id=1, source_target_pairs={{0,192},{1,65},{2,194},{3,67},{4,196},{5,69},{6,198},{7,71},{8,200... | collective-permute-start | bytes 626696 | tf_op jit(solution)/shard_map/ppermute | solution.py:438
  19.7 8.5 %collective-permute-start.4 = (bf16[272,384]{1,0:T(8,128)(2,1)S(1)}, bf16[272,384]{1,0:T(8,128)(2,1)S(1)}, u32[]{:S(2)}, u32[]{:S(2)}) collective-permute-start(bf16[272,384]{1,0:T(8,128)(2,1)S(1)} %shard_map.77.before), channel_id=1, source_target_pairs={{0,64},{1,193},{2,66},{3,195},{4,68},{5,197},{6,70},{7,199},{8,72}... | collective-permute-start | bytes 626696 | tf_op jit(solution)/shard_map/ppermute | solution.py:437
  24.4 8.5 %collective-permute-start.7 = (bf16[272,384]{1,0:T(8,128)(2,1)S(1)}, bf16[272,384]{1,0:T(8,128)(2,1)S(1)}, u32[]{:S(2)}, u32[]{:S(2)}) collective-permute-start(bf16[272,384]{1,0:T(8,128)(2,1)S(1)} %get-tuple-element.20), channel_id=1, source_target_pairs={{0,64},{1,193},{2,66},{3,195},{4,68},{5,197},{6,70},{7,199},{8,72}... | collective-permute-start | bytes 626696 | tf_op jit(solution)/shard_map/ppermute | solution.py:437
  26.1 6.8 %collective-permute-start.8 = (bf16[272,384]{1,0:T(8,128)(2,1)S(1)}, bf16[272,384]{1,0:T(8,128)(2,1)S(1)}, u32[]{:S(2)}, u32[]{:S(2)}) collective-permute-start(bf16[272,384]{1,0:T(8,128)(2,1)S(1)} %get-tuple-element.20), channel_id=1, source_target_pairs={{0,192},{1,65},{2,194},{3,67},{4,196},{5,69},{6,198},{7,71},{8,200... | collective-permute-start | bytes 626696 | tf_op jit(solution)/shard_map/ppermute | solution.py:438
  27.7 12.2 %collective-permute-start.10 = (bf16[544,384]{1,0:T(8,128)(2,1)S(1)}, bf16[544,384]{1,0:T(8,128)(2,1)S(1)}, u32[]{:S(2)}, u32[]{:S(2)}) collective-permute-start(bf16[544,384]{1,0:T(8,128)(2,1)S(1)} %get-tuple-element.19.refs_0_), channel_id=1, source_target_pairs={{0,1},{1,0},{2,3},{3,2},{4,5},{5,4},{6,7},{7,6},{8,9},{9,8},{10,11... | collective-permute-start | bytes 1253384 | tf_op jit(solution)/shard_map/ppermute | solution.py:441
  27.7 5.3 %collective-permute-start.12 = (bf16[272,384]{1,0:T(8,128)(2,1)S(1)}, bf16[272,384]{1,0:T(8,128)(2,1)S(1)}, u32[]{:S(2)}, u32[]{:S(2)}) collective-permute-start(bf16[272,384]{1,0:T(8,128)(2,1)S(1)} %collective-permute-done.5.refs_2_), channel_id=1, source_target_pairs={{0,1},{1,0},{2,3},{3,2},{4,5},{5,4},{6,7},{7,6},{8,9},{9,8},{10,11... | collective-permute-start | bytes 626696 | tf_op jit(solution)/shard_map/ppermute | solution.py:441
  28.2 7.0 %collective-permute-start.6 = (bf16[272,384]{1,0:T(8,128)(2,1)S(1)}, bf16[272,384]{1,0:T(8,128)(2,1)S(1)}, u32[]{:S(2)}, u32[]{:S(2)}) collective-permute-start(bf16[272,384]{1,0:T(8,128)(2,1)S(1)} %collective-permute-done.4.refs_1_), channel_id=1, source_target_pairs={{0,64},{1,193},{2,66},{3,195},{4,68},{5,197},{6,70},{7,199},{8,72}... | collective-permute-start | bytes 626696 | tf_op jit(solution)/shard_map/ppermute | solution.py:439
  32.9 7.0 %collective-permute-start.9 = (bf16[272,384]{1,0:T(8,128)(2,1)S(1)}, bf16[272,384]{1,0:T(8,128)(2,1)S(1)}, u32[]{:S(2)}, u32[]{:S(2)}) collective-permute-start(bf16[272,384]{1,0:T(8,128)(2,1)S(1)} %collective-permute-done.7.refs_0_), channel_id=1, source_target_pairs={{0,64},{1,193},{2,66},{3,195},{4,68},{5,197},{6,70},{7,199},{8,72}... | collective-permute-start | bytes 626696 | tf_op jit(solution)/shard_map/ppermute | solution.py:439
  32.9 8.4 %collective-permute-start.14 = (bf16[544,384]{1,0:T(8,128)(2,1)S(1)}, bf16[544,384]{1,0:T(8,128)(2,1)S(1)}, u32[]{:S(2)}, u32[]{:S(2)}) collective-permute-start(bf16[544,384]{1,0:T(8,128)(2,1)S(1)} %shard_map.79.refs_4_), channel_id=1, source_target_pairs={{0,1},{1,0},{2,3},{3,2},{4,5},{5,4},{6,7},{7,6},{8,9},{9,8},{10,11... | collective-permute-start | bytes 1253384 | tf_op jit(solution)/shard_map/ppermute | solution.py:441
  33.1 6.9 %collective-permute-start.11 = (bf16[272,384]{1,0:T(8,128)(2,1)S(1)}, bf16[272,384]{1,0:T(8,128)(2,1)S(1)}, u32[]{:S(2)}, u32[]{:S(2)}) collective-permute-start(bf16[272,384]{1,0:T(8,128)(2,1)S(1)} %collective-permute-done.4.refs_1_), channel_id=1, source_target_pairs={{0,1},{1,0},{2,3},{3,2},{4,5},{5,4},{6,7},{7,6},{8,9},{9,8},{10,11... | collective-permute-start | bytes 626696 | tf_op jit(solution)/shard_map/ppermute | solution.py:441
  35.3 4.7 %collective-permute-start.13 = (bf16[272,384]{1,0:T(8,128)(2,1)S(1)}, bf16[272,384]{1,0:T(8,128)(2,1)S(1)}, u32[]{:S(2)}, u32[]{:S(2)}) collective-permute-start(bf16[272,384]{1,0:T(8,128)(2,1)S(1)} %collective-permute-done.6.refs_3_), channel_id=1, source_target_pairs={{0,1},{1,0},{2,3},{3,2},{4,5},{5,4},{6,7},{7,6},{8,9},{9,8},{10,11... | collective-permute-start | bytes 626696 | tf_op jit(solution)/shard_map/ppermute | solution.py:441
  39.9 1.5 %collective-permute-start.15 = (bf16[272,384]{1,0:T(8,128)(2,1)S(1)}, bf16[272,384]{1,0:T(8,128)(2,1)S(1)}, u32[]{:S(2)}, u32[]{:S(2)}) collective-permute-start(bf16[272,384]{1,0:T(8,128)(2,1)S(1)} %collective-permute-done.9.refs_5_), channel_id=1, source_target_pairs={{0,1},{1,0},{2,3},{3,2},{4,5},{5,4},{6,7},{7,6},{8,9},{9,8},{10,11... | collective-permute-start | bytes 626696 | tf_op jit(solution)/shard_map/ppermute | solution.py:441
  43.1 1.4 %collective-permute-start.16 = (f32[8,256]{1,0:T(8,128)S(1)}, f32[8,256]{1,0:T(8,128)S(1)}, u32[]{:S(2)}, u32[]{:S(2)}) collective-permute-start(f32[8,256]{1,0:T(8,128)S(1)} %shard_map.80), channel_id=1, source_target_pairs={{0,1},{1,0},{2,3},{3,2},{4,5},{5,4},{6,7},{7,6},{8,9},{9,8},{10,11... | collective-permute-start | bytes 24584 | tf_op jit(solution)/shard_map/ppermute | solution.py:443
  44.5 4.9 %collective-permute-start.19 = (f32[16,256]{1,0:T(8,128)S(1)}, f32[16,256]{1,0:T(8,128)S(1)}, u32[]{:S(2)}, u32[]{:S(2)}) collective-permute-start(f32[16,256]{1,0:T(8,128)S(1)} %pad_maximum_fusion.refs_12_), channel_id=1, source_target_pairs={{0,192},{1,193},{2,194},{3,195},{4,196},{5,197},{6,198},{7,199},{8... | collective-permute-start | bytes 49160 | tf_op jit(solution)/shard_map/ppermute | solution.py:444
  46.9 5.2 %collective-permute-start.18 = (f32[16,256]{1,0:T(8,128)S(1)}, f32[16,256]{1,0:T(8,128)S(1)}, u32[]{:S(2)}, u32[]{:S(2)}) collective-permute-start(f32[16,256]{1,0:T(8,128)S(1)} %pad_maximum_fusion.refs_12_), channel_id=1, source_target_pairs={{0,128},{1,129},{2,130},{3,131},{4,132},{5,133},{6,134},{7,135},{8... | collective-permute-start | bytes 49160 | tf_op jit(solution)/shard_map/ppermute | solution.py:444
  48.1 4.0 %collective-permute-start.17 = (f32[16,256]{1,0:T(8,128)S(1)}, f32[16,256]{1,0:T(8,128)S(1)}, u32[]{:S(2)}, u32[]{:S(2)}) collective-permute-start(f32[16,256]{1,0:T(8,128)S(1)} %pad_maximum_fusion.refs_12_), channel_id=1, source_target_pairs={{0,64},{1,65},{2,66},{3,67},{4,68},{5,69},{6,70},{7,71},{8,72},{9,... | collective-permute-start | bytes 49160 | tf_op jit(solution)/shard_map/ppermute | solution.py:444
  58.5 7.5 %collective-permute-start.20 = (bf16[144,128]{1,0:T(8,128)(2,1)S(1)}, bf16[144,128]{1,0:T(8,128)(2,1)S(1)}, u32[]{:S(2)}, u32[]{:S(2)}) collective-permute-start(bf16[144,128]{1,0:T(8,128)(2,1)S(1)} %get-tuple-element.21), channel_id=1, source_target_pairs={{0,0},{8,1},{2,2},{10,3},{4,4},{12,5},{6,6},{14,7},{1,8},{9,9},{3,... | collective-permute-start | bytes 110600 | tf_op jit(solution)/shard_map/ppermute | solution.py:447
  60.6 5.4 %collective-permute-start.21 = (bf16[144,128]{1,0:T(8,128)(2,1)S(1)}, bf16[144,128]{1,0:T(8,128)(2,1)S(1)}, u32[]{:S(2)}, u32[]{:S(2)}) collective-permute-start(bf16[144,128]{1,0:T(8,128)(2,1)S(1)} %get-tuple-element.22), channel_id=1, source_target_pairs={{16,0},{24,1},{18,2},{26,3},{20,4},{28,5},{22,6},{30,7},{17,8},{25... | collective-permute-start | bytes 110600 | tf_op jit(solution)/shard_map/ppermute | solution.py:447
  62.0 6.4 %collective-permute-start.22 = (bf16[144,128]{1,0:T(8,128)(2,1)S(1)}, bf16[144,128]{1,0:T(8,128)(2,1)S(1)}, u32[]{:S(2)}, u32[]{:S(2)}) collective-permute-start(bf16[144,128]{1,0:T(8,128)(2,1)S(1)} %get-tuple-element.23), channel_id=1, source_target_pairs={{32,0},{40,1},{34,2},{42,3},{36,4},{44,5},{38,6},{46,7},{33,8},{41... | collective-permute-start | bytes 110600 | tf_op jit(solution)/shard_map/ppermute | solution.py:447
  63.4 6.4 %collective-permute-start.23 = (bf16[144,128]{1,0:T(8,128)(2,1)S(1)}, bf16[144,128]{1,0:T(8,128)(2,1)S(1)}, u32[]{:S(2)}, u32[]{:S(2)}) collective-permute-start(bf16[144,128]{1,0:T(8,128)(2,1)S(1)} %get-tuple-element.24), channel_id=1, source_target_pairs={{48,0},{56,1},{50,2},{58,3},{52,4},{60,5},{54,6},{62,7},{49,8},{57... | collective-permute-start | bytes 110600 | tf_op jit(solution)/shard_map/ppermute | solution.py:447
  69.8 1.2 %collective-permute-start.24 = (f32[8,128]{1,0:T(8,128)S(1)}, f32[8,128]{1,0:T(8,128)S(1)}, u32[]{:S(2)}, u32[]{:S(2)}) collective-permute-start(f32[8,128]{1,0:T(8,128)S(1)} %bitcast_reduce_fusion), channel_id=1, source_target_pairs={{0,1},{1,0},{2,3},{3,2},{4,5},{5,4},{6,7},{7,6},{8,9},{9,8},{10,11... | collective-permute-start | bytes 12296 | tf_op jit(solution)/shard_map/ppermute | solution.py:451
  71.0 4.8 %collective-permute-start.27 = (f32[8,128]{1,0:T(8,128)S(1)}, f32[8,128]{1,0:T(8,128)S(1)}, u32[]{:S(2)}, u32[]{:S(2)}) collective-permute-start(f32[8,128]{1,0:T(8,128)S(1)} %add.24), channel_id=1, source_target_pairs={{0,6},{1,7},{2,4},{3,5},{4,2},{5,3},{6,0},{7,1},{8,14},{9,15},{10,... | collective-permute-start | bytes 12296 | tf_op jit(solution)/shard_map/ppermute | solution.py:452
  73.8 5.1 %collective-permute-start.26 = (f32[8,128]{1,0:T(8,128)S(1)}, f32[8,128]{1,0:T(8,128)S(1)}, u32[]{:S(2)}, u32[]{:S(2)}) collective-permute-start(f32[8,128]{1,0:T(8,128)S(1)} %add.24), channel_id=1, source_target_pairs={{0,4},{1,5},{2,6},{3,7},{4,0},{5,1},{6,2},{7,3},{8,12},{9,13},{10,... | collective-permute-start | bytes 12296 | tf_op jit(solution)/shard_map/ppermute | solution.py:452
  74.6 4.3 %collective-permute-start.25 = (f32[8,128]{1,0:T(8,128)S(1)}, f32[8,128]{1,0:T(8,128)S(1)}, u32[]{:S(2)}, u32[]{:S(2)}) collective-permute-start(f32[8,128]{1,0:T(8,128)S(1)} %add.24), channel_id=1, source_target_pairs={{0,2},{1,3},{2,0},{3,1},{4,6},{5,7},{6,4},{7,5},{8,10},{9,11},{10,... | collective-permute-start | bytes 12296 | tf_op jit(solution)/shard_map/ppermute | solution.py:452

commit v4 on v2

--- a/solution.py
+++ b/solution.py
@@ -339,24 +339,15 @@
 
         lax.fori_loop(0, (stop - begin) // n, body, 0)
 
+    wide = UNROLL * TILE
     diag = 4 * y
-    plain = jnp.minimum((start_high + TILE - 1) // TILE, diag)
-    begin = start_low // TILE
-    odd = plain - (plain - begin) % UNROLL
-    run(begin, odd, "below", True, UNROLL)
-    run(odd, plain, "below", True)
-    odd = plain + (diag - plain) % UNROLL
-    run(plain, odd, "below", False)
-    run(odd, diag, "below", False, UNROLL)
-    run(diag, diag + 4, "diagonal", True, 2)
-    plain = jnp.maximum(end_low // TILE, diag + 4)
-    odd = diag + 4 + (plain - diag - 4) % UNROLL
-    run(diag + 4, odd, "above", False)
-    run(odd, plain, "above", False, UNROLL)
-    stop = (end_high + TILE - 1) // TILE
-    odd = plain + (stop - plain) % UNROLL
-    run(plain, odd, "above", True)
-    run(odd, stop, "above", True, UNROLL)
+    plain = jnp.minimum((start_high + wide - 1) // wide * UNROLL, diag)
+    run(start_low // wide * UNROLL, plain, "below", True, UNROLL)
+    run(plain, diag, "below", False, UNROLL)
+    run(diag, diag + 4, "diagonal", True, UNROLL)
+    plain = jnp.maximum(end_low // wide * UNROLL, diag + 4)
+    run(diag + 4, plain, "above", False, UNROLL)
+    run(plain, (end_high + wide - 1) // wide * UNROLL, "above", True, UNROLL)
     for b in range(4):
         for j in range(4):
 
@@ -455,7 +446,7 @@
     parts += [lax.ppermute(part, AXES, CORE_PAIRS) for part in parts]
     packet = call_norm(parts)
     both = jnp.concatenate([packet, lax.ppermute(packet, AXES, CORE_PAIRS)])
-    others = {step: lax.ppermute(both, AXES, mirror_pairs(step)) for step in (2, 1, 3)}
+    others = {step: lax.ppermute(both, AXES, mirror_pairs(step)) for step in (3, 1, 2)}
     packets = [both] + [others[step] for step in (1, 2, 3)]
     grads = call_grad(parts, packets)
     backs = {j: lax.ppermute(grads[j], AXES, collect_pairs(j)) for j in (2, 3, 1, 0)}

time: 82.7 us -> 82.3 us (level)
  starting transfers between devices: 37.4 us -> 35.5 us
  waiting for transfers between devices: 30.6 us -> 32 us
    ppermute x1, starting transfers between devices: 3 us -> 0.62 us  [per_device(): both = jnp.concatenate([packet, lax.ppermute(packet, AXES, CORE_PAIRS)])]
    ppermute x3, waiting for transfers between devices: 1.89 us -> 3.79 us  [per_device(): lax.ppermute(both, AXES, mirror_pairs(step))]
  transfers between devices with their start and end apart: 28 -> 28, of which waited for: 14 -> 13; matrix products, arithmetic and copies ran while one was open for 0% -> 0% of each run, Pallas kernels for 1% -> 1%
where the time goes in v4:
time: 82.3 us; the launch traced here: 81.6 us
  starting transfers between devices  35.5 us (43%)
  waiting for transfers between devices  32 us (39%)
  Pallas kernels  11 us (13%)
  between operations  2.51 us (3%)
    ppermute x4, starting transfers between devices, per_device(): gots = [lax.ppermute(sends[j], AXES, spread_pairs(j)) for j in ORDER]  11.5 us
    ppermute x4, starting transfers between devices, per_device(): lax.ppermute(grads[j], AXES, collect_pairs(j))  7.27 us
    ppermute x4, waiting for transfers between devices, per_device(): gots = [lax.ppermute(sends[j], AXES, spread_pairs(j)) for j in ORDER]  7.15 us
    ppermute x2, waiting for transfers between devices, per_device(): lax.ppermute(near, AXES, near_pairs(1))  6.36 us
    pallas_call x1, Pallas kernels, call_grad(): pl.pallas_call(grad_kernel, out_shape=[jax.ShapeDtypeStruct((ROWS + 16, H...  6.3 us
    ppermute x2, starting transfers between devices, per_device(): lax.ppermute(mine, AXES, near_pairs(-1))  4.75 us
    ppermute x2, waiting for transfers between devices, per_device(): lax.ppermute(mine, AXES, near_pairs(1))  4.29 us
    ppermute x3, starting transfers between devices, per_device(): lax.ppermute(both, AXES, mirror_pairs(step))  4.09 us
  transfers between devices with their start and end apart: 28, of which 13 were waited for; matrix products, arithmetic and copies ran while one was open for 0% of the time, Pallas kernels for 1%

profile of v4, /device:TPU:32, one launch (start us, length us, event | category | flops | bytes accessed | tf_op | source)
XLA Modules:
  0.0 81.6 jit_solution(3614281008458946371)
XLA Ops:
  0.6 1.9 %shard_map.76 = (bf16[144,384]{1,0:T(8,128)(2,1)}, bf16[144,384]{1,0:T(8,128)(2,1)}, bf16[144,384]{1,0:T(8,128)(2,1)}, bf16[144,384]{1,0:T(8,128)(2,1)}) custom-call(bf16[128,512]{1,0:T(8,128)(2,1)} %tq.1, bf16[128,512]{1,0:T(8,128)(2,1)} %tk.1, bf16[128,256]{1,0:T(8,128)(2,1)} %sq.1, bf16[128,256]{1,0:T(8,128)(2,1)} %sk.1, s32[1,128]{1,0:T(1,128)} %bitcast.3), custom_call_target="tpu_custom_call" | custom-call | tf_op jit(solution)/shard_map/pallas_call | solution.py:411
  2.6 1.9 %collective-permute-start = (bf16[144,384]{1,0:T(8,128)(2,1)}, bf16[144,384]{1,0:T(8,128)(2,1)S(1)}, u32[]{:S(2)}, u32[]{:S(2)}) collective-permute-start(bf16[144,384]{1,0:T(8,128)(2,1)} %get-tuple-element.15), channel_id=1, source_target_pairs={{0,0},{1,8},{2,2},{3,10},{4,4},{5,12},{6,6},{7,14},{8,1},{9,9},{10... | collective-permute-start | bytes 331784 | tf_op jit(solution)/shard_map/ppermute | solution.py:423
  4.5 3.6 %collective-permute-start.1 = (bf16[144,384]{1,0:T(8,128)(2,1)}, bf16[144,384]{1,0:T(8,128)(2,1)S(1)}, u32[]{:S(2)}, u32[]{:S(2)}) collective-permute-start(bf16[144,384]{1,0:T(8,128)(2,1)} %get-tuple-element.16), channel_id=1, source_target_pairs={{0,16},{1,24},{2,18},{3,26},{4,20},{5,28},{6,22},{7,30},{8,17},{9,... | collective-permute-start | bytes 331784 | tf_op jit(solution)/shard_map/ppermute | solution.py:423
  8.1 3.1 %collective-permute-start.2 = (bf16[144,384]{1,0:T(8,128)(2,1)}, bf16[144,384]{1,0:T(8,128)(2,1)S(1)}, u32[]{:S(2)}, u32[]{:S(2)}) collective-permute-start(bf16[144,384]{1,0:T(8,128)(2,1)} %get-tuple-element.17), channel_id=1, source_target_pairs={{0,48},{1,56},{2,50},{3,58},{4,52},{5,60},{6,54},{7,62},{8,49},{9,... | collective-permute-start | bytes 331784 | tf_op jit(solution)/shard_map/ppermute | solution.py:423
  11.2 2.9 %collective-permute-start.3 = (bf16[144,384]{1,0:T(8,128)(2,1)}, bf16[144,384]{1,0:T(8,128)(2,1)S(1)}, u32[]{:S(2)}, u32[]{:S(2)}) collective-permute-start(bf16[144,384]{1,0:T(8,128)(2,1)} %get-tuple-element.18), channel_id=1, source_target_pairs={{0,32},{1,40},{2,34},{3,42},{4,36},{5,44},{6,38},{7,46},{8,33},{9,... | collective-permute-start | bytes 331784 | tf_op jit(solution)/shard_map/ppermute | solution.py:423
  14.1 2.5 %collective-permute-done.1.second = bf16[144,384]{1,0:T(8,128)(2,1)S(1)} collective-permute-done((bf16[144,384]{1,0:T(8,128)(2,1)}, bf16[144,384]{1,0:T(8,128)(2,1)S(1)}, u32[]{:S(2)}, u32[]{:S(2)}) %collective-permute-start.1) | collective-permute-done | bytes 110624 | tf_op jit(solution)/shard_map/ppermute | solution.py:423
  16.6 3.1 %collective-permute-start.5 = (bf16[272,384]{1,0:T(8,128)(2,1)S(1)}, bf16[272,384]{1,0:T(8,128)(2,1)S(1)}, u32[]{:S(2)}, u32[]{:S(2)}) collective-permute-start(bf16[272,384]{1,0:T(8,128)(2,1)S(1)} %shard_map.77.before), channel_id=1, source_target_pairs={{0,192},{1,65},{2,194},{3,67},{4,196},{5,69},{6,198},{7,71},{8,200... | collective-permute-start | bytes 626696 | tf_op jit(solution)/shard_map/ppermute | solution.py:443
  19.7 4.6 %collective-permute-done.3.second = bf16[144,384]{1,0:T(8,128)(2,1)S(1)} collective-permute-done((bf16[144,384]{1,0:T(8,128)(2,1)}, bf16[144,384]{1,0:T(8,128)(2,1)S(1)}, u32[]{:S(2)}, u32[]{:S(2)}) %collective-permute-start.3) | collective-permute-done | bytes 110624 | tf_op jit(solution)/shard_map/ppermute | solution.py:423
  24.4 1.7 %collective-permute-start.7 = (bf16[272,384]{1,0:T(8,128)(2,1)S(1)}, bf16[272,384]{1,0:T(8,128)(2,1)S(1)}, u32[]{:S(2)}, u32[]{:S(2)}) collective-permute-start(bf16[272,384]{1,0:T(8,128)(2,1)S(1)} %get-tuple-element.20), channel_id=1, source_target_pairs={{0,64},{1,193},{2,66},{3,195},{4,68},{5,197},{6,70},{7,199},{8,72}... | collective-permute-start | bytes 626696 | tf_op jit(solution)/shard_map/ppermute | solution.py:442
  26.1 1.7 %collective-permute-start.8 = (bf16[272,384]{1,0:T(8,128)(2,1)S(1)}, bf16[272,384]{1,0:T(8,128)(2,1)S(1)}, u32[]{:S(2)}, u32[]{:S(2)}) collective-permute-start(bf16[272,384]{1,0:T(8,128)(2,1)S(1)} %get-tuple-element.20), channel_id=1, source_target_pairs={{0,192},{1,65},{2,194},{3,67},{4,196},{5,69},{6,198},{7,71},{8,200... | collective-permute-start | bytes 626696 | tf_op jit(solution)/shard_map/ppermute | solution.py:443
  28.6 4.3 %collective-permute-done.7.refs_0_ = bf16[272,384]{1,0:T(8,128)(2,1)S(1)} collective-permute-done((bf16[272,384]{1,0:T(8,128)(2,1)S(1)}, bf16[272,384]{1,0:T(8,128)(2,1)S(1)}, u32[]{:S(2)}, u32[]{:S(2)}) %collective-permute-start.7) | collective-permute-done | bytes 208928 | tf_op jit(solution)/shard_map/ppermute | solution.py:442
  33.6 1.7 %collective-permute-done.6.refs_3_ = bf16[272,384]{1,0:T(8,128)(2,1)S(1)} collective-permute-done((bf16[272,384]{1,0:T(8,128)(2,1)S(1)}, bf16[272,384]{1,0:T(8,128)(2,1)S(1)}, u32[]{:S(2)}, u32[]{:S(2)}) %collective-permute-start.6) | collective-permute-done | bytes 208928 | tf_op jit(solution)/shard_map/ppermute | solution.py:444
  35.3 4.6 %collective-permute-done.9.refs_5_ = bf16[272,384]{1,0:T(8,128)(2,1)S(1)} collective-permute-done((bf16[272,384]{1,0:T(8,128)(2,1)S(1)}, bf16[272,384]{1,0:T(8,128)(2,1)S(1)}, u32[]{:S(2)}, u32[]{:S(2)}) %collective-permute-start.9) | collective-permute-done | bytes 208928 | tf_op jit(solution)/shard_map/ppermute | solution.py:444
  39.9 1.4 %collective-permute-done.15.refs_11_ = bf16[272,384]{1,0:T(8,128)(2,1)S(1)} collective-permute-done((bf16[272,384]{1,0:T(8,128)(2,1)S(1)}, bf16[272,384]{1,0:T(8,128)(2,1)S(1)}, u32[]{:S(2)}, u32[]{:S(2)}) %collective-permute-start.15) | collective-permute-done | bytes 208928 | tf_op jit(solution)/shard_map/ppermute | solution.py:446
  41.4 2.0 %shard_map.80 = f32[8,256]{1,0:T(8,128)S(1)} custom-call(bf16[544,384]{1,0:T(8,128)(2,1)S(1)} %get-tuple-element.19.refs_0_, bf16[272,384]{1,0:T(8,128)(2,1)S(1)} %collective-permute-done.4.refs_1_, bf16[272,384]{1,0:T(8,128)(2,1)S(1)} %collective-permute-done.5.refs_2_, bf16[272,384]{1,0:T(8,128)(2,1)S(1)} %collective-permute-done.6.refs_3_, ...), custom_call_target="tpu_custom_call" | custom-call | tf_op jit(solution)/shard_map/pallas_call | solution.py:378
  44.0 0.8 %collective-permute-done.16 = f32[8,256]{1,0:T(8,128)S(1)} collective-permute-done((f32[8,256]{1,0:T(8,128)S(1)}, f32[8,256]{1,0:T(8,128)S(1)}, u32[]{:S(2)}, u32[]{:S(2)}) %collective-permute-start.16) | collective-permute-done | bytes 8224 | tf_op jit(solution)/shard_map/ppermute | solution.py:448
  44.8 2.6 %collective-permute-start.19 = (f32[16,256]{1,0:T(8,128)S(1)}, f32[16,256]{1,0:T(8,128)S(1)}, u32[]{:S(2)}, u32[]{:S(2)}) collective-permute-start(f32[16,256]{1,0:T(8,128)S(1)} %pad_maximum_fusion.refs_12_), channel_id=1, source_target_pairs={{0,192},{1,193},{2,194},{3,195},{4,196},{5,197},{6,198},{7,199},{8... | collective-permute-start | bytes 49160 | tf_op jit(solution)/shard_map/ppermute | solution.py:449
  47.5 1.1 %collective-permute-start.18 = (f32[16,256]{1,0:T(8,128)S(1)}, f32[16,256]{1,0:T(8,128)S(1)}, u32[]{:S(2)}, u32[]{:S(2)}) collective-permute-start(f32[16,256]{1,0:T(8,128)S(1)} %pad_maximum_fusion.refs_12_), channel_id=1, source_target_pairs={{0,128},{1,129},{2,130},{3,131},{4,132},{5,133},{6,134},{7,135},{8... | collective-permute-start | bytes 49160 | tf_op jit(solution)/shard_map/ppermute | solution.py:449
  48.9 0.9 %collective-permute-done.19.refs_15_ = f32[16,256]{1,0:T(8,128)S(1)} collective-permute-done((f32[16,256]{1,0:T(8,128)S(1)}, f32[16,256]{1,0:T(8,128)S(1)}, u32[]{:S(2)}, u32[]{:S(2)}) %collective-permute-start.19) | collective-permute-done | bytes 16416 | tf_op jit(solution)/shard_map/ppermute | solution.py:449
  49.8 2.9 %collective-permute-done.18.refs_14_ = f32[16,256]{1,0:T(8,128)S(1)} collective-permute-done((f32[16,256]{1,0:T(8,128)S(1)}, f32[16,256]{1,0:T(8,128)S(1)}, u32[]{:S(2)}, u32[]{:S(2)}) %collective-permute-start.18) | collective-permute-done | bytes 16416 | tf_op jit(solution)/shard_map/ppermute | solution.py:449
  52.7 6.3 %shard_map.81 = (bf16[144,128]{1,0:T(8,128)(2,1)S(1)}, bf16[144,128]{1,0:T(8,128)(2,1)S(1)}, bf16[144,128]{1,0:T(8,128)(2,1)S(1)}, bf16[144,128]{1,0:T(8,128)(2,1)S(1)}) custom-call(bf16[544,384]{1,0:T(8,128)(2,1)S(1)} %get-tuple-element.19.refs_0_, bf16[272,384]{1,0:T(8,128)(2,1)S(1)} %collective-permute-done.4.refs_1_, ...), custom_call_target="tpu_custom_call" | custom-call | tf_op jit(solution)/shard_map/pallas_call | solution.py:393
  59.0 1.9 %collective-permute-start.20 = (bf16[144,128]{1,0:T(8,128)(2,1)S(1)}, bf16[144,128]{1,0:T(8,128)(2,1)S(1)}, u32[]{:S(2)}, u32[]{:S(2)}) collective-permute-start(bf16[144,128]{1,0:T(8,128)(2,1)S(1)} %get-tuple-element.21), channel_id=1, source_target_pairs={{0,0},{8,1},{2,2},{10,3},{4,4},{12,5},{6,6},{14,7},{1,8},{9,9},{3,... | collective-permute-start | bytes 110600 | tf_op jit(solution)/shard_map/ppermute | solution.py:452
  60.9 1.4 %collective-permute-start.21 = (bf16[144,128]{1,0:T(8,128)(2,1)S(1)}, bf16[144,128]{1,0:T(8,128)(2,1)S(1)}, u32[]{:S(2)}, u32[]{:S(2)}) collective-permute-start(bf16[144,128]{1,0:T(8,128)(2,1)S(1)} %get-tuple-element.22), channel_id=1, source_target_pairs={{16,0},{24,1},{18,2},{26,3},{20,4},{28,5},{22,6},{30,7},{17,8},{25... | collective-permute-start | bytes 110600 | tf_op jit(solution)/shard_map/ppermute | solution.py:452
  62.4 1.4 %collective-permute-start.22 = (bf16[144,128]{1,0:T(8,128)(2,1)S(1)}, bf16[144,128]{1,0:T(8,128)(2,1)S(1)}, u32[]{:S(2)}, u32[]{:S(2)}) collective-permute-start(bf16[144,128]{1,0:T(8,128)(2,1)S(1)} %get-tuple-element.23), channel_id=1, source_target_pairs={{32,0},{40,1},{34,2},{42,3},{36,4},{44,5},{38,6},{46,7},{33,8},{41... | collective-permute-start | bytes 110600 | tf_op jit(solution)/shard_map/ppermute | solution.py:452
  63.7 2.5 %collective-permute-start.23 = (bf16[144,128]{1,0:T(8,128)(2,1)S(1)}, bf16[144,128]{1,0:T(8,128)(2,1)S(1)}, u32[]{:S(2)}, u32[]{:S(2)}) collective-permute-start(bf16[144,128]{1,0:T(8,128)(2,1)S(1)} %get-tuple-element.24), channel_id=1, source_target_pairs={{48,0},{56,1},{50,2},{58,3},{52,4},{60,5},{54,6},{62,7},{49,8},{57... | collective-permute-start | bytes 110600 | tf_op jit(solution)/shard_map/ppermute | solution.py:452
  66.3 2.5 %collective-permute-done.22.g2 = bf16[144,128]{1,0:T(8,128)(2,1)S(1)} collective-permute-done((bf16[144,128]{1,0:T(8,128)(2,1)S(1)}, bf16[144,128]{1,0:T(8,128)(2,1)S(1)}, u32[]{:S(2)}, u32[]{:S(2)}) %collective-permute-start.22) | collective-permute-done | bytes 36896 | tf_op jit(solution)/shard_map/ppermute | solution.py:452
  68.8 1.4 %collective-permute-done.23.g3 = bf16[144,128]{1,0:T(8,128)(2,1)S(1)} collective-permute-done((bf16[144,128]{1,0:T(8,128)(2,1)S(1)}, bf16[144,128]{1,0:T(8,128)(2,1)S(1)}, u32[]{:S(2)}, u32[]{:S(2)}) %collective-permute-start.23) | collective-permute-done | bytes 36896 | tf_op jit(solution)/shard_map/ppermute | solution.py:452
  70.2 1.2 %collective-permute-done.24 = f32[8,128]{1,0:T(8,128)S(1)} collective-permute-done((f32[8,128]{1,0:T(8,128)S(1)}, f32[8,128]{1,0:T(8,128)S(1)}, u32[]{:S(2)}, u32[]{:S(2)}) %collective-permute-start.24) | collective-permute-done | bytes 4128 | tf_op jit(solution)/shard_map/ppermute | solution.py:456
  71.3 2.8 %collective-permute-start.27 = (f32[8,128]{1,0:T(8,128)S(1)}, f32[8,128]{1,0:T(8,128)S(1)}, u32[]{:S(2)}, u32[]{:S(2)}) collective-permute-start(f32[8,128]{1,0:T(8,128)S(1)} %add.24), channel_id=1, source_target_pairs={{0,6},{1,7},{2,4},{3,5},{4,2},{5,3},{6,0},{7,1},{8,14},{9,15},{10,... | collective-permute-start | bytes 12296 | tf_op jit(solution)/shard_map/ppermute | solution.py:457
  74.1 0.8 collective-permute-start.26
  75.4 0.7 shard_map.82
  76.2 3.1 %collective-permute-done.26 = f32[8,128]{1,0:T(8,128)S(1)} collective-permute-done((f32[8,128]{1,0:T(8,128)S(1)}, f32[8,128]{1,0:T(8,128)S(1)}, u32[]{:S(2)}, u32[]{:S(2)}) %collective-permute-start.26) | collective-permute-done | bytes 4128 | tf_op jit(solution)/shard_map/ppermute | solution.py:457
  (35 shorter events, 3.8 us)
Async XLA Ops:
  2.6 11.5 %collective-permute-start = (bf16[144,384]{1,0:T(8,128)(2,1)}, bf16[144,384]{1,0:T(8,128)(2,1)S(1)}, u32[]{:S(2)}, u32[]{:S(2)}) collective-permute-start(bf16[144,384]{1,0:T(8,128)(2,1)} %get-tuple-element.15), channel_id=1, source_target_pairs={{0,0},{1,8},{2,2},{3,10},{4,4},{5,12},{6,6},{7,14},{8,1},{9,9},{10... | collective-permute-start | bytes 331784 | tf_op jit(solution)/shard_map/ppermute | solution.py:423
  4.5 12.1 %collective-permute-start.1 = (bf16[144,384]{1,0:T(8,128)(2,1)}, bf16[144,384]{1,0:T(8,128)(2,1)S(1)}, u32[]{:S(2)}, u32[]{:S(2)}) collective-permute-start(bf16[144,384]{1,0:T(8,128)(2,1)} %get-tuple-element.16), channel_id=1, source_target_pairs={{0,16},{1,24},{2,18},{3,26},{4,20},{5,28},{6,22},{7,30},{8,17},{9,... | collective-permute-start | bytes 331784 | tf_op jit(solution)/shard_map/ppermute | solution.py:423
  8.1 11.6 %collective-permute-start.2 = (bf16[144,384]{1,0:T(8,128)(2,1)}, bf16[144,384]{1,0:T(8,128)(2,1)S(1)}, u32[]{:S(2)}, u32[]{:S(2)}) collective-permute-start(bf16[144,384]{1,0:T(8,128)(2,1)} %get-tuple-element.17), channel_id=1, source_target_pairs={{0,48},{1,56},{2,50},{3,58},{4,52},{5,60},{6,54},{7,62},{8,49},{9,... | collective-permute-start | bytes 331784 | tf_op jit(solution)/shard_map/ppermute | solution.py:423
  11.2 13.1 %collective-permute-start.3 = (bf16[144,384]{1,0:T(8,128)(2,1)}, bf16[144,384]{1,0:T(8,128)(2,1)S(1)}, u32[]{:S(2)}, u32[]{:S(2)}) collective-permute-start(bf16[144,384]{1,0:T(8,128)(2,1)} %get-tuple-element.18), channel_id=1, source_target_pairs={{0,32},{1,40},{2,34},{3,42},{4,36},{5,44},{6,38},{7,46},{8,33},{9,... | collective-permute-start | bytes 331784 | tf_op jit(solution)/shard_map/ppermute | solution.py:423
  16.6 11.1 %collective-permute-start.5 = (bf16[272,384]{1,0:T(8,128)(2,1)S(1)}, bf16[272,384]{1,0:T(8,128)(2,1)S(1)}, u32[]{:S(2)}, u32[]{:S(2)}) collective-permute-start(bf16[272,384]{1,0:T(8,128)(2,1)S(1)} %shard_map.77.before), channel_id=1, source_target_pairs={{0,192},{1,65},{2,194},{3,67},{4,196},{5,69},{6,198},{7,71},{8,200... | collective-permute-start | bytes 626696 | tf_op jit(solution)/shard_map/ppermute | solution.py:443
  19.7 8.5 %collective-permute-start.4 = (bf16[272,384]{1,0:T(8,128)(2,1)S(1)}, bf16[272,384]{1,0:T(8,128)(2,1)S(1)}, u32[]{:S(2)}, u32[]{:S(2)}) collective-permute-start(bf16[272,384]{1,0:T(8,128)(2,1)S(1)} %shard_map.77.before), channel_id=1, source_target_pairs={{0,64},{1,193},{2,66},{3,195},{4,68},{5,197},{6,70},{7,199},{8,72}... | collective-permute-start | bytes 626696 | tf_op jit(solution)/shard_map/ppermute | solution.py:442
  24.4 8.5 %collective-permute-start.7 = (bf16[272,384]{1,0:T(8,128)(2,1)S(1)}, bf16[272,384]{1,0:T(8,128)(2,1)S(1)}, u32[]{:S(2)}, u32[]{:S(2)}) collective-permute-start(bf16[272,384]{1,0:T(8,128)(2,1)S(1)} %get-tuple-element.20), channel_id=1, source_target_pairs={{0,64},{1,193},{2,66},{3,195},{4,68},{5,197},{6,70},{7,199},{8,72}... | collective-permute-start | bytes 626696 | tf_op jit(solution)/shard_map/ppermute | solution.py:442
  26.1 6.8 %collective-permute-start.8 = (bf16[272,384]{1,0:T(8,128)(2,1)S(1)}, bf16[272,384]{1,0:T(8,128)(2,1)S(1)}, u32[]{:S(2)}, u32[]{:S(2)}) collective-permute-start(bf16[272,384]{1,0:T(8,128)(2,1)S(1)} %get-tuple-element.20), channel_id=1, source_target_pairs={{0,192},{1,65},{2,194},{3,67},{4,196},{5,69},{6,198},{7,71},{8,200... | collective-permute-start | bytes 626696 | tf_op jit(solution)/shard_map/ppermute | solution.py:443
  27.7 12.2 %collective-permute-start.10 = (bf16[544,384]{1,0:T(8,128)(2,1)S(1)}, bf16[544,384]{1,0:T(8,128)(2,1)S(1)}, u32[]{:S(2)}, u32[]{:S(2)}) collective-permute-start(bf16[544,384]{1,0:T(8,128)(2,1)S(1)} %get-tuple-element.19.refs_0_), channel_id=1, source_target_pairs={{0,1},{1,0},{2,3},{3,2},{4,5},{5,4},{6,7},{7,6},{8,9},{9,8},{10,11... | collective-permute-start | bytes 1253384 | tf_op jit(solution)/shard_map/ppermute | solution.py:446
  27.7 5.3 %collective-permute-start.12 = (bf16[272,384]{1,0:T(8,128)(2,1)S(1)}, bf16[272,384]{1,0:T(8,128)(2,1)S(1)}, u32[]{:S(2)}, u32[]{:S(2)}) collective-permute-start(bf16[272,384]{1,0:T(8,128)(2,1)S(1)} %collective-permute-done.5.refs_2_), channel_id=1, source_target_pairs={{0,1},{1,0},{2,3},{3,2},{4,5},{5,4},{6,7},{7,6},{8,9},{9,8},{10,11... | collective-permute-start | bytes 626696 | tf_op jit(solution)/shard_map/ppermute | solution.py:446
  28.2 7.0 %collective-permute-start.6 = (bf16[272,384]{1,0:T(8,128)(2,1)S(1)}, bf16[272,384]{1,0:T(8,128)(2,1)S(1)}, u32[]{:S(2)}, u32[]{:S(2)}) collective-permute-start(bf16[272,384]{1,0:T(8,128)(2,1)S(1)} %collective-permute-done.4.refs_1_), channel_id=1, source_target_pairs={{0,64},{1,193},{2,66},{3,195},{4,68},{5,197},{6,70},{7,199},{8,72}... | collective-permute-start | bytes 626696 | tf_op jit(solution)/shard_map/ppermute | solution.py:444
  32.9 7.0 %collective-permute-start.9 = (bf16[272,384]{1,0:T(8,128)(2,1)S(1)}, bf16[272,384]{1,0:T(8,128)(2,1)S(1)}, u32[]{:S(2)}, u32[]{:S(2)}) collective-permute-start(bf16[272,384]{1,0:T(8,128)(2,1)S(1)} %collective-permute-done.7.refs_0_), channel_id=1, source_target_pairs={{0,64},{1,193},{2,66},{3,195},{4,68},{5,197},{6,70},{7,199},{8,72}... | collective-permute-start | bytes 626696 | tf_op jit(solution)/shard_map/ppermute | solution.py:444
  32.9 8.4 %collective-permute-start.14 = (bf16[544,384]{1,0:T(8,128)(2,1)S(1)}, bf16[544,384]{1,0:T(8,128)(2,1)S(1)}, u32[]{:S(2)}, u32[]{:S(2)}) collective-permute-start(bf16[544,384]{1,0:T(8,128)(2,1)S(1)} %shard_map.79.refs_4_), channel_id=1, source_target_pairs={{0,1},{1,0},{2,3},{3,2},{4,5},{5,4},{6,7},{7,6},{8,9},{9,8},{10,11... | collective-permute-start | bytes 1253384 | tf_op jit(solution)/shard_map/ppermute | solution.py:446
  33.1 6.9 %collective-permute-start.11 = (bf16[272,384]{1,0:T(8,128)(2,1)S(1)}, bf16[272,384]{1,0:T(8,128)(2,1)S(1)}, u32[]{:S(2)}, u32[]{:S(2)}) collective-permute-start(bf16[272,384]{1,0:T(8,128)(2,1)S(1)} %collective-permute-done.4.refs_1_), channel_id=1, source_target_pairs={{0,1},{1,0},{2,3},{3,2},{4,5},{5,4},{6,7},{7,6},{8,9},{9,8},{10,11... | collective-permute-start | bytes 626696 | tf_op jit(solution)/shard_map/ppermute | solution.py:446
  35.3 4.7 %collective-permute-start.13 = (bf16[272,384]{1,0:T(8,128)(2,1)S(1)}, bf16[272,384]{1,0:T(8,128)(2,1)S(1)}, u32[]{:S(2)}, u32[]{:S(2)}) collective-permute-start(bf16[272,384]{1,0:T(8,128)(2,1)S(1)} %collective-permute-done.6.refs_3_), channel_id=1, source_target_pairs={{0,1},{1,0},{2,3},{3,2},{4,5},{5,4},{6,7},{7,6},{8,9},{9,8},{10,11... | collective-permute-start | bytes 626696 | tf_op jit(solution)/shard_map/ppermute | solution.py:446
  39.9 1.5 %collective-permute-start.15 = (bf16[272,384]{1,0:T(8,128)(2,1)S(1)}, bf16[272,384]{1,0:T(8,128)(2,1)S(1)}, u32[]{:S(2)}, u32[]{:S(2)}) collective-permute-start(bf16[272,384]{1,0:T(8,128)(2,1)S(1)} %collective-permute-done.9.refs_5_), channel_id=1, source_target_pairs={{0,1},{1,0},{2,3},{3,2},{4,5},{5,4},{6,7},{7,6},{8,9},{9,8},{10,11... | collective-permute-start | bytes 626696 | tf_op jit(solution)/shard_map/ppermute | solution.py:446
  43.4 1.4 %collective-permute-start.16 = (f32[8,256]{1,0:T(8,128)S(1)}, f32[8,256]{1,0:T(8,128)S(1)}, u32[]{:S(2)}, u32[]{:S(2)}) collective-permute-start(f32[8,256]{1,0:T(8,128)S(1)} %shard_map.80), channel_id=1, source_target_pairs={{0,1},{1,0},{2,3},{3,2},{4,5},{5,4},{6,7},{7,6},{8,9},{9,8},{10,11... | collective-permute-start | bytes 24584 | tf_op jit(solution)/shard_map/ppermute | solution.py:448
  44.8 4.9 %collective-permute-start.19 = (f32[16,256]{1,0:T(8,128)S(1)}, f32[16,256]{1,0:T(8,128)S(1)}, u32[]{:S(2)}, u32[]{:S(2)}) collective-permute-start(f32[16,256]{1,0:T(8,128)S(1)} %pad_maximum_fusion.refs_12_), channel_id=1, source_target_pairs={{0,192},{1,193},{2,194},{3,195},{4,196},{5,197},{6,198},{7,199},{8... | collective-permute-start | bytes 49160 | tf_op jit(solution)/shard_map/ppermute | solution.py:449
  47.5 5.2 %collective-permute-start.18 = (f32[16,256]{1,0:T(8,128)S(1)}, f32[16,256]{1,0:T(8,128)S(1)}, u32[]{:S(2)}, u32[]{:S(2)}) collective-permute-start(f32[16,256]{1,0:T(8,128)S(1)} %pad_maximum_fusion.refs_12_), channel_id=1, source_target_pairs={{0,128},{1,129},{2,130},{3,131},{4,132},{5,133},{6,134},{7,135},{8... | collective-permute-start | bytes 49160 | tf_op jit(solution)/shard_map/ppermute | solution.py:449
  48.5 4.2 %collective-permute-start.17 = (f32[16,256]{1,0:T(8,128)S(1)}, f32[16,256]{1,0:T(8,128)S(1)}, u32[]{:S(2)}, u32[]{:S(2)}) collective-permute-start(f32[16,256]{1,0:T(8,128)S(1)} %pad_maximum_fusion.refs_12_), channel_id=1, source_target_pairs={{0,64},{1,65},{2,66},{3,67},{4,68},{5,69},{6,70},{7,71},{8,72},{9,... | collective-permute-start | bytes 49160 | tf_op jit(solution)/shard_map/ppermute | solution.py:449
  59.0 7.3 %collective-permute-start.20 = (bf16[144,128]{1,0:T(8,128)(2,1)S(1)}, bf16[144,128]{1,0:T(8,128)(2,1)S(1)}, u32[]{:S(2)}, u32[]{:S(2)}) collective-permute-start(bf16[144,128]{1,0:T(8,128)(2,1)S(1)} %get-tuple-element.21), channel_id=1, source_target_pairs={{0,0},{8,1},{2,2},{10,3},{4,4},{12,5},{6,6},{14,7},{1,8},{9,9},{3,... | collective-permute-start | bytes 110600 | tf_op jit(solution)/shard_map/ppermute | solution.py:452
  60.9 5.4 %collective-permute-start.21 = (bf16[144,128]{1,0:T(8,128)(2,1)S(1)}, bf16[144,128]{1,0:T(8,128)(2,1)S(1)}, u32[]{:S(2)}, u32[]{:S(2)}) collective-permute-start(bf16[144,128]{1,0:T(8,128)(2,1)S(1)} %get-tuple-element.22), channel_id=1, source_target_pairs={{16,0},{24,1},{18,2},{26,3},{20,4},{28,5},{22,6},{30,7},{17,8},{25... | collective-permute-start | bytes 110600 | tf_op jit(solution)/shard_map/ppermute | solution.py:452
  62.4 6.4 %collective-permute-start.22 = (bf16[144,128]{1,0:T(8,128)(2,1)S(1)}, bf16[144,128]{1,0:T(8,128)(2,1)S(1)}, u32[]{:S(2)}, u32[]{:S(2)}) collective-permute-start(bf16[144,128]{1,0:T(8,128)(2,1)S(1)} %get-tuple-element.23), channel_id=1, source_target_pairs={{32,0},{40,1},{34,2},{42,3},{36,4},{44,5},{38,6},{46,7},{33,8},{41... | collective-permute-start | bytes 110600 | tf_op jit(solution)/shard_map/ppermute | solution.py:452
  63.7 6.4 %collective-permute-start.23 = (bf16[144,128]{1,0:T(8,128)(2,1)S(1)}, bf16[144,128]{1,0:T(8,128)(2,1)S(1)}, u32[]{:S(2)}, u32[]{:S(2)}) collective-permute-start(bf16[144,128]{1,0:T(8,128)(2,1)S(1)} %get-tuple-element.24), channel_id=1, source_target_pairs={{48,0},{56,1},{50,2},{58,3},{52,4},{60,5},{54,6},{62,7},{49,8},{57... | collective-permute-start | bytes 110600 | tf_op jit(solution)/shard_map/ppermute | solution.py:452
  70.2 1.2 %collective-permute-start.24 = (f32[8,128]{1,0:T(8,128)S(1)}, f32[8,128]{1,0:T(8,128)S(1)}, u32[]{:S(2)}, u32[]{:S(2)}) collective-permute-start(f32[8,128]{1,0:T(8,128)S(1)} %bitcast_reduce_fusion), channel_id=1, source_target_pairs={{0,1},{1,0},{2,3},{3,2},{4,5},{5,4},{6,7},{7,6},{8,9},{9,8},{10,11... | collective-permute-start | bytes 12296 | tf_op jit(solution)/shard_map/ppermute | solution.py:456
  71.3 4.8 %collective-permute-start.27 = (f32[8,128]{1,0:T(8,128)S(1)}, f32[8,128]{1,0:T(8,128)S(1)}, u32[]{:S(2)}, u32[]{:S(2)}) collective-permute-start(f32[8,128]{1,0:T(8,128)S(1)} %add.24), channel_id=1, source_target_pairs={{0,6},{1,7},{2,4},{3,5},{4,2},{5,3},{6,0},{7,1},{8,14},{9,15},{10,... | collective-permute-start | bytes 12296 | tf_op jit(solution)/shard_map/ppermute | solution.py:457
  74.1 5.1 %collective-permute-start.26 = (f32[8,128]{1,0:T(8,128)S(1)}, f32[8,128]{1,0:T(8,128)S(1)}, u32[]{:S(2)}, u32[]{:S(2)}) collective-permute-start(f32[8,128]{1,0:T(8,128)S(1)} %add.24), channel_id=1, source_target_pairs={{0,4},{1,5},{2,6},{3,7},{4,0},{5,1},{6,2},{7,3},{8,12},{9,13},{10,... | collective-permute-start | bytes 12296 | tf_op jit(solution)/shard_map/ppermute | solution.py:457
  74.9 4.3 %collective-permute-start.25 = (f32[8,128]{1,0:T(8,128)S(1)}, f32[8,128]{1,0:T(8,128)S(1)}, u32[]{:S(2)}, u32[]{:S(2)}) collective-permute-start(f32[8,128]{1,0:T(8,128)S(1)} %add.24), channel_id=1, source_target_pairs={{0,2},{1,3},{2,0},{3,1},{4,6},{5,7},{6,4},{7,5},{8,10},{9,11},{10,... | collective-permute-start | bytes 12296 | tf_op jit(solution)/shard_map/ppermute | solution.py:457
